TPU v7x, 256 devices: a whole 4x4x8 slice. The times are simulated.
256 devices in a mesh: req: 8 (over y, core), mp: 32 (over z, x).
Axes of the slice: x: 4, y: 4, z: 8, core: 2. Of those that a mesh axis runs over, the one named last changes fastest.
Arguments:
- draft_hidden: bfloat16 [16, 2048], P('req'), may hold values from -6 to 6
- draft_weight: bfloat16 [4, 2048, 2048], P(None, None, 'mp'), may hold values from -0.125 to 0.125
- vocab_weight: bfloat16 [98304, 2048], P(('req', 'mp')), may hold values from -0.375 to 0.375
- tree_inputs: bfloat16 [768, 2048], P('req')
- tree_parent: int32 [16, 48], P('req'), may hold values from -1 to 41, as said below
- cache_len: int32 [16], P('req'), may hold values from 1 to 8192, as said below
- page_table: int32 [16, 64], P('req'), may hold values from -1 to 1023, as said below
- kv_cache: bfloat16 [1024, 2, 128, 2048], P(('req', 'mp'))
- accepted_node: int32 [16], P('req'), may hold values from 0 to 47
- qkv_weight: bfloat16 [2048, 3, 2048], P(None, None, 'mp'), may hold values from -0.125 to 0.125
- norm_gains: bfloat16 [4, 2048], replicated, may hold values from 0.5 to 1.5
- out_weight: bfloat16 [2048, 2048], P(None, 'mp'), may hold values from -0.125 to 0.125
- gate_up_weight: bfloat16 [2048, 2, 8192], P(None, None, 'mp'), may hold values from -0.125 to 0.125
- down_weight: bfloat16 [8192, 2048], P('mp'), may hold values from -0.0625 to 0.0625
Outputs:
- draft_logits: float32 [16, 4, 98304], P(None, None, ('req', 'mp'))
- layer_out: bfloat16 [768, 2048], P(('req', 'mp'))
- accepted_kv: bfloat16 [16, 4, 2, 2048], P('req', None, None, 'mp')
Inputs may be any that keep to these rules, and one draw needn't show every extreme that they name: `page_table`: row r lists the pool pages of request r in the order of its tokens, ceil(cache_len[r] / 128) of them, then -1. The pages of the requests of one index of req lie in that index's part of kv_cache, and no page serves two requests. `cache_len`: on every index of req some request has exactly 8192 cached tokens. `tree_parent`: A parent has a smaller index than its child; a node has at most 3 ancestors.
All inputs are finite; a program needn't handle non-finite values.
Results may differ from a plain program's by a relative error of at most 0.01355.
Values may be sent and summed in bfloat16 or wider, within the bound.
No kernel may reach another device: no remote copies, remote signals or barrier semaphores. Data moves between devices by JAX's collectives and lax.ppermute only.
A program may use at most 128 MiB of HBM per device.

v0:
```python
import jax
import jax.numpy as jnp
from jax import lax
from jax.sharding import PartitionSpec as P

HEADS = 16
HEAD_DIM = 128


rope_base = 500000.0
norm_epsilon = 1e-06
masked_score = -1e30


def combined_all(part, axis, combine):
    gathered = jax.tree.map(lambda a: lax.all_gather(a, axis), part)

    def take(source):
        return jax.tree.map(lambda a: lax.dynamic_index_in_dim(a, source, 0, False), gathered)

    return lax.fori_loop(
        1, lax.axis_size(axis), lambda source, state: combine(state, take(source)), take(0)
    )


def rms_scaled(entries, gain_row):
    mean_square = jnp.mean(entries * entries, axis=-1, keepdims=True)
    return entries * lax.rsqrt(mean_square + norm_epsilon) * gain_row


def tree_shape(parents):
    node_count = parents.shape[-1]
    step_one = (
        parents[..., :, None] == jnp.arange(node_count, dtype=jnp.int32)[None, None, :]
    ).astype(jnp.float32)
    step_two = jnp.einsum("rij,rjk->rik", step_one, step_one, precision=lax.Precision.HIGHEST)
    step_three = jnp.einsum("rij,rjk->rik", step_two, step_one, precision=lax.Precision.HIGHEST)
    ancestry = jnp.eye(node_count, dtype=jnp.float32)[None] + step_one + step_two + step_three
    return (ancestry, jnp.sum(ancestry, axis=-1))


def rotate(entries, positions):
    row_count = entries.shape[0]
    half_dim = HEAD_DIM // 2
    shaped = entries.reshape(row_count, HEADS, HEAD_DIM)
    freqs = rope_base ** (-jnp.arange(half_dim, dtype=jnp.float32) * 2.0 / HEAD_DIM)
    angles = positions[:, None] * freqs[None, :]
    cosine = jnp.cos(angles)[:, None, :]
    sine_part = jnp.sin(angles)[:, None, :]
    front = shaped[..., :half_dim]
    back_half = shaped[..., half_dim:]
    turned = jnp.concatenate(
        [front * cosine - back_half * sine_part, back_half * cosine + front * sine_part], axis=-1
    )
    return turned.reshape(row_count, HEADS * HEAD_DIM)


def fold_states(left_state, right_state):
    top_left, total_left, mixed_left = left_state
    top_right, total_right, mixed_right = right_state
    top_both = jnp.maximum(top_left, top_right)
    factor_left = jnp.exp(top_left - top_both)
    factor_right = jnp.exp(top_right - top_both)
    return (
        top_both,
        total_left * factor_left + total_right * factor_right,
        mixed_left * factor_left[..., None] + mixed_right * factor_right[..., None],
    )


def tree_states(query_part, key_part, value_part, ancestry):
    scale = HEAD_DIM ** (-0.5)
    scores = (
        jnp.einsum("rthe,rshe->rths", query_part, key_part, preferred_element_type=jnp.float32)
        * scale
    )
    visible = (ancestry > 0.5)[:, :, None, :]
    scores = jnp.where(visible, scores, masked_score)
    top_score = jnp.max(scores, axis=-1)
    weights = jnp.where(visible, jnp.exp(scores - top_score[..., None]), 0.0)
    totals = jnp.sum(weights, axis=-1)
    mixed = jnp.einsum(
        "rths,rshe->rthe",
        weights.astype(jnp.bfloat16),
        value_part,
        preferred_element_type=jnp.float32,
    )
    return (top_score, totals, mixed)


def page_states(queries, cache_len, page_table, kv_cache, first_slot):
    scale = HEAD_DIM ** (-0.5)
    page_count = kv_cache.shape[0]
    page_len = kv_cache.shape[2]
    table_width = page_table.shape[1]
    req_local = page_table.shape[0]
    slots = first_slot + jnp.arange(page_count, dtype=jnp.int32)
    matches = page_table[None, :, :] == slots[:, None, None]
    owner_hot = jnp.any(matches, axis=2)
    page_index = jnp.sum(
        jnp.where(matches, jnp.arange(table_width, dtype=jnp.int32)[None, None, :], 0), axis=(1, 2)
    )
    owner = jnp.sum(
        jnp.where(matches, jnp.arange(req_local, dtype=jnp.int32)[None, :, None], 0), axis=(1, 2)
    )
    in_use = jnp.any(matches, axis=(1, 2))
    limit = jnp.take(cache_len, owner)
    token_pos = page_index[:, None] * page_len + jnp.arange(page_len, dtype=jnp.int32)[None, :]
    valid = in_use[:, None] & (token_pos < limit[:, None])
    page_keys = kv_cache[:, 0].reshape(page_count, page_len, HEADS, HEAD_DIM)
    page_values = kv_cache[:, 1].reshape(page_count, page_len, HEADS, HEAD_DIM)
    asked = jnp.take(queries, owner, axis=0)
    scores = (
        jnp.einsum("pthe,pshe->phts", asked, page_keys, preferred_element_type=jnp.float32) * scale
    )
    visible = valid[:, None, None, :]
    scores = jnp.where(visible, scores, masked_score)
    top_score = jnp.max(scores, axis=-1)
    weights = jnp.where(visible, jnp.exp(scores - top_score[..., None]), 0.0)
    totals = jnp.sum(weights, axis=-1)
    mixed = jnp.einsum(
        "phts,pshe->pthe",
        weights.astype(jnp.bfloat16),
        page_values,
        preferred_element_type=jnp.float32,
    )
    owner_mask = owner_hot[:, :, None, None]
    top_request = jnp.max(jnp.where(owner_mask, top_score[:, None], masked_score), axis=0)
    spread_gap = jnp.where(owner_mask, top_score[:, None] - top_request[None], 0.0)
    factor = jnp.where(owner_mask, jnp.exp(spread_gap), 0.0)
    total_request = jnp.sum(factor * totals[:, None], axis=0)
    mixed_request = jnp.einsum("prht,pthe->rthe", factor, mixed, precision=lax.Precision.HIGHEST)
    return (
        jnp.transpose(top_request, (0, 2, 1)),
        jnp.transpose(total_request, (0, 2, 1)),
        mixed_request,
    )


def per_device(
    draft_hidden,
    draft_weight,
    vocab_weight,
    tree_inputs,
    tree_parent,
    cache_len,
    page_table,
    kv_cache,
    accepted_node,
    qkv_weight,
    norm_gains,
    out_weight,
    gate_up_weight,
    down_weight,
):
    mp_count = lax.axis_size("mp")
    req_count = lax.axis_size("req")
    mp_place = lax.axis_index("mp")
    req_place = lax.axis_index("req")
    req_local = draft_hidden.shape[0]
    model_width = draft_hidden.shape[1]
    draft_count = draft_weight.shape[0]
    slab_width = draft_weight.shape[2]
    vocab_local = vocab_weight.shape[0]
    draft_raw = jnp.einsum(
        "rd,kde->rke", draft_hidden, draft_weight, preferred_element_type=jnp.float32
    )
    own_columns = lax.dynamic_slice_in_dim(
        draft_hidden, mp_place * slab_width, slab_width, 1
    ).astype(jnp.float32)
    drafted = (own_columns[:, None, :] + jax.nn.silu(draft_raw)).astype(jnp.bfloat16)
    collected = lax.all_gather(drafted[None], ("req", "mp"), axis=0, tiled=True)
    collected = collected.reshape(req_count, mp_count, req_local, draft_count, slab_width)
    vocab_table = vocab_weight.reshape(vocab_local, mp_count, slab_width)
    draft_logits = jnp.einsum(
        "gmrkc,vmc->grkv", collected, vocab_table, preferred_element_type=jnp.float32
    ).reshape(req_count * req_local, draft_count, vocab_local)
    row_count = tree_inputs.shape[0]
    tree_size = tree_parent.shape[1]
    own_projection = jnp.einsum(
        "td,dce->tce", tree_inputs, qkv_weight, preferred_element_type=jnp.float32
    ).astype(jnp.bfloat16)
    projected = lax.all_gather(own_projection, "mp", axis=2, tiled=True)
    ancestry, node_depth = tree_shape(tree_parent)
    positions = (cache_len[:, None].astype(jnp.float32) + node_depth - 1.0).reshape(row_count)
    gain_rows = norm_gains.astype(jnp.float32)
    queries = (
        rotate(rms_scaled(projected[:, 0].astype(jnp.float32), gain_rows[0]), positions)
        .astype(jnp.bfloat16)
        .reshape(req_local, tree_size, HEADS, HEAD_DIM)
    )
    keys_tree = (
        rotate(rms_scaled(projected[:, 1].astype(jnp.float32), gain_rows[1]), positions)
        .astype(jnp.bfloat16)
        .reshape(req_local, tree_size, HEADS, HEAD_DIM)
    )
    values_tree = projected[:, 2].reshape(req_local, tree_size, HEADS, HEAD_DIM)
    chosen = (accepted_node[:, None] == jnp.arange(tree_size, dtype=jnp.int32)[None, :]).astype(
        jnp.float32
    )
    on_path = jnp.einsum("rt,rts->rs", chosen, ancestry, precision=lax.Precision.HIGHEST)
    levels = jnp.arange(1, draft_count + 1, dtype=jnp.float32)
    picker = on_path[:, None, :] * (node_depth[:, None, :] == levels[None, :, None]).astype(
        jnp.float32
    )
    key_columns = lax.dynamic_slice_in_dim(
        keys_tree.reshape(req_local, tree_size, model_width), mp_place * slab_width, slab_width, 2
    )
    value_columns = own_projection[:, 2].reshape(req_local, tree_size, slab_width)
    stacked = jnp.stack([key_columns, value_columns], axis=2)
    accepted_kv = jnp.einsum(
        "rjs,rsce->rjce", picker.astype(jnp.bfloat16), stacked, preferred_element_type=jnp.float32
    ).astype(jnp.bfloat16)
    first_slot = (req_place * mp_count + mp_place) * kv_cache.shape[0]
    page_part = page_states(queries, cache_len, page_table, kv_cache, first_slot)
    identity = (
        jnp.full((req_local, tree_size, HEADS), masked_score, jnp.float32),
        jnp.zeros((req_local, tree_size, HEADS), jnp.float32),
        jnp.zeros((req_local, tree_size, HEADS, HEAD_DIM), jnp.float32),
    )
    tree_part = lax.cond(
        mp_place == 0,
        lambda: tree_states(queries, keys_tree, values_tree, ancestry),
        lambda: identity,
    )
    local_state = fold_states(page_part, tree_part)
    merged = combined_all(local_state, "mp", fold_states)
    attended = (
        (merged[2] / merged[1][..., None]).astype(jnp.bfloat16).reshape(row_count, model_width)
    )
    out_columns = jnp.dot(attended, out_weight, preferred_element_type=jnp.float32).astype(
        jnp.bfloat16
    )
    projected_out = lax.all_gather(out_columns, "mp", axis=1, tiled=True)
    residual = (
        tree_inputs.astype(jnp.float32)
        + rms_scaled(projected_out.astype(jnp.float32), gain_rows[2])
    ).astype(jnp.bfloat16)
    gate_up = jnp.einsum(
        "td,dce->tce", residual, gate_up_weight, preferred_element_type=jnp.float32
    )
    hidden = (jax.nn.silu(gate_up[:, 0]) * gate_up[:, 1]).astype(jnp.bfloat16)
    row_share = row_count // mp_count
    first_row = mp_place * row_share
    summed = lax.psum(
        jnp.dot(hidden, down_weight, preferred_element_type=jnp.float32).astype(jnp.bfloat16), "mp"
    ).astype(jnp.float32)
    own_rows = lax.dynamic_slice_in_dim(summed, first_row, row_share, 0)
    residual_rows = lax.dynamic_slice_in_dim(residual, first_row, row_share, 0).astype(jnp.float32)
    layer_out = (residual_rows + rms_scaled(own_rows, gain_rows[3])).astype(jnp.bfloat16)
    return (draft_logits, layer_out, accepted_kv)


def solution(mesh):
    placed = (
        P("req", None),
        P(None, None, "mp"),
        P(("req", "mp"), None),
        P("req", None),
        P("req", None),
        P("req"),
        P("req", None),
        P(("req", "mp"), None, None, None),
        P("req"),
        P(None, None, "mp"),
        P(),
        P(None, "mp"),
        P(None, None, "mp"),
        P("mp", None),
    )
    return jax.shard_map(
        per_device,
        mesh=mesh,
        in_specs=placed,
        out_specs=(
            P(None, None, ("req", "mp")),
            P(("req", "mp"), None),
            P("req", None, None, "mp"),
        ),
        check_vma=False,
    )
```

profile of v0, /device:TPU:48, one launch (start us, length us, event | category | flops | bytes accessed | tf_op | source)
XLA Modules:
  0.0 611.6 jit_solution(11031418135957718343)
XLA Ops:
  7.2 1.7 fusion.81
  13.2 4.8 fusion.77
  18.1 4.0 copy.281
  22.0 4.0 copy.280
  27.2 62.7 %all-gather.7.cloned.1.call-done = bf16[96,3,2048]{0,2,1:T(8,128)(2,1)} async-done(((bf16[96,3,64]{0,2,1:T(8,128)(2,1)}), bf16[96,3,2048]{0,2,1:T(8,128)(2,1)}) %all-gather.7.cloned.1.call-update) | async-done | bytes 1179664 | tf_op jit(solution)/shard_map/all_gather | solution.py:183
  90.0 2.3 slice_convert_fusion.1
  92.3 2.5 copy.242
  101.9 3.5 fusion.80
  105.6 2.4 fusion.20
  108.1 4.4 convolution_bitcast_fusion.1
  114.5 8.8 %fusion.17 = f32[48,16,128,2]{2,3,1,0:T(2,128)} fusion(f32[4,48,16,128]{3,1,2,0:T(8,128)} %convolution_bitcast_fusion.1, pred[4,2]{0,1:T(4,128)(4,1)S(1)} %get-tuple-element.271, f32[2,16,48]{0,1,2:T(8,128)S(1)} %select_reduce_fusion, f32[4,16,48]{0,1,2:T(8,128)S(1)} %copy.248), kind=kOutput, calls=%fused_computation.29 | convolution fusion | flops 9455616 | bytes 2377736 | tf_op jit(solution)/shard_map/prht,pthe->rthe/dot_general | solution.py:132
  123.3 2.8 multiply_reduce_fusion.2
  127.3 2.1 pad_maximum_fusion
  131.8 2.5 fusion.26
  135.9 1.7 fusion.54
  137.7 74.9 %all-gather = bf16[512,4,64]{2,1,0:T(4,128)(2,1)S(1)} all-gather(bf16[2,4,64]{2,1,0:T(4,128)(2,1)S(1)} %add_convert_fusion.1), channel_id=2, replica_groups=mesh['req'=8,'mp'=32] {'req','mp'}, dimensions={0}, use_global_device_ids=true | all-gather | bytes 263168 | tf_op jit(solution)/shard_map/all_gather | solution.py:172
  212.9 2.6 copy.241
  215.6 1.9 convolution_bitcast_fusion.2
  219.0 49.7 %all-gather.2 = f32[64,48,16]{1,2,0:T(8,128)S(1)} all-gather(f32[2,48,16]{1,2,0:T(8,128)S(1)} %copy-done.9), channel_id=4, replica_groups=mesh['req'=8,'mp'=32] {'mp'}, dimensions={0}, use_global_device_ids=true | all-gather | bytes 202752 | tf_op jit(solution)/shard_map/all_gather | solution.py:16
  268.7 47.5 %all-gather.1 = f32[64,48,16]{1,2,0:T(8,128)S(1)} all-gather(f32[2,48,16]{1,2,0:T(8,128)S(1)} %get-tuple-element.307), channel_id=3, replica_groups=mesh['req'=8,'mp'=32] {'mp'}, dimensions={0}, use_global_device_ids=true | all-gather | bytes 202752 | tf_op jit(solution)/shard_map/all_gather | solution.py:16
  317.0 7.4 %all-gather.9.cloned.1.call-done = f32[64,48,16,128]{3,2,1,0:T(8,128)} async-done(((f32[2,48,16,128]{3,2,1,0:T(8,128)}), f32[64,48,16,128]{3,2,1,0:T(8,128)}) %all-gather.9.cloned.1.call-update) | async-done | bytes 25165840 | tf_op jit(solution)/shard_map/all_gather | solution.py:16
  325.6 80.2 %while.19 = (s32[]{:T(128)}, f32[2,48,16]{1,2,0:T(8,128)S(1)}, f32[2,48,16]{1,2,0:T(8,128)S(1)}, f32[2,48,16,128]{3,2,1,0:T(8,128)S(1)}, f32[32,2,48,16]{2,3,1,0...) while((s32[]{:T(128)}, f32[2,48,16]{1,2,0:T(8,128)S(1)}, ...), condition=%wide.region_16.17_spmd, body=%wide.region_15.16_spmd.sunk | while | flops 599045 | bytes 2445455 | solution.py:21
  407.5 48.3 %all_gather.35 = bf16[96,2048]{0,1:T(8,128)(2,1)S(1)} all-gather(bf16[96,64]{0,1:T(8,128)(2,1)S(1)} %convolution_convert_fusion.1), channel_id=1, replica_groups=mesh['req'=8,'mp'=32] {'mp'}, dimensions={1}, use_global_device_ids=true | all-gather | bytes 405504 | tf_op jit(solution)/shard_map/all_gather | solution.py:234
  460.8 141.7 %all-reduce.2.cloned.1.call-done = bf16[96,2048]{1,0:T(8,128)(2,1)} async-done(((bf16[96,2048]{1,0:T(8,128)(2,1)}), bf16[96,2048]{1,0:T(8,128)(2,1)}) %all-reduce.2.cloned.1.call-update) | async-done | bytes 393232 | tf_op jit(solution)/shard_map/psum | solution.py:245
  (238 shorter events, 113.0 us)
Async XLA Ops:
  7.2 449.2 %copy-start = (bf16[2048,2,256]{2,1,0:T(2,128)(2,1)S(1)}, bf16[2048,2,256]{2,1,0:T(2,128)(2,1)}, u32[]{:S(2)}) copy-start(bf16[2048,2,256]{2,1,0:T(2,128)(2,1)} %param.30) | copy-start | bytes 6291460
  7.2 5.2 copy-start.1
  7.2 5.0 copy-start.14
  7.2 82.7 %all-gather.7.cloned.1.call-start = ((), (), s32[]{:S(2)}) async-start(), calls=%async_computation | async-start | bytes 1622016 | tf_op jit(solution)/shard_map/all_gather | solution.py:183
  9.7 314.7 %all-gather.9.cloned.1.call-start = ((), (), s32[]{:S(2)}) async-start(), calls=%async_computation.2 | async-start | bytes 25952256 | tf_op jit(solution)/shard_map/all_gather | solution.py:16
  12.4 5.7 copy-start.15
  22.0 4.0 copy-start.17
  22.0 4.6 copy-start.8
  96.0 2.9 copy-start.3
  105.6 2.4 copy-start.2
  114.5 8.8 %copy-start.5 = (f32[4,16,48]{0,1,2:T(8,128)S(1)}, f32[4,16,48]{0,1,2:T(8,128)}, u32[]{:S(2)}) copy-start(f32[4,16,48]{0,1,2:T(8,128)} %copy.253) | copy-start | bytes 36868
  131.8 4.0 copy-start.13
  134.3 468.2 %all-reduce.2.cloned.1.call-start = ((), (), s32[]{:S(2)}) async-start(), calls=%async_computation.1 | async-start | bytes 786432 | tf_op jit(solution)/shard_map/psum | solution.py:245
  215.6 2.6 copy-start.19
  215.6 3.4 copy-start.9
  316.1 0.8 copy-start.7
  406.2 50.0 %copy-start.4 = (bf16[96,2048]{1,0:T(8,128)(2,1)S(1)}, bf16[96,2048]{1,0:T(8,128)(2,1)}, u32[]{:S(2)}) copy-start(bf16[96,2048]{1,0:T(8,128)(2,1)} %param.21) | copy-start | bytes 1179652
  406.2 50.0 %copy-start.10 = (f32[1,2048]{1,0:T(1,128)S(1)}, f32[1,2048]{1,0:T(1,128)}, u32[]{:S(2)}) copy-start(f32[1,2048]{1,0:T(1,128)} %get-tuple-element.308) | copy-start | bytes 24580
  456.4 1.2 copy-start.6
  457.6 2.4 copy-start.12
  457.6 2.4 copy-start.16
  457.6 2.4 copy-start.18
  457.6 145.9 %copy-start.11 = (f32[1,2048]{1,0:T(1,128)S(1)}, f32[1,2048]{1,0:T(1,128)}, u32[]{:S(2)}) copy-start(f32[1,2048]{1,0:T(1,128)} %get-tuple-element.311) | copy-start | bytes 24580
Sparse Core Ops, SparseCore 0:
  11.2 78.7 all-gather.6
  134.5 189.8 all-gather.8
  458.9 143.6 all-reduce.1
where the time goes:
time: 617 us; the launch traced here: 612 us
  blocking collectives  220 us (36%)
  waiting for transfers between devices  212 us (34%)
  other arithmetic  100 us (16%)
  local copies, waits for them, and re-layouts  37.1 us (6%)
  matrix products  26.8 us (4%)
  between operations  14.1 us (2%)
    psum x1, waiting for transfers between devices, per_device(): lax.psum(jnp.dot(hidden, down_weight, preferred_element_type=jnp.float32)...  142 us
    all_gather x2, blocking collectives, combined_all(): gathered = jax.tree.map(lambda a: lax.all_gather(a, axis), part)  97.1 us
    all_gather x1, blocking collectives, per_device(): collected = lax.all_gather(drafted[None], ('req', 'mp'), axis=0, tiled=True)  74.9 us
    all_gather x1, waiting for transfers between devices, per_device(): projected = lax.all_gather(own_projection, 'mp', axis=2, tiled=True)  62.7 us
    add x32, other arithmetic, fold_states(): mixed_left * factor_left[..., None] + mixed_right * factor_right[..., None]  54 us
    all_gather x1, blocking collectives, per_device(): projected_out = lax.all_gather(out_columns, 'mp', axis=1, tiled=True)  48.3 us
    add x32, other arithmetic, fold_states(): total_left * factor_left + total_right * factor_right  24.4 us
    unnamed x45, local copies, waits for them, and re-layouts  13.5 us
  transfers between devices with their start and end apart: 3, of which 3 were waited for; matrix products, arithmetic and copies ran while one was open for 5% of the time, Pallas kernels for 0%

commit v1 on v0

v1 whole, which is shorter than its diff:
```python
import functools

import jax
import jax.numpy as jnp
from jax import lax
from jax.experimental import pallas as pl
from jax.experimental.pallas import tpu as pltpu
from jax.sharding import PartitionSpec as P

HEADS = 16
HEAD_DIM = 128
HALF = HEAD_DIM // 2
LANES = 128

rope_base = 500000.0
norm_epsilon = 1e-06
masked_score = -1e30


def tree_shape(parents):
    node_count = parents.shape[-1]
    step_one = (
        parents[..., :, None] == jnp.arange(node_count, dtype=jnp.int32)[None, None, :]
    ).astype(jnp.float32)
    step_two = jnp.einsum("rij,rjk->rik", step_one, step_one, precision=lax.Precision.HIGHEST)
    step_three = jnp.einsum("rij,rjk->rik", step_two, step_one, precision=lax.Precision.HIGHEST)
    ancestry = jnp.eye(node_count, dtype=jnp.float32)[None] + step_one + step_two + step_three
    return (ancestry, jnp.sum(ancestry, axis=-1))


def split_three(value):
    top = value.astype(jnp.bfloat16).astype(jnp.float32)
    rest = value - top
    middle = rest.astype(jnp.bfloat16).astype(jnp.float32)
    return top, middle, (rest - middle).astype(jnp.bfloat16).astype(jnp.float32)


def rotated(front, back, cosine, sine):
    return front * cosine - back * sine, back * cosine + front * sine


def pages_kernel(
    rows_request, counts, gathered, gains, cosine, sine, cache, out, queries, key_square, kv, sems
):
    pages, _, page_len, width = cache.shape
    groups = sems.shape[0]
    group_width = width // groups

    def fetch(group):
        columns = pl.ds(group * group_width, group_width)
        return pltpu.make_async_copy(
            cache.at[:, :, :, columns], kv.at[:, :, :, columns], sems.at[group]
        )

    for group in range(groups):
        fetch(group).start()
    lane = lax.broadcasted_iota(jnp.int32, (8, LANES), 1)
    squares = jnp.zeros((HALF, LANES), jnp.float32)
    extra = jnp.zeros((8, LANES), jnp.float32)
    for source in range(2 * HEADS):
        chunk = gathered[source].astype(jnp.float32)
        squares = squares + chunk * chunk
        extra = extra + chunk[0:8]
    inverse = lax.rsqrt(jnp.sum(squares, axis=0, keepdims=True) / width + norm_epsilon)
    key_square[...] = extra
    limits = []
    first = lax.broadcasted_iota(jnp.int32, (1, LANES), 1) < rows_request
    for page in range(pages):
        limits.append(jnp.where(first, counts[2 * page], counts[2 * page + 1]))
    token = lax.broadcasted_iota(jnp.int32, (page_len, LANES), 0)
    visible = [token < limit for limit in limits]
    scale = HEAD_DIM ** (-0.5)
    cos_rows = cosine[...]
    sin_rows = sine[...]
    for head in range(HEADS):
        if head % (HEADS // groups) == 0:
            fetch(head // (HEADS // groups)).wait()
        base = head * HEAD_DIM
        front = (
            gathered[2 * head].astype(jnp.float32)
            * inverse
            * gains[base : base + HALF].astype(jnp.float32)
        )
        back = (
            gathered[2 * head + 1].astype(jnp.float32)
            * inverse
            * gains[base + HALF : base + HEAD_DIM].astype(jnp.float32)
        )
        front, back = rotated(front, back, cos_rows, sin_rows)
        query = jnp.concatenate([front, back], axis=0).astype(jnp.bfloat16)
        queries[base : base + HEAD_DIM] = query
        keys = kv[:, 0, :, base : base + HEAD_DIM].reshape(pages * page_len, HEAD_DIM)
        scores = jnp.dot(keys, query, preferred_element_type=jnp.float32) * scale
        parts = [
            jnp.where(
                visible[page], scores[page * page_len : (page + 1) * page_len], masked_score
            )
            for page in range(pages)
        ]
        top = functools.reduce(jnp.maximum, parts)
        top = jnp.max(top, axis=0, keepdims=True)
        weights = [
            jnp.where(visible[page], jnp.exp(parts[page] - top), 0.0) for page in range(pages)
        ]
        total = jnp.sum(functools.reduce(jnp.add, weights), axis=0, keepdims=True)
        weight = jnp.concatenate(weights, axis=0).astype(jnp.bfloat16)
        values = kv[:, 1, :, base : base + HEAD_DIM].reshape(pages * page_len, HEAD_DIM)
        mixed = lax.dot_general(
            values, weight, (((0,), (0,)), ((), ())), preferred_element_type=jnp.float32
        )
        zero = jnp.zeros_like(top)
        stats = jnp.concatenate([*split_three(top), *split_three(total), zero, zero], axis=0)
        tail = jnp.concatenate(
            [
                pltpu.roll(stats, 96, 1),
                pltpu.roll(stats, 64, 1),
                pltpu.roll(stats, 32, 1),
                jnp.zeros((HALF - 24, LANES), jnp.float32),
            ],
            axis=0,
        )
        spare = lax.broadcasted_iota(jnp.int32, (HALF, LANES), 1) >= 96
        out[2 * head] = jnp.where(spare, tail, mixed[:HALF]).astype(jnp.bfloat16)
        out[2 * head + 1] = jnp.where(spare, tail, mixed[HALF:]).astype(jnp.bfloat16)


def unpacked(chunk):
    lane = lax.broadcasted_iota(jnp.int32, (8, LANES), 1)
    return jnp.where(
        lane < 32,
        pltpu.roll(chunk[0:8], 32, 1),
        jnp.where(lane < 64, pltpu.roll(chunk[8:16], 64, 1), pltpu.roll(chunk[16:24], 96, 1)),
    )


def tree_kernel(
    place, query, own_key, other_key, key_square, gain, cosine, sine, values, mask, keys_out, mixed_out, stats_out
):
    width = 2 * HEADS * HALF
    even = place[0] == 0
    packed = key_square[...]
    both = packed[0:3] + packed[3:6]
    lane = lax.broadcasted_iota(jnp.int32, (1, LANES), 1)
    wide = jnp.concatenate([both, jnp.zeros((5, LANES), jnp.float32)], axis=0)
    square = jnp.where(
        lane < 32,
        pltpu.roll(wide, 32, 1)[0:1],
        jnp.where(lane < 64, pltpu.roll(wide, 64, 1)[1:2], pltpu.roll(wide, 96, 1)[2:3]),
    )
    inverse = lax.rsqrt(square / width + norm_epsilon)
    own = own_key[...].astype(jnp.float32)
    other = other_key[...].astype(jnp.float32)
    gain_rows = gain[...].astype(jnp.float32)
    front = jnp.where(even, own, other) * inverse * gain_rows[:HALF]
    back = jnp.where(even, other, own) * inverse * gain_rows[HALF:]
    front, back = rotated(front, back, cosine[...], sine[...])
    keys_out[...] = jnp.where(even, front, back).astype(jnp.bfloat16)
    keys = jnp.concatenate([front, back], axis=0).astype(jnp.bfloat16)
    scores = lax.dot_general(
        keys, query[...], (((0,), (0,)), ((), ())), preferred_element_type=jnp.float32
    ) * (HEAD_DIM ** (-0.5))
    visible = mask[...] > 0.5
    scores = jnp.where(visible, scores, masked_score)
    top = jnp.max(scores, axis=0, keepdims=True)
    weights = jnp.where(visible, jnp.exp(scores - top), 0.0)
    total = jnp.sum(weights, axis=0, keepdims=True)
    mixed_out[...] = jnp.dot(
        values[...], weights.astype(jnp.bfloat16), preferred_element_type=jnp.float32
    )
    stats_out[...] = jnp.concatenate(
        [top, total, jnp.zeros((6, LANES), jnp.float32)], axis=0
    )


def merge_kernel(parts, tree_mixed, tree_stats, drafted, out):
    count = parts.shape[0]
    top_tree = tree_stats[0:1]
    tops = []
    totals = []
    for source in range(count):
        stats = unpacked(parts[source].astype(jnp.float32))
        tops.append((stats[0:1] + stats[1:2]) + stats[2:3])
        totals.append((stats[3:4] + stats[4:5]) + stats[5:6])
    top = functools.reduce(jnp.maximum, tops, top_tree)
    factor = jnp.exp(top_tree - top)
    total = factor * tree_stats[1:2]
    mixed = factor * tree_mixed[...]
    for source in range(count):
        factor = jnp.exp(tops[source] - top)
        total = total + factor * totals[source]
        mixed = mixed + factor * parts[source].astype(jnp.float32)
    spare = lax.broadcasted_iota(jnp.int32, (HALF, LANES), 1) >= 96
    result = jnp.where(spare, drafted[...].astype(jnp.float32), mixed / total).astype(jnp.bfloat16)
    for target in range(count):
        out[target] = result


def vmem(count):
    return [pl.BlockSpec(memory_space=pltpu.VMEM)] * count


SMEM = pl.BlockSpec(memory_space=pltpu.SMEM)


def broadcast_gather(chunk, count):
    copies = jnp.broadcast_to(chunk[None], (count,) + chunk.shape)
    return lax.all_to_all(copies, "mp", 0, 0)


def per_device(
    draft_hidden,
    draft_weight,
    vocab_weight,
    tree_inputs,
    tree_parent,
    cache_len,
    page_table,
    kv_cache,
    accepted_node,
    qkv_weight,
    norm_gains,
    out_weight,
    gate_up_weight,
    down_weight,
):
    mp_count = lax.axis_size("mp")
    req_count = lax.axis_size("req")
    mp_place = lax.axis_index("mp")
    req_place = lax.axis_index("req")
    req_local, model_width = draft_hidden.shape
    draft_count = draft_weight.shape[0]
    slab = draft_weight.shape[2]
    vocab_local = vocab_weight.shape[0]
    rows = tree_inputs.shape[0]
    tree_size = tree_parent.shape[1]
    page_count, _, page_len, _ = kv_cache.shape
    table_width = page_table.shape[1]
    bf16 = jnp.bfloat16
    f32 = jnp.float32

    own = jnp.einsum("td,dce->cet", tree_inputs, qkv_weight, preferred_element_type=f32).astype(bf16)
    key_part = own[1].astype(f32)
    square = jnp.sum(key_part * key_part, axis=0)
    square_top = lax.reduce_precision(square, 8, 7)
    square_rest = lax.reduce_precision(square - square_top, 8, 7)
    packed = jnp.concatenate([square_top.reshape(3, 32), square_rest.reshape(3, 32)], axis=0)
    packed = jnp.pad(packed, ((0, slab - 6), (0, 0))).astype(bf16)
    gathered = broadcast_gather(jnp.concatenate([own[0], packed], axis=1), mp_count)
    other_key = lax.ppermute(own[1], "mp", [(i, i ^ 1) for i in range(mp_count)])

    pair = lax.ppermute(draft_hidden, "req", [(i, i ^ 1) for i in range(req_count)])
    both = jnp.concatenate([draft_hidden, pair], axis=0)
    turns = req_count // 2
    hidden_parts = [both] + [
        lax.ppermute(both, "req", [(i, (i + 2 * k) % req_count) for i in range(req_count)])
        for k in range(1, turns)
    ]
    hidden_all = jnp.concatenate(hidden_parts, axis=0)
    spot = jnp.arange(req_count * req_local, dtype=jnp.int32)
    turn = spot // (2 * req_local)
    side = (spot // req_local) % 2
    holder = 2 * ((req_place // 2 - turn) % turns) + ((req_place % 2) ^ side)
    origin = holder * req_local + spot % req_local
    order = (origin[None, :] == spot[:, None]).astype(bf16)
    hidden_all = jnp.dot(order, hidden_all, preferred_element_type=f32).astype(bf16)
    draft_raw = jnp.einsum("rd,kde->erk", hidden_all, draft_weight, preferred_element_type=f32)
    own_columns = lax.dynamic_slice_in_dim(hidden_all, mp_place * slab, slab, 1).astype(f32).T
    drafted = (own_columns[:, :, None] + jax.nn.silu(draft_raw)).astype(bf16)
    drafted = drafted.reshape(slab, req_count * req_local * draft_count)

    ancestry, node_depth = tree_shape(tree_parent)
    positions = (cache_len[:, None].astype(f32) + node_depth - 1.0).reshape(rows)
    freqs = rope_base ** (-jnp.arange(HALF, dtype=f32) * 2.0 / HEAD_DIM)
    angles = jnp.pad(positions, (0, LANES - rows))[None, :] * freqs[:, None]
    cosine = jnp.cos(angles)
    sine = jnp.sin(angles)
    mask = jnp.zeros((LANES, LANES), f32)
    for r in range(req_local):
        mask = lax.dynamic_update_slice(mask, ancestry[r].T, (r * tree_size, r * tree_size))
    gain_rows = norm_gains.astype(f32)
    query_gain = jnp.broadcast_to(norm_gains[0][:, None], (model_width, LANES))
    key_gain = lax.dynamic_slice_in_dim(
        norm_gains[1], (mp_place // 2) * HEAD_DIM, HEAD_DIM, 0
    )
    key_gain = jnp.broadcast_to(key_gain[:, None], (HEAD_DIM, LANES))

    slots = (req_place * mp_count + mp_place) * page_count + jnp.arange(page_count, dtype=jnp.int32)
    matches = page_table[None, :, :] == slots[:, None, None]
    starts = jnp.arange(table_width, dtype=jnp.int32) * page_len
    left = jnp.clip(cache_len[:, None] - starts[None, :], 0, page_len)
    counts = jnp.sum(jnp.where(matches, left[None], 0), axis=2).reshape(page_count * req_local)

    groups = 4
    parts, queries, key_square = pl.pallas_call(
        functools.partial(pages_kernel, tree_size),
        out_shape=(
            jax.ShapeDtypeStruct((mp_count, slab, LANES), bf16),
            jax.ShapeDtypeStruct((model_width, LANES), bf16),
            jax.ShapeDtypeStruct((8, LANES), f32),
        ),
        in_specs=[SMEM, *vmem(4), pl.BlockSpec(memory_space=pl.ANY)],
        out_specs=tuple(vmem(3)),
        scratch_shapes=[
            pltpu.VMEM(kv_cache.shape, bf16),
            pltpu.SemaphoreType.DMA((groups,)),
        ],
        compiler_params=pltpu.CompilerParams(vmem_limit_bytes=24 * 2**20),
        cost_estimate=pl.CostEstimate(
            flops=4 * page_count * page_len * LANES * model_width,
            bytes_accessed=kv_cache.size * 2,
            transcendentals=page_count * page_len * LANES * HEADS,
        ),
        name="pages",
    )(counts, gathered, query_gain, cosine, sine, kv_cache)
    arrived = lax.all_to_all(parts, "mp", 0, 0)

    wide = lambda a: jnp.pad(a, ((0, 0), (0, LANES - rows)))
    head_query = lax.dynamic_slice_in_dim(queries, (mp_place // 2) * HEAD_DIM, HEAD_DIM, 0)
    own_keys, tree_mixed, tree_stats = pl.pallas_call(
        tree_kernel,
        out_shape=(
            jax.ShapeDtypeStruct((slab, LANES), bf16),
            jax.ShapeDtypeStruct((slab, LANES), f32),
            jax.ShapeDtypeStruct((8, LANES), f32),
        ),
        in_specs=[SMEM, *vmem(9)],
        out_specs=tuple(vmem(3)),
        name="tree",
    )(
        (mp_place % 2).reshape(1),
        head_query,
        wide(own[1]),
        wide(other_key),
        key_square,
        key_gain,
        cosine,
        sine,
        wide(own[2]),
        mask,
    )

    spare = LANES - rows
    attended_copies = pl.pallas_call(
        merge_kernel,
        out_shape=jax.ShapeDtypeStruct((mp_count, slab, LANES), bf16),
        in_specs=vmem(4),
        out_specs=vmem(1)[0],
        name="merge",
    )(
        arrived,
        tree_mixed,
        tree_stats,
        jnp.pad(drafted[:, :spare], ((0, 0), (rows, 0))),
    )
    attended = lax.all_to_all(attended_copies, "mp", 0, 0).reshape(model_width, LANES)
    out_columns = lax.dot_general(
        out_weight, attended, (((0,), (0,)), ((), ())), preferred_element_type=f32
    ).astype(bf16)
    projected_out = broadcast_gather(
        jnp.concatenate([out_columns[:, :rows], drafted[:, spare:]], axis=1), mp_count
    ).reshape(model_width, LANES)

    projected_rows = projected_out[:, :rows].astype(f32)
    mean_square = jnp.mean(projected_rows * projected_rows, axis=0, keepdims=True)
    residual = (
        tree_inputs.T.astype(f32)
        + projected_rows * lax.rsqrt(mean_square + norm_epsilon) * gain_rows[2][:, None]
    ).astype(bf16)
    gate_up = jnp.einsum("dt,dce->tce", residual, gate_up_weight, preferred_element_type=f32)
    hidden = (jax.nn.silu(gate_up[:, 0]) * gate_up[:, 1]).astype(bf16)
    row_share = rows // mp_count
    partial = jnp.dot(hidden, down_weight, preferred_element_type=f32).astype(bf16)
    shares = lax.all_to_all(partial.reshape(mp_count, row_share, model_width), "mp", 0, 0)

    drafted_all = jnp.concatenate([attended[:, rows:], projected_out[:, rows:]], axis=1)
    draft_logits = lax.dot_general(
        drafted_all, vocab_weight, (((0,), (1,)), ((), ())), preferred_element_type=f32
    ).reshape(req_count * req_local, draft_count, vocab_local)
    chosen = (accepted_node[:, None] == jnp.arange(tree_size, dtype=jnp.int32)[None, :]).astype(f32)
    on_path = jnp.einsum("rt,rts->rs", chosen, ancestry, precision=lax.Precision.HIGHEST)
    levels = jnp.arange(1, draft_count + 1, dtype=f32)
    picker = on_path[:, None, :] * (node_depth[:, None, :] == levels[None, :, None]).astype(f32)
    stacked = jnp.stack([own_keys[:, :rows], own[2]]).reshape(2, slab, req_local, tree_size)
    accepted_kv = jnp.einsum(
        "rjs,cers->rjce", picker.astype(bf16), stacked, preferred_element_type=f32
    ).astype(bf16)
    residual_rows = lax.dynamic_slice_in_dim(residual, mp_place * row_share, row_share, 1).T
    own_rows = jnp.sum(shares.astype(f32), axis=0)
    row_square = jnp.mean(own_rows * own_rows, axis=-1, keepdims=True)
    layer_out = (
        residual_rows.astype(f32)
        + own_rows * lax.rsqrt(row_square + norm_epsilon) * gain_rows[3]
    ).astype(bf16)
    return (draft_logits, layer_out, accepted_kv)


def solution(mesh):
    placed = (
        P("req", None),
        P(None, None, "mp"),
        P(("req", "mp"), None),
        P("req", None),
        P("req", None),
        P("req"),
        P("req", None),
        P(("req", "mp"), None, None, None),
        P("req"),
        P(None, None, "mp"),
        P(),
        P(None, "mp"),
        P(None, None, "mp"),
        P("mp", None),
    )
    return jax.shard_map(
        per_device,
        mesh=mesh,
        in_specs=placed,
        out_specs=(
            P(None, None, ("req", "mp")),
            P(("req", "mp"), None),
            P("req", None, None, "mp"),
        ),
        check_vma=False,
    )
```

time: 617 us -> 142 us (0.23)
  blocking collectives: 220 us -> 0 us
  waiting for transfers between devices: 212 us -> 54.6 us
  other arithmetic: 100 us -> 7.07 us
  starting transfers between devices: 0.12 us -> 37.8 us
  matrix products: 26.8 us -> 8.35 us
  local copies, waits for them, and re-layouts: 37.1 us -> 20.3 us
  between operations: 14.1 us -> 1.09 us
  Pallas kernels: 0 us -> 10.2 us
    all_gather x4 -> x0, blocking collectives: 220 us -> none  [the longest x2 97.1 us: combined_all(): gathered = jax.tree.map(lambda a: lax.all_gather(a, axis), part)]
    psum x1 -> x0, waiting for transfers between devices: 142 us -> none  [per_device(): lax.psum(jnp.dot(hidden, down_weight, preferred_element_type=jnp.float32)...]
    add x66 -> x3, other arithmetic: 78.5 us -> 0.6 us  [the longest x1 0.59 us: per_device(): origin = holder * req_local + spot % req_local]
    all_gather x2 -> x0, waiting for transfers between devices: 70.2 us -> none  [the longest x1 62.7 us: per_device(): projected = lax.all_gather(own_projection, 'mp', axis=2, tiled=True)]
    all_to_all x0 -> x5, waiting for transfers between devices: none -> 54.6 us  [the longest x2 25 us: broadcast_gather(): return lax.all_to_all(copies, 'mp', 0, 0)]
    all_to_all x0 -> x5, starting transfers between devices: none -> 33.2 us  [the longest x2 16.3 us: broadcast_gather(): return lax.all_to_all(copies, 'mp', 0, 0)]
    dot_general x9 -> x8, matrix products: 23.2 us -> 7.07 us  [the longest x1 1.76 us: per_device(): jnp.einsum('rd,kde->erk', hidden_all, draft_weight, preferred_element_typ...]
    pallas_call x0 -> x3, Pallas kernels: none -> 10.2 us  [the longest x1 5.95 us: per_device(): pl.pallas_call(functools.partial(pages_kernel, tree_size), out_shape=(jax...]
  transfers between devices with their start and end apart: 3 -> 10, of which waited for: 3 -> 5; matrix products, arithmetic and copies ran while one was open for 5% -> 17% of each run, Pallas kernels for 0% -> 6%
where the time goes in v1:
time: 142 us; the launch traced here: 139 us
  waiting for transfers between devices  54.6 us (38%)
  starting transfers between devices  37.8 us (27%)
  local copies, waits for them, and re-layouts  20.3 us (14%)
  Pallas kernels  10.2 us (7%)
  matrix products  8.35 us (6%)
  other arithmetic  7.07 us (5%)
    all_to_all x2, waiting for transfers between devices, broadcast_gather(): return lax.all_to_all(copies, 'mp', 0, 0)  25 us
    all_to_all x2, starting transfers between devices, broadcast_gather(): return lax.all_to_all(copies, 'mp', 0, 0)  16.3 us
    all_to_all x1, waiting for transfers between devices, per_device(): lax.all_to_all(attended_copies, 'mp', 0, 0).reshape(model_width, LANES)  16 us
    all_to_all x1, waiting for transfers between devices, per_device(): lax.all_to_all(partial.reshape(mp_count, row_share, model_width), 'mp', 0...  10.3 us
    all_to_all x1, starting transfers between devices, per_device(): lax.all_to_all(attended_copies, 'mp', 0, 0).reshape(model_width, LANES)  6.44 us
    pallas_call x1, Pallas kernels, per_device(): pl.pallas_call(functools.partial(pages_kernel, tree_size), out_shape=(jax...  5.95 us
    unnamed x48, local copies, waits for them, and re-layouts  5.59 us
    all_to_all x1, starting transfers between devices, per_device(): arrived = lax.all_to_all(parts, 'mp', 0, 0)  5.26 us
  transfers between devices with their start and end apart: 10, of which 5 were waited for; matrix products, arithmetic and copies ran while one was open for 17% of the time, Pallas kernels for 6%

profile of v1, /device:TPU:48, one launch (start us, length us, event | category | flops | bytes accessed | tf_op | source)
XLA Modules:
  0.0 139.4 jit_solution(3143189567727605870)
XLA Ops:
  0.8 1.7 %convolution_convert_fusion.2 = bf16[3,64,96]{2,1,0:T(8,128)(2,1)S(1)} fusion(bf16[2048,3,64]{0,2,1:T(8,128)(2,1)} %param.23, bf16[96,2048]{1,0:T(8,128)(2,1)} %param.17), kind=kOutput, calls=%fused_computation.4 | convolution fusion | flops 75515904 | bytes 1216512 | tf_op jit(solution)/shard_map/td,dce->cet/dot_general | solution.py:241
  3.7 11.2 %all-to-all-start = ((bf16[32,64,128]{2,1,0:T(8,128)(2,1)}), bf16[32,64,128]{2,1,0:T(8,128)(2,1)S(1)}, u32[]{:S(2)}, u32[]{:S(2)}) async-start(bf16[32,64,128]{2,1,0:T(8,128)(2,1)} %broadcast_in_dim.22), calls=%async_computation | async-start | bytes 1048576 | tf_op jit(solution)/shard_map/all_to_all | solution.py:207
  14.9 1.6 %collective-permute-start = (bf16[64,96]{1,0:T(8,128)(2,1)S(1)}, bf16[64,96]{1,0:T(8,128)(2,1)}, u32[]{:S(2)}, u32[]{:S(2)}) collective-permute-start(bf16[64,96]{1,0:T(8,128)(2,1)S(1)} %get-tuple-element.29), channel_id=1, source_target_pairs={{0,1},{1,0},{2,3},{3,2},{4,5},{5,4},{6,7},{7,6},{8,9},{9,8},{10,11... | collective-permute-start | bytes 36872 | tf_op jit(solution)/shard_map/ppermute | solution.py:249
  19.1 1.3 collective-permute-start.2
  22.1 10.4 %all-to-all-done.gathered = bf16[32,64,128]{2,1,0:T(8,128)(2,1)S(1)} async-done(((bf16[32,64,128]{2,1,0:T(8,128)(2,1)}), bf16[32,64,128]{2,1,0:T(8,128)(2,1)S(1)}, u32[]{:S(2)}, u32[]{:S(2)}) %all-to-all-start) | async-done | bytes 524320 | tf_op jit(solution)/shard_map/all_to_all | solution.py:207
  32.9 2.2 %copy-done.1 = bf16[4,2,128,2048]{3,2,1,0:T(8,128)(2,1)S(1)} copy-done((bf16[4,2,128,2048]{3,2,1,0:T(8,128)(2,1)S(1)}, bf16[4,2,128,2048]{3,2,1,0:T(8,128)(2,1)}, u32[]{:S(2)}) %copy-start.1) | copy-done | bytes 4194328
  35.1 6.0 %pages.1 = (bf16[32,64,128]{2,1,0:T(8,128)(2,1)}, bf16[2048,128]{1,0:T(8,128)(2,1)S(1)}, f32[8,128]{1,0:T(8,128)S(1)}) custom-call(s32[8]{0:T(128)S(1)} %reshape.182.counts, bf16[32,64,128]{2,1,0:T(8,128)(2,1)S(1)} %all-to-all-done.gathered, bf16[2048,128]{1,0:T(8,128)(2,1)S(1)} %broadcast_in_dim.24.gains, f32[64,128]{1,0:T(8,128)S(1)} %get-tuple-element.42.cosine, ...), custom_call_target="tpu_custom_call" | custom-call | flops 536870912 | bytes 4194304 | tf_op jit(solution)/shard_map/pages/pallas_call | solution.py:294
  41.7 5.3 %all-to-all-start.1 = ((bf16[32,64,128]{2,1,0:T(8,128)(2,1)}), bf16[32,64,128]{2,1,0:T(8,128)(2,1)S(1)}, u32[]{:S(2)}, u32[]{:S(2)}) async-start(bf16[32,64,128]{2,1,0:T(8,128)(2,1)} %get-tuple-element.9), calls=%async_computation.1 | async-start | bytes 1048576 | tf_op jit(solution)/shard_map/all_to_all | solution.py:315
  49.9 1.3 pad.27.other_key
  51.2 1.6 %concatenate.24 = bf16[16,2048]{1,0:T(8,128)(2,1)S(1)} concatenate(bf16[2,2048]{1,0:T(2,128)(2,1)} %param.14, bf16[2,2048]{1,0:T(2,128)(2,1)} %copy-done.15, bf16[4,2048]{1,0:T(4,128)(2,1)} %collective-permute-done.2, bf16[4,2048]{1,0:T(4,128)(2,1)} %collective-permute-done.3, bf16[4,2048]{1,0:T(4,128)(2,1)} %collective-permute-done.4), dimensions={0} | concatenate | bytes 131072 | tf_op jit(solution)/shard_map/concatenate | solution.py:258
  53.7 1.8 %add_convert_fusion = bf16[64,16,4]{0,1,2:T(8,128)(2,1)S(1)} fusion(bf16[4,2048,64]{1,2,0:T(8,128)(2,1)} %param.15, bf16[16,2048]{1,0:T(8,128)(2,1)S(1)} %convolution_convert_fusion.1, f32[64,16]{0,1:T(8,128)S(1)} %convert_bitcast_fusion), kind=kOutput, calls=%fused_computation.42 | convolution fusion | flops 16801792 | bytes 1126400 | tf_op jit(solution)/shard_map/rd,kde->erk/dot_general | solution.py:266
  56.9 1.4 broadcast_in_dim.26.gain
  58.2 2.0 %tree.1 = (bf16[64,128]{1,0:T(8,128)(2,1)}, f32[64,128]{1,0:T(8,128)}, f32[8,128]{1,0:T(8,128)}) custom-call(s32[1]{0:T(128)} %bitcast.3.place, bf16[128,128]{1,0:T(8,128)(2,1)} %constant_dynamic-slice_fusion.1.query, bf16[64,128]{1,0:T(8,128)(2,1)} %pad.26.own_key, bf16[64,128]{1,0:T(8,128)(2,1)} %pad.27.other_key, f32[8,128]{1,0:T(8,128)} %copy-done.4, ...), custom_call_target="tpu_custom_call" | custom-call | tf_op jit(solution)/shard_map/tree/pallas_call | solution.py:319
  60.2 3.3 %all-to-all-done.1.parts = bf16[32,64,128]{2,1,0:T(8,128)(2,1)S(1)} async-done(((bf16[32,64,128]{2,1,0:T(8,128)(2,1)}), bf16[32,64,128]{2,1,0:T(8,128)(2,1)S(1)}, u32[]{:S(2)}, u32[]{:S(2)}) %all-to-all-start.1) | async-done | bytes 524320 | tf_op jit(solution)/shard_map/all_to_all | solution.py:315
  64.4 2.2 %merge.1 = bf16[32,64,128]{2,1,0:T(8,128)(2,1)} custom-call(bf16[32,64,128]{2,1,0:T(8,128)(2,1)} %copy-done.5, f32[64,128]{1,0:T(8,128)} %get-tuple-element.12.tree_mixed, f32[8,128]{1,0:T(8,128)} %get-tuple-element.13.tree_stats, bf16[64,128]{1,0:T(8,128)(2,1)} %pad.29.drafted), custom_call_target="tpu_custom_call" | custom-call | tf_op jit(solution)/shard_map/merge/pallas_call | solution.py:343
  66.6 6.4 %all-to-all-start.2 = ((bf16[32,64,128]{2,1,0:T(8,128)(2,1)}), bf16[32,64,128]{2,1,0:T(8,128)(2,1)S(1)}, u32[]{:S(2)}, u32[]{:S(2)}) async-start(bf16[32,64,128]{2,1,0:T(8,128)(2,1)} %merge.1), calls=%async_computation.2 | async-start | bytes 1048576 | tf_op jit(solution)/shard_map/all_to_all | solution.py:355
  73.1 16.0 %all-to-all-done.2 = bf16[32,64,128]{2,1,0:T(8,128)(2,1)S(1)} async-done(((bf16[32,64,128]{2,1,0:T(8,128)(2,1)}), bf16[32,64,128]{2,1,0:T(8,128)(2,1)S(1)}, u32[]{:S(2)}, u32[]{:S(2)}) %all-to-all-start.2) | async-done | bytes 524320 | tf_op jit(solution)/shard_map/all_to_all | solution.py:355
  90.3 5.1 %all-to-all-start.3 = ((bf16[32,64,128]{2,1,0:T(8,128)(2,1)}), bf16[32,64,128]{2,1,0:T(8,128)(2,1)S(1)}, u32[]{:S(2)}, u32[]{:S(2)}) async-start(bf16[32,64,128]{2,1,0:T(8,128)(2,1)} %broadcast_in_dim.27), calls=%async_computation.3 | async-start | bytes 1048576 | tf_op jit(solution)/shard_map/all_to_all | solution.py:207
  96.7 14.6 %all-to-all-done.3 = bf16[32,64,128]{2,1,0:T(8,128)(2,1)S(1)} async-done(((bf16[32,64,128]{2,1,0:T(8,128)(2,1)}), bf16[32,64,128]{2,1,0:T(8,128)(2,1)S(1)}, u32[]{:S(2)}, u32[]{:S(2)}) %all-to-all-start.3) | async-done | bytes 524320 | tf_op jit(solution)/shard_map/all_to_all | solution.py:207
  111.7 1.3 fusion.6
  115.5 5.2 %all-to-all-start.4 = ((bf16[32,3,2048]{2,1,0:T(4,128)(2,1)}), bf16[32,3,2048]{2,1,0:T(4,128)(2,1)}, u32[]{:S(2)}, u32[]{:S(2)}) async-start(bf16[32,3,2048]{2,1,0:T(4,128)(2,1)} %reshape.188), calls=%async_computation.4 | async-start | bytes 1048576 | tf_op jit(solution)/shard_map/all_to_all | solution.py:373
  126.2 10.3 %all-to-all-done.4 = bf16[32,3,2048]{2,1,0:T(4,128)(2,1)} async-done(((bf16[32,3,2048]{2,1,0:T(4,128)(2,1)}), bf16[32,3,2048]{2,1,0:T(4,128)(2,1)}, u32[]{:S(2)}, u32[]{:S(2)}) %all-to-all-start.4) | async-done | bytes 393248 | tf_op jit(solution)/shard_map/all_to_all | solution.py:373
  136.5 1.3 convert_reduce_fusion
  137.9 1.5 %fusion.24 = bf16[3,2048]{1,0:T(4,128)(2,1)} fusion(f32[3,2048]{1,0:T(4,128)S(1)} %convert_reduce_fusion, f32[2048]{0:T(1024)S(1)} %bitcast.95, f32[3]{0:T(128)S(1)} %add_rsqrt_fusion, bf16[2048,96]{0,1:T(8,128)(2,1)} %copy-done.9, s32[]{:T(128)S(6)} %select_n.87), kind=kLoop, calls=%fused_computation.40 | loop fusion | flops 30720 | bytes 57360 | tf_op jit(solution)/shard_map/convert_element_type | solution.py:393
  (114 shorter events, 23.5 us)
Async XLA Ops:
  0.6 113.1 %copy-start = (bf16[2048,2,256]{2,1,0:T(2,128)(2,1)S(1)}, bf16[2048,2,256]{2,1,0:T(2,128)(2,1)}, u32[]{:S(2)}) copy-start(bf16[2048,2,256]{2,1,0:T(2,128)(2,1)} %param.26) | copy-start | bytes 6291460
  0.6 17.9 %copy-start.14 = (bf16[2,2048]{1,0:T(2,128)(2,1)S(1)}, bf16[2,2048]{1,0:T(2,128)(2,1)}, u32[]{:S(2)}) copy-start(bf16[2,2048]{1,0:T(2,128)(2,1)} %param.14) | copy-start | bytes 24580
  0.7 15.8 %copy-start.20 = (s32[2]{0:T(128)S(1)}, s32[2]{0:T(128)}, u32[]{:S(2)}) copy-start(s32[2]{0:T(128)} %param.19) | copy-start | bytes 28
  0.7 15.9 %copy-start.17 = (s32[2,48]{1,0:T(2,128)S(1)}, s32[2,48]{1,0:T(2,128)}, u32[]{:S(2)}) copy-start(s32[2,48]{1,0:T(2,128)} %param.18) | copy-start | bytes 1156
  0.7 16.3 %copy-start.19 = (s32[2,64]{1,0:T(2,128)S(1)}, s32[2,64]{1,0:T(2,128)}, u32[]{:S(2)}) copy-start(s32[2,64]{1,0:T(2,128)} %param.20) | copy-start | bytes 1540
  0.7 16.8 %copy-start.12 = (bf16[4,2048]{1,0:T(4,128)(2,1)S(1)}, bf16[4,2048]{1,0:T(4,128)(2,1)}, u32[]{:S(2)}) copy-start(bf16[4,2048]{1,0:T(4,128)(2,1)} %param.24) | copy-start | bytes 49156
  0.7 17.8 %collective-permute-start.1 = (bf16[2,2048]{1,0:T(2,128)(2,1)}, bf16[2,2048]{1,0:T(2,128)(2,1)S(1)}, u32[]{:S(2)}, u32[]{:S(2)}) collective-permute-start(bf16[2,2048]{1,0:T(2,128)(2,1)} %param.14), channel_id=1, source_target_pairs={{0,32},{32,0},{64,96},{96,64},{128,160},{160,128},{192,224},{224,1... | collective-permute-start | bytes 24584 | tf_op jit(solution)/shard_map/ppermute | solution.py:251
  3.7 28.9 %all-to-all-start = ((bf16[32,64,128]{2,1,0:T(8,128)(2,1)}), bf16[32,64,128]{2,1,0:T(8,128)(2,1)S(1)}, u32[]{:S(2)}, u32[]{:S(2)}) async-start(bf16[32,64,128]{2,1,0:T(8,128)(2,1)} %broadcast_in_dim.22), calls=%async_computation | async-start | bytes 1048576 | tf_op jit(solution)/shard_map/all_to_all | solution.py:207
  14.9 35.0 %collective-permute-start = (bf16[64,96]{1,0:T(8,128)(2,1)S(1)}, bf16[64,96]{1,0:T(8,128)(2,1)}, u32[]{:S(2)}, u32[]{:S(2)}) collective-permute-start(bf16[64,96]{1,0:T(8,128)(2,1)S(1)} %get-tuple-element.29), channel_id=1, source_target_pairs={{0,1},{1,0},{2,3},{3,2},{4,5},{5,4},{6,7},{7,6},{8,9},{9,8},{10,11... | collective-permute-start | bytes 36872 | tf_op jit(solution)/shard_map/ppermute | solution.py:249
  16.9 16.0 %copy-start.8 = (f32[2,48,48]{1,2,0:T(8,128)}, f32[2,48,48]{1,2,0:T(8,128)S(1)}, u32[]{:S(2)}) copy-start(f32[2,48,48]{1,2,0:T(8,128)S(1)} %get-tuple-element.44) | copy-start | bytes 55300
  17.7 23.4 %copy-start.2 = (f32[64,128]{1,0:T(8,128)}, f32[64,128]{1,0:T(8,128)S(1)}, u32[]{:S(2)}) copy-start(f32[64,128]{1,0:T(8,128)S(1)} %get-tuple-element.41.sine) | copy-start | bytes 98308
  17.7 23.4 %copy-start.3 = (f32[64,128]{1,0:T(8,128)}, f32[64,128]{1,0:T(8,128)S(1)}, u32[]{:S(2)}) copy-start(f32[64,128]{1,0:T(8,128)S(1)} %get-tuple-element.42.cosine) | copy-start | bytes 98308
  18.5 22.6 %copy-start.15 = (bf16[2,2048]{1,0:T(2,128)(2,1)}, bf16[2,2048]{1,0:T(2,128)(2,1)S(1)}, u32[]{:S(2)}) copy-start(bf16[2,2048]{1,0:T(2,128)(2,1)S(1)} %collective-permute-done.1) | copy-start | bytes 24580
  19.1 32.1 %collective-permute-start.2 = (bf16[4,2048]{1,0:T(4,128)(2,1)}, bf16[4,2048]{1,0:T(4,128)(2,1)}, u32[]{:S(2)}, u32[]{:S(2)}) collective-permute-start(bf16[4,2048]{1,0:T(4,128)(2,1)} %pad_maximum_fusion.1), channel_id=1, source_target_pairs={{0,64},{32,96},{64,128},{96,160},{128,192},{160,224},{192,0},{224,... | collective-permute-start | bytes 49160 | tf_op jit(solution)/shard_map/ppermute | solution.py:255
  20.4 30.8 %collective-permute-start.3 = (bf16[4,2048]{1,0:T(4,128)(2,1)}, bf16[4,2048]{1,0:T(4,128)(2,1)}, u32[]{:S(2)}, u32[]{:S(2)}) collective-permute-start(bf16[4,2048]{1,0:T(4,128)(2,1)} %pad_maximum_fusion.1), channel_id=1, source_target_pairs={{0,128},{32,160},{64,192},{96,224},{128,0},{160,32},{192,64},{224,... | collective-permute-start | bytes 49160 | tf_op jit(solution)/shard_map/ppermute | solution.py:255
  21.0 30.2 %collective-permute-start.4 = (bf16[4,2048]{1,0:T(4,128)(2,1)}, bf16[4,2048]{1,0:T(4,128)(2,1)}, u32[]{:S(2)}, u32[]{:S(2)}) collective-permute-start(bf16[4,2048]{1,0:T(4,128)(2,1)} %pad_maximum_fusion.1), channel_id=1, source_target_pairs={{0,192},{32,224},{64,0},{96,32},{128,64},{160,96},{192,128},{224,1... | collective-permute-start | bytes 49160 | tf_op jit(solution)/shard_map/ppermute | solution.py:255
  41.7 21.9 %all-to-all-start.1 = ((bf16[32,64,128]{2,1,0:T(8,128)(2,1)}), bf16[32,64,128]{2,1,0:T(8,128)(2,1)S(1)}, u32[]{:S(2)}, u32[]{:S(2)}) async-start(bf16[32,64,128]{2,1,0:T(8,128)(2,1)} %get-tuple-element.9), calls=%async_computation.1 | async-start | bytes 1048576 | tf_op jit(solution)/shard_map/all_to_all | solution.py:315
  48.7 40.4 %copy-start.10 = (bf16[2048,64]{0,1:T(8,128)(2,1)S(1)}, bf16[2048,64]{0,1:T(8,128)(2,1)}, u32[]{:S(2)}) copy-start(bf16[2048,64]{0,1:T(8,128)(2,1)} %param.25) | copy-start | bytes 786436
  64.4 31.1 %copy-start.21 = (s32[2]{0:T(128)S(1)}, s32[2]{0:T(128)}, u32[]{:S(2)}) copy-start(s32[2]{0:T(128)} %param.22) | copy-start | bytes 28
  64.4 31.7 %copy-start.13 = (bf16[4,2048]{1,0:T(4,128)(2,1)S(1)}, bf16[4,2048]{1,0:T(4,128)(2,1)}, u32[]{:S(2)}) copy-start(bf16[4,2048]{1,0:T(4,128)(2,1)} %param.24) | copy-start | bytes 49156
  66.6 22.5 %all-to-all-start.2 = ((bf16[32,64,128]{2,1,0:T(8,128)(2,1)}), bf16[32,64,128]{2,1,0:T(8,128)(2,1)S(1)}, u32[]{:S(2)}, u32[]{:S(2)}) async-start(bf16[32,64,128]{2,1,0:T(8,128)(2,1)} %merge.1), calls=%async_computation.2 | async-start | bytes 1048576 | tf_op jit(solution)/shard_map/all_to_all | solution.py:355
  90.3 20.9 %all-to-all-start.3 = ((bf16[32,64,128]{2,1,0:T(8,128)(2,1)}), bf16[32,64,128]{2,1,0:T(8,128)(2,1)S(1)}, u32[]{:S(2)}, u32[]{:S(2)}) async-start(bf16[32,64,128]{2,1,0:T(8,128)(2,1)} %broadcast_in_dim.27), calls=%async_computation.3 | async-start | bytes 1048576 | tf_op jit(solution)/shard_map/all_to_all | solution.py:207
  115.5 20.9 %all-to-all-start.4 = ((bf16[32,3,2048]{2,1,0:T(4,128)(2,1)}), bf16[32,3,2048]{2,1,0:T(4,128)(2,1)}, u32[]{:S(2)}, u32[]{:S(2)}) async-start(bf16[32,3,2048]{2,1,0:T(4,128)(2,1)} %reshape.188), calls=%async_computation.4 | async-start | bytes 1048576 | tf_op jit(solution)/shard_map/all_to_all | solution.py:373
  124.4 13.4 %copy-start.16 = (f32[1,2048]{1,0:T(1,128)S(1)}, f32[1,2048]{1,0:T(1,128)}, u32[]{:S(2)}) copy-start(f32[1,2048]{1,0:T(1,128)} %get-tuple-element.33) | copy-start | bytes 24580
  (8 other events, 17.8 us)

commit v2 on v1

v2 whole, which is shorter than its diff:
```python
import functools

import jax
import jax.numpy as jnp
from jax import lax
from jax.experimental import pallas as pl
from jax.experimental.pallas import tpu as pltpu
from jax.sharding import PartitionSpec as P

HEADS = 16
HEAD_DIM = 128
HALF = HEAD_DIM // 2
LANES = 128

rope_base = 500000.0
norm_epsilon = 1e-06
masked_score = -1e30


def tree_shape(parents):
    node_count = parents.shape[-1]
    step_one = (
        parents[..., :, None] == jnp.arange(node_count, dtype=jnp.int32)[None, None, :]
    ).astype(jnp.float32)
    step_two = jnp.einsum("rij,rjk->rik", step_one, step_one, precision=lax.Precision.HIGHEST)
    step_three = jnp.einsum("rij,rjk->rik", step_two, step_one, precision=lax.Precision.HIGHEST)
    ancestry = jnp.eye(node_count, dtype=jnp.float32)[None] + step_one + step_two + step_three
    return (ancestry, jnp.sum(ancestry, axis=-1))


def split_three(value):
    top = value.astype(jnp.bfloat16).astype(jnp.float32)
    rest = value - top
    middle = rest.astype(jnp.bfloat16).astype(jnp.float32)
    return top, middle, (rest - middle).astype(jnp.bfloat16).astype(jnp.float32)


def in_first(rows):
    return lax.broadcasted_iota(jnp.int32, (rows, LANES), 1) < HALF


def paired(left, right):
    first = in_first(left.shape[0])
    return (
        jnp.where(first, left, pltpu.roll(right, HALF, 1)),
        jnp.where(first, pltpu.roll(left, HALF, 1), right),
    )


def packed_inverse(squares, width):
    first = in_first(squares.shape[0])
    zero = jnp.zeros_like(squares)
    left = jnp.sum(jnp.where(first, squares, zero), axis=1, keepdims=True)
    right = jnp.sum(jnp.where(first, zero, squares), axis=1, keepdims=True)
    return lax.rsqrt(jnp.where(first, left, right) / width + norm_epsilon)


def columns_to_rows(columns):
    rest = LANES - columns.shape[0]
    return jnp.concatenate([columns, jnp.zeros((rest, LANES), jnp.float32)], axis=0).T


def pages_kernel(
    counts, owners, gathered, gains, cosine, sine, cache, out, queries, key_square, kv, held, sems
):
    pages, _, page_len, width = cache.shape
    nodes = cosine.shape[0]
    groups = sems.shape[0]
    group_width = width // groups

    def fetch(group):
        columns = pl.ds(group * group_width, group_width)
        return pltpu.make_async_copy(
            cache.at[:, :, :, columns], kv.at[:, :, :, columns], sems.at[group]
        )

    for group in range(groups):
        fetch(group).start()
    squares = jnp.zeros((nodes, LANES), jnp.float32)
    extra = jnp.zeros((8, LANES), jnp.float32)
    for source in range(2 * HEADS):
        chunk = gathered[source].astype(jnp.float32)
        squares = squares + chunk[:nodes] * chunk[:nodes]
        extra = extra + chunk[nodes : nodes + 8]
    inverse = packed_inverse(squares, width)
    key_square[...] = extra
    token = lax.broadcasted_iota(jnp.int32, (nodes, page_len), 1)
    bias = [jnp.where(token < counts[page], 0.0, masked_score) for page in range(pages)]
    second = [jnp.full((nodes, LANES), owners[page], jnp.int32) == 1 for page in range(pages)]
    scale = HEAD_DIM ** (-0.5)
    cos_rows = cosine[...]
    sin_rows = sine[...]
    lane = lax.broadcasted_iota(jnp.int32, (nodes, LANES), 1)
    stats = jnp.zeros((nodes, LANES), jnp.float32)
    for head in range(HEADS):
        if head % (HEADS // groups) == 0:
            fetch(head // (HEADS // groups)).wait()
        base = head * HEAD_DIM
        front = gathered[2 * head][:nodes].astype(jnp.float32) * inverse * gains[2 * head : 2 * head + 1]
        back = gathered[2 * head + 1][:nodes].astype(jnp.float32) * inverse * gains[2 * head + 1 : 2 * head + 2]
        front, back = rotated(front, back, cos_rows, sin_rows)
        mine = paired(front, back)
        both = jnp.concatenate(mine, axis=0).astype(jnp.bfloat16)
        queries[head] = both
        scores = []
        for page in range(pages):
            asked = jnp.where(second[page], mine[1], mine[0]).astype(jnp.bfloat16)
            keys = kv[page, 0, :, base : base + HEAD_DIM]
            score = lax.dot_general(
                asked, keys, (((1,), (1,)), ((), ())), preferred_element_type=jnp.float32
            )
            scores.append(score * scale + bias[page])
        low = jnp.full((nodes, LANES), masked_score, jnp.float32)
        tops = []
        for request in range(2):
            best = functools.reduce(
                jnp.maximum,
                [
                    jnp.where(second[page] == (request == 1), scores[page], low)
                    for page in range(pages)
                ],
            )
            tops.append(jnp.max(best, axis=1, keepdims=True))
        zero = jnp.zeros((nodes, LANES), jnp.float32)
        sums = [zero, zero]
        mixed = [zero, zero]
        for page in range(pages):
            weight = jnp.exp(scores[page] - jnp.where(second[page], tops[1], tops[0]))
            values = kv[page, 1, :, base : base + HEAD_DIM]
            share = jnp.dot(
                weight.astype(jnp.bfloat16), values, preferred_element_type=jnp.float32
            )
            for request in range(2):
                mine_too = second[page] == (request == 1)
                sums[request] = sums[request] + jnp.where(mine_too, weight, zero)
                mixed[request] = mixed[request] + jnp.where(mine_too, share, zero)
        found = [*tops, *[jnp.sum(part, axis=1, keepdims=True) for part in sums]]
        for place, column in enumerate(found):
            stats = jnp.where(lane == place * HEADS + head, column, stats)
        left, right = paired(mixed[0], mixed[1])
        held[2 * head] = left
        held[2 * head + 1] = right
    turned = columns_to_rows(stats)
    first = in_first(HEADS)

    def by_request(place):
        left = turned[place * HEADS : (place + 1) * HEADS]
        right = turned[(place + 1) * HEADS : (place + 2) * HEADS]
        return jnp.where(first, left, pltpu.roll(right, HALF, 1))

    rows = [*split_three(by_request(0)), *split_three(by_request(2))]
    rows += [jnp.zeros_like(rows[0])] * 2
    for head in range(HEADS):
        tail = jnp.concatenate([row[head : head + 1] for row in rows], axis=0)
        for half in range(2):
            block = jnp.concatenate([held[2 * head + half], tail], axis=0)
            out[2 * head + half] = block.astype(jnp.bfloat16)


def tree_kernel(
    place,
    accepted,
    queries,
    own_key,
    other_key,
    own_value,
    key_square,
    gains,
    cosine,
    sine,
    ancestry,
    depth,
    path_out,
    mixed_out,
    stats_out,
):
    width = 2 * HEADS * HALF
    requests, nodes, _ = ancestry.shape
    head = place[0] // 2
    even = jnp.full((nodes, LANES), place[0] % 2, jnp.int32) == 0
    first = in_first(nodes)
    sums = key_square[0:1] + key_square[1:2]
    square = jnp.broadcast_to(sums, (LANES, LANES)).T
    square = jnp.where(first, square[:nodes], square[nodes : 2 * nodes])
    inverse = lax.rsqrt(square / width + norm_epsilon)
    own = own_key[...].astype(jnp.float32)
    other = other_key[...].astype(jnp.float32)
    front = jnp.where(even, own, other) * inverse * gains[pl.ds(2 * head, 1)]
    back = jnp.where(even, other, own) * inverse * gains[pl.ds(2 * head + 1, 1)]
    front, back = rotated(front, back, cosine[...], sine[...])
    kept = jnp.where(even, front, back).astype(jnp.bfloat16)
    keys = paired(front, back)
    value = own_value[...]
    query = queries[head]
    lane = lax.broadcasted_iota(jnp.int32, (nodes, LANES), 1)
    stats = jnp.zeros((nodes, LANES), jnp.float32)
    mixed = []
    pickers = []
    for request in range(requests):
        line = ancestry[request]
        scores = lax.dot_general(
            query[request * nodes : (request + 1) * nodes],
            keys[request].astype(jnp.bfloat16),
            (((1,), (1,)), ((), ())),
            preferred_element_type=jnp.float32,
        ) * (HEAD_DIM ** (-0.5))
        visible = line > 0.5
        scores = jnp.where(visible, scores, masked_score)
        top = jnp.max(scores, axis=1, keepdims=True)
        weights = jnp.where(visible, jnp.exp(scores - top), 0.0)
        total = jnp.sum(weights, axis=1, keepdims=True)
        mixed.append(jnp.dot(weights.astype(jnp.bfloat16), value, preferred_element_type=jnp.float32))
        stats = jnp.where(lane == request, top, stats)
        stats = jnp.where(lane == request + 2, total, stats)
        on_path = ancestry[request, pl.ds(accepted[request], 1), :]
        levels = depth[pl.ds(request, 1), :]
        wanted = (lax.broadcasted_iota(jnp.int32, (8, nodes), 0) + 1).astype(jnp.float32)
        picker = jnp.where(wanted == levels, on_path, 0.0).astype(jnp.bfloat16)
        pickers.append(picker)
    mixed_out[...] = jnp.where(first, mixed[0], mixed[1])
    turned = columns_to_rows(stats)
    row = in_first(1)
    stats_out[0:1] = jnp.where(row, turned[0:1], pltpu.roll(turned[1:2], HALF, 1))
    stats_out[1:2] = jnp.where(row, turned[2:3], pltpu.roll(turned[3:4], HALF, 1))
    for kind, block in enumerate((kept, value)):
        picked = [
            jnp.dot(picker, block, preferred_element_type=jnp.float32) for picker in pickers
        ]
        path_out[kind] = jnp.where(in_first(8), picked[0], picked[1])


def merge_kernel(parts, tree_mixed, tree_stats, drafted, out):
    count = parts.shape[0]
    nodes = tree_mixed.shape[0]
    top_tree = tree_stats[0:1]
    tops = []
    totals = []
    for source in range(count):
        tail = parts[source].astype(jnp.float32)[nodes : nodes + 8]
        tops.append((tail[0:1] + tail[1:2]) + tail[2:3])
        totals.append((tail[3:4] + tail[4:5]) + tail[5:6])
    tops = jnp.concatenate(tops, axis=0)
    totals = jnp.concatenate(totals, axis=0)
    top = jnp.maximum(jnp.max(tops, axis=0, keepdims=True), top_tree)
    factors = jnp.exp(tops - top)
    factor_tree = jnp.exp(top_tree - top)
    total = jnp.sum(factors * totals, axis=0, keepdims=True) + factor_tree * tree_stats[1:2]
    shares = jnp.concatenate([factors / total, factor_tree / total], axis=0)
    turned = columns_to_rows(shares)
    first = in_first(nodes)

    def spread(source):
        return jnp.where(
            first,
            turned[0:nodes, source : source + 1],
            turned[HALF : HALF + nodes, source : source + 1],
        )

    mixed = spread(count) * tree_mixed[...]
    for source in range(count):
        mixed = mixed + spread(source) * parts[source].astype(jnp.float32)[:nodes]
    result = jnp.concatenate([mixed, drafted[...].astype(jnp.float32)], axis=0).astype(jnp.bfloat16)
    for target in range(count):
        out[target] = result


def out_kernel(gathered, weight, drafted, out):
    count = gathered.shape[0]
    nodes = gathered.shape[1] - drafted.shape[0]
    total = jnp.zeros((2 * nodes, LANES), jnp.float32)
    for head in range(count // 2):
        both = paired(
            gathered[2 * head][:nodes].astype(jnp.float32),
            gathered[2 * head + 1][:nodes].astype(jnp.float32),
        )
        block = jnp.concatenate(both, axis=0).astype(jnp.bfloat16)
        total = total + lax.dot_general(
            block,
            weight[:, head * HEAD_DIM : (head + 1) * HEAD_DIM],
            (((1,), (1,)), ((), ())),
            preferred_element_type=jnp.float32,
        )
    packed = jnp.where(in_first(nodes), total[:nodes], total[nodes:])
    result = jnp.concatenate([packed, drafted[...].astype(jnp.float32)], axis=0).astype(jnp.bfloat16)
    for target in range(count):
        out[target] = result


def residual_kernel(gathered, gain, inputs, out):
    count = gathered.shape[0]
    nodes = inputs.shape[0] // 2
    squares = jnp.zeros((nodes, LANES), jnp.float32)
    for source in range(count):
        chunk = gathered[source].astype(jnp.float32)[:nodes]
        squares = squares + chunk * chunk
    inverse = packed_inverse(squares, count * HALF)
    for head in range(count // 2):
        both = paired(
            gathered[2 * head].astype(jnp.float32)[:nodes] * inverse,
            gathered[2 * head + 1].astype(jnp.float32)[:nodes] * inverse,
        )
        columns = slice(head * HEAD_DIM, (head + 1) * HEAD_DIM)
        block = jnp.concatenate(both, axis=0) * gain[:, columns]
        out[:, columns] = (inputs[:, columns].astype(jnp.float32) + block).astype(jnp.bfloat16)


def split_three(value):
    top = value.astype(jnp.bfloat16).astype(jnp.float32)
    rest = value - top
    middle = rest.astype(jnp.bfloat16).astype(jnp.float32)
    return top, middle, (rest - middle).astype(jnp.bfloat16).astype(jnp.float32)


def in_first(rows):
    return lax.broadcasted_iota(jnp.int32, (rows, LANES), 1) < HALF


def paired(left, right):
    first = in_first(left.shape[0])
    return (
        jnp.where(first, left, pltpu.roll(right, HALF, 1)),
        jnp.where(first, pltpu.roll(left, HALF, 1), right),
    )


def packed_inverse(squares, width):
    first = in_first(squares.shape[0])
    zero = jnp.zeros_like(squares)
    left = jnp.sum(jnp.where(first, squares, zero), axis=1, keepdims=True)
    right = jnp.sum(jnp.where(first, zero, squares), axis=1, keepdims=True)
    return lax.rsqrt(jnp.where(first, left, right) / width + norm_epsilon)


def columns_to_rows(columns):
    rest = LANES - columns.shape[0]
    return jnp.concatenate([columns, jnp.zeros((rest, LANES), jnp.float32)], axis=0).T


def pages_kernel(
    counts, owners, gathered, gains, cosine, sine, cache, out, queries, key_square, kv, held, sems
):
    pages, _, page_len, width = cache.shape
    nodes = cosine.shape[0]
    groups = sems.shape[0]
    group_width = width // groups

    def fetch(group):
        columns = pl.ds(group * group_width, group_width)
        return pltpu.make_async_copy(
            cache.at[:, :, :, columns], kv.at[:, :, :, columns], sems.at[group]
        )

    for group in range(groups):
        fetch(group).start()
    squares = jnp.zeros((nodes, LANES), jnp.float32)
    extra = jnp.zeros((8, LANES), jnp.float32)
    for source in range(2 * HEADS):
        chunk = gathered[source].astype(jnp.float32)
        squares = squares + chunk[:nodes] * chunk[:nodes]
        extra = extra + chunk[nodes : nodes + 8]
    inverse = packed_inverse(squares, width)
    key_square[...] = extra
    token = lax.broadcasted_iota(jnp.int32, (nodes, page_len), 1)
    bias = [jnp.where(token < counts[page], 0.0, masked_score) for page in range(pages)]
    second = [jnp.full((nodes, LANES), owners[page], jnp.int32) == 1 for page in range(pages)]
    scale = HEAD_DIM ** (-0.5)
    cos_rows = cosine[...]
    sin_rows = sine[...]
    lane = lax.broadcasted_iota(jnp.int32, (nodes, LANES), 1)
    stats = jnp.zeros((nodes, LANES), jnp.float32)
    for head in range(HEADS):
        if head % (HEADS // groups) == 0:
            fetch(head // (HEADS // groups)).wait()
        base = head * HEAD_DIM
        front = gathered[2 * head][:nodes].astype(jnp.float32) * inverse * gains[2 * head : 2 * head + 1]
        back = gathered[2 * head + 1][:nodes].astype(jnp.float32) * inverse * gains[2 * head + 1 : 2 * head + 2]
        front, back = rotated(front, back, cos_rows, sin_rows)
        mine = paired(front, back)
        both = jnp.concatenate(mine, axis=0).astype(jnp.bfloat16)
        queries[head] = both
        scores = []
        for page in range(pages):
            asked = jnp.where(second[page], mine[1], mine[0]).astype(jnp.bfloat16)
            keys = kv[page, 0, :, base : base + HEAD_DIM]
            score = lax.dot_general(
                asked, keys, (((1,), (1,)), ((), ())), preferred_element_type=jnp.float32
            )
            scores.append(score * scale + bias[page])
        low = jnp.full((nodes, LANES), masked_score, jnp.float32)
        tops = []
        for request in range(2):
            best = functools.reduce(
                jnp.maximum,
                [
                    jnp.where(second[page] == (request == 1), scores[page], low)
                    for page in range(pages)
                ],
            )
            tops.append(jnp.max(best, axis=1, keepdims=True))
        zero = jnp.zeros((nodes, LANES), jnp.float32)
        sums = [zero, zero]
        mixed = [zero, zero]
        for page in range(pages):
            weight = jnp.exp(scores[page] - jnp.where(second[page], tops[1], tops[0]))
            values = kv[page, 1, :, base : base + HEAD_DIM]
            share = jnp.dot(
                weight.astype(jnp.bfloat16), values, preferred_element_type=jnp.float32
            )
            for request in range(2):
                mine_too = second[page] == (request == 1)
                sums[request] = sums[request] + jnp.where(mine_too, weight, zero)
                mixed[request] = mixed[request] + jnp.where(mine_too, share, zero)
        found = [*tops, *[jnp.sum(part, axis=1, keepdims=True) for part in sums]]
        for place, column in enumerate(found):
            stats = jnp.where(lane == place * HEADS + head, column, stats)
        left, right = paired(mixed[0], mixed[1])
        held[2 * head] = left
        held[2 * head + 1] = right
    turned = columns_to_rows(stats)
    first = in_first(HEADS)

    def by_request(place):
        left = turned[place * HEADS : (place + 1) * HEADS]
        right = turned[(place + 1) * HEADS : (place + 2) * HEADS]
        return jnp.where(first, left, pltpu.roll(right, HALF, 1))

    rows = [*split_three(by_request(0)), *split_three(by_request(2))]
    rows += [jnp.zeros_like(rows[0])] * 2
    for head in range(HEADS):
        tail = jnp.concatenate([row[head : head + 1] for row in rows], axis=0)
        for half in range(2):
            block = jnp.concatenate([held[2 * head + half], tail], axis=0)
            out[2 * head + half] = block.astype(jnp.bfloat16)


def tree_kernel(
    place,
    accepted,
    queries,
    own_key,
    other_key,
    own_value,
    key_square,
    gains,
    cosine,
    sine,
    ancestry,
    depth,
    path_out,
    mixed_out,
    stats_out,
):
    width = 2 * HEADS * HALF
    requests, nodes, _ = ancestry.shape
    head = place[0] // 2
    even = jnp.full((nodes, LANES), place[0] % 2, jnp.int32) == 0
    first = in_first(nodes)
    sums = key_square[0:1] + key_square[1:2]
    square = jnp.broadcast_to(sums, (LANES, LANES)).T
    square = jnp.where(first, square[:nodes], square[nodes : 2 * nodes])
    inverse = lax.rsqrt(square / width + norm_epsilon)
    own = own_key[...].astype(jnp.float32)
    other = other_key[...].astype(jnp.float32)
    front = jnp.where(even, own, other) * inverse * gains[pl.ds(2 * head, 1)]
    back = jnp.where(even, other, own) * inverse * gains[pl.ds(2 * head + 1, 1)]
    front, back = rotated(front, back, cosine[...], sine[...])
    kept = jnp.where(even, front, back).astype(jnp.bfloat16)
    keys = paired(front, back)
    value = own_value[...]
    query = queries[head]
    lane = lax.broadcasted_iota(jnp.int32, (nodes, LANES), 1)
    stats = jnp.zeros((nodes, LANES), jnp.float32)
    mixed = []
    pickers = []
    for request in range(requests):
        line = ancestry[request]
        scores = lax.dot_general(
            query[request * nodes : (request + 1) * nodes],
            keys[request].astype(jnp.bfloat16),
            (((1,), (1,)), ((), ())),
            preferred_element_type=jnp.float32,
        ) * (HEAD_DIM ** (-0.5))
        visible = line > 0.5
        scores = jnp.where(visible, scores, masked_score)
        top = jnp.max(scores, axis=1, keepdims=True)
        weights = jnp.where(visible, jnp.exp(scores - top), 0.0)
        total = jnp.sum(weights, axis=1, keepdims=True)
        mixed.append(jnp.dot(weights.astype(jnp.bfloat16), value, preferred_element_type=jnp.float32))
        stats = jnp.where(lane == request, top, stats)
        stats = jnp.where(lane == request + 2, total, stats)
        on_path = ancestry[request, pl.ds(accepted[request], 1), :]
        levels = depth[pl.ds(request, 1), :]
        wanted = (lax.broadcasted_iota(jnp.int32, (8, nodes), 0) + 1).astype(jnp.float32)
        picker = jnp.where(wanted == levels, on_path, 0.0).astype(jnp.bfloat16)
        pickers.append(picker)
    mixed_out[...] = jnp.where(first, mixed[0], mixed[1])
    turned = columns_to_rows(stats)
    row = in_first(1)
    stats_out[0:1] = jnp.where(row, turned[0:1], pltpu.roll(turned[1:2], HALF, 1))
    stats_out[1:2] = jnp.where(row, turned[2:3], pltpu.roll(turned[3:4], HALF, 1))
    for kind, block in enumerate((kept, value)):
        picked = [
            jnp.dot(picker, block, preferred_element_type=jnp.float32) for picker in pickers
        ]
        path_out[kind] = jnp.where(in_first(8), picked[0], picked[1])


def merge_kernel(parts, tree_mixed, tree_stats, drafted, out):
    count = parts.shape[0]
    nodes = tree_mixed.shape[0]
    top_tree = tree_stats[0:1]
    tops = []
    totals = []
    for source in range(count):
        tail = parts[source].astype(jnp.float32)[nodes : nodes + 8]
        tops.append((tail[0:1] + tail[1:2]) + tail[2:3])
        totals.append((tail[3:4] + tail[4:5]) + tail[5:6])
    tops = jnp.concatenate(tops, axis=0)
    totals = jnp.concatenate(totals, axis=0)
    top = jnp.maximum(jnp.max(tops, axis=0, keepdims=True), top_tree)
    factors = jnp.exp(tops - top)
    factor_tree = jnp.exp(top_tree - top)
    total = jnp.sum(factors * totals, axis=0, keepdims=True) + factor_tree * tree_stats[1:2]
    shares = jnp.concatenate([factors / total, factor_tree / total], axis=0)
    turned = columns_to_rows(shares)
    first = in_first(nodes)

    def spread(source):
        return jnp.where(
            first,
            turned[0:nodes, source : source + 1],
            turned[HALF : HALF + nodes, source : source + 1],
        )

    mixed = spread(count) * tree_mixed[...]
    for source in range(count):
        mixed = mixed + spread(source) * parts[source].astype(jnp.float32)[:nodes]
    result = jnp.concatenate([mixed, drafted[...].astype(jnp.float32)], axis=0).astype(jnp.bfloat16)
    for target in range(count):
        out[target] = result


def out_kernel(gathered, weight, drafted, out):
    count = gathered.shape[0]
    nodes = gathered.shape[1] - drafted.shape[0]
    total = jnp.zeros((2 * nodes, LANES), jnp.float32)
    for head in range(count // 2):
        both = paired(
            gathered[2 * head][:nodes].astype(jnp.float32),
            gathered[2 * head + 1][:nodes].astype(jnp.float32),
        )
        block = jnp.concatenate(both, axis=0).astype(jnp.bfloat16)
        total = total + lax.dot_general(
            block,
            weight[:, head * HEAD_DIM : (head + 1) * HEAD_DIM],
            (((1,), (1,)), ((), ())),
            preferred_element_type=jnp.float32,
        )
    packed = jnp.where(in_first(nodes), total[:nodes], total[nodes:])
    result = jnp.concatenate([packed, drafted[...].astype(jnp.float32)], axis=0).astype(jnp.bfloat16)
    for target in range(count):
        out[target] = result


def residual_kernel(gathered, gain, inputs, out):
    count = gathered.shape[0]
    nodes = inputs.shape[0] // 2
    squares = jnp.zeros((nodes, LANES), jnp.float32)
    for source in range(count):
        chunk = gathered[source].astype(jnp.float32)[:nodes]
        squares = squares + chunk * chunk
    inverse = packed_inverse(squares, count * HALF)
    for head in range(count // 2):
        both = paired(
            gathered[2 * head].astype(jnp.float32)[:nodes] * inverse,
            gathered[2 * head + 1].astype(jnp.float32)[:nodes] * inverse,
        )
        columns = slice(head * HEAD_DIM, (head + 1) * HEAD_DIM)
        block = jnp.concatenate(both, axis=0) * gain[:, columns]
        out[:, columns] = (inputs[:, columns].astype(jnp.float32) + block).astype(jnp.bfloat16)


def rotated(front, back, cosine, sine):
    return front * cosine - back * sine, back * cosine + front * sine


def vmem(count):
    return [pl.BlockSpec(memory_space=pltpu.VMEM)] * count


SMEM = pl.BlockSpec(memory_space=pltpu.SMEM)


def broadcast_gather(chunk, count):
    copies = jnp.broadcast_to(chunk[None], (count,) + chunk.shape)
    return lax.all_to_all(copies, "mp", 0, 0)


def per_device(
    draft_hidden,
    draft_weight,
    vocab_weight,
    tree_inputs,
    tree_parent,
    cache_len,
    page_table,
    kv_cache,
    accepted_node,
    qkv_weight,
    norm_gains,
    out_weight,
    gate_up_weight,
    down_weight,
):
    mp_count = lax.axis_size("mp")
    req_count = lax.axis_size("req")
    mp_place = lax.axis_index("mp")
    req_place = lax.axis_index("req")
    req_local, model_width = draft_hidden.shape
    draft_count = draft_weight.shape[0]
    slab = draft_weight.shape[2]
    vocab_local = vocab_weight.shape[0]
    rows = tree_inputs.shape[0]
    tree_size = tree_parent.shape[1]
    page_count, _, page_len, _ = kv_cache.shape
    table_width = page_table.shape[1]
    bf16 = jnp.bfloat16
    f32 = jnp.float32

    own = jnp.einsum(
        "rtd,dce->ctre",
        tree_inputs.reshape(req_local, tree_size, model_width),
        qkv_weight,
        preferred_element_type=f32,
    )
    own = own.astype(bf16).reshape(3, tree_size, LANES)
    key_part = own[1].astype(f32).reshape(tree_size, req_local, slab)
    square = jnp.sum(key_part * key_part, axis=2).T.reshape(1, rows)
    square_top = lax.reduce_precision(square, 8, 7)
    square_rest = lax.reduce_precision(square - square_top, 8, 7)
    extra = jnp.concatenate([square_top, square_rest], axis=0).astype(bf16)
    extra = jnp.pad(extra, ((0, 6), (0, LANES - rows)))
    gathered = broadcast_gather(jnp.concatenate([own[0], extra], axis=0), mp_count)
    other_key = lax.ppermute(own[1], "mp", [(i, i ^ 1) for i in range(mp_count)])

    pair = lax.ppermute(draft_hidden, "req", [(i, i ^ 1) for i in range(req_count)])
    both = jnp.concatenate([draft_hidden, pair], axis=0)
    turns = req_count // 2
    hidden_parts = [both] + [
        lax.ppermute(both, "req", [(i, (i + 2 * k) % req_count) for i in range(req_count)])
        for k in range(1, turns)
    ]
    hidden_all = jnp.concatenate(hidden_parts, axis=0)
    spot = jnp.arange(req_count * req_local, dtype=jnp.int32)
    turn = spot // (2 * req_local)
    side = (spot // req_local) % 2
    holder = 2 * ((req_place // 2 - turn) % turns) + ((req_place % 2) ^ side)
    origin = holder * req_local + spot % req_local
    order = (origin[None, :] == spot[:, None]).astype(bf16)
    hidden_all = jnp.dot(order, hidden_all, preferred_element_type=f32).astype(bf16)
    draft_raw = jnp.einsum("rd,kde->rke", hidden_all, draft_weight, preferred_element_type=f32)
    own_columns = lax.dynamic_slice_in_dim(hidden_all, mp_place * slab, slab, 1).astype(f32)
    drafted = (own_columns[:, None, :] + jax.nn.silu(draft_raw)).astype(bf16)
    half_count = req_count * req_local * draft_count // 2
    drafted = drafted.reshape(2, half_count, slab)
    drafted = jnp.concatenate([drafted[0], drafted[1]], axis=1)

    ancestry, node_depth = tree_shape(tree_parent)
    positions = cache_len[:, None].astype(f32) + node_depth - 1.0
    freqs = rope_base ** (-jnp.arange(HALF, dtype=f32) * 2.0 / HEAD_DIM)
    angles = positions.T[:, :, None] * freqs[None, None, :]
    angles = angles.reshape(tree_size, LANES)
    cosine = jnp.cos(angles)
    sine = jnp.sin(angles)
    gain_rows = norm_gains.astype(f32)
    twice = gain_rows[:2].reshape(2, mp_count, slab)
    twice = jnp.concatenate([twice, twice], axis=2)

    slots = (req_place * mp_count + mp_place) * page_count + jnp.arange(page_count, dtype=jnp.int32)
    matches = page_table[None, :, :] == slots[:, None, None]
    starts = jnp.arange(table_width, dtype=jnp.int32) * page_len
    left = jnp.clip(cache_len[:, None] - starts[None, :], 0, page_len)
    counts = jnp.sum(jnp.where(matches, left[None], 0), axis=(1, 2))
    owners = jnp.any(matches[:, 1], axis=1).astype(jnp.int32)

    groups = 4
    parts, queries, key_square = pl.pallas_call(
        pages_kernel,
        out_shape=(
            jax.ShapeDtypeStruct((mp_count, tree_size + 8, LANES), bf16),
            jax.ShapeDtypeStruct((HEADS, rows, HEAD_DIM), bf16),
            jax.ShapeDtypeStruct((8, LANES), f32),
        ),
        in_specs=[SMEM, SMEM, *vmem(4), pl.BlockSpec(memory_space=pltpu.HBM)],
        out_specs=tuple(vmem(3)),
        scratch_shapes=[
            pltpu.VMEM(kv_cache.shape, bf16),
            pltpu.VMEM((mp_count, tree_size, LANES), f32),
            pltpu.SemaphoreType.DMA((groups,)),
        ],
        compiler_params=pltpu.CompilerParams(vmem_limit_bytes=16 * 2**20),
        cost_estimate=pl.CostEstimate(
            flops=4 * page_count * page_len * LANES * model_width,
            bytes_accessed=kv_cache.size * 2,
            transcendentals=page_count * page_len * tree_size * HEADS,
        ),
        name="pages",
    )(counts, owners, gathered, twice[0], cosine, sine, kv_cache)
    arrived = lax.all_to_all(parts, "mp", 0, 0)

    path, tree_mixed, tree_stats = pl.pallas_call(
        tree_kernel,
        out_shape=(
            jax.ShapeDtypeStruct((2, 8, LANES), f32),
            jax.ShapeDtypeStruct((tree_size, LANES), f32),
            jax.ShapeDtypeStruct((2, LANES), f32),
        ),
        in_specs=[SMEM, SMEM, *vmem(10)],
        out_specs=tuple(vmem(3)),
        compiler_params=pltpu.CompilerParams(vmem_limit_bytes=8 * 2**20),
        cost_estimate=pl.CostEstimate(flops=2**24, bytes_accessed=2**20, transcendentals=2**13),
        name="tree",
    )(
        mp_place.reshape(1),
        accepted_node,
        queries,
        own[1],
        other_key,
        own[2],
        key_square,
        twice[1],
        cosine,
        sine,
        ancestry,
        node_depth,
    )
    accepted_kv = jnp.transpose(
        path[:, :draft_count].reshape(2, draft_count, req_local, slab), (2, 1, 0, 3)
    ).astype(bf16)

    ride = half_count // 2
    first_ride, second_ride = drafted[:ride], drafted[ride:]
    out_twice = jnp.concatenate([out_weight.T, out_weight.T], axis=0)
    attended_copies = pl.pallas_call(
        merge_kernel,
        out_shape=jax.ShapeDtypeStruct((mp_count, tree_size + ride, LANES), bf16),
        in_specs=vmem(4),
        out_specs=vmem(1)[0],
        compiler_params=pltpu.CompilerParams(vmem_limit_bytes=8 * 2**20),
        name="merge",
    )(arrived, tree_mixed, tree_stats, first_ride)
    attended_copies, out_twice, second_ride, accepted_kv = lax.optimization_barrier(
        (attended_copies, out_twice, second_ride, accepted_kv)
    )
    attended = lax.all_to_all(attended_copies, "mp", 0, 0)
    out_copies = pl.pallas_call(
        out_kernel,
        out_shape=jax.ShapeDtypeStruct((mp_count, tree_size + ride, LANES), bf16),
        in_specs=vmem(3),
        out_specs=vmem(1)[0],
        compiler_params=pltpu.CompilerParams(vmem_limit_bytes=8 * 2**20),
        name="out_columns",
    )(attended, out_twice, second_ride)
    projected_out = lax.all_to_all(out_copies, "mp", 0, 0)
    residual = pl.pallas_call(
        residual_kernel,
        out_shape=jax.ShapeDtypeStruct((rows, model_width), bf16),
        in_specs=vmem(3),
        out_specs=vmem(1)[0],
        compiler_params=pltpu.CompilerParams(vmem_limit_bytes=8 * 2**20),
        name="residual",
    )(projected_out, gain_rows[2:3], tree_inputs)
    gate_up = jnp.einsum("td,dce->tce", residual, gate_up_weight, preferred_element_type=f32)
    hidden = (jax.nn.silu(gate_up[:, 0]) * gate_up[:, 1]).astype(bf16)
    row_share = rows // mp_count
    partial = jnp.dot(hidden, down_weight, preferred_element_type=f32).astype(bf16)
    shares = lax.all_to_all(partial.reshape(mp_count, row_share, model_width), "mp", 0, 0)

    riders = jnp.concatenate([attended[:, tree_size:], projected_out[:, tree_size:]], axis=1)
    riders = jnp.transpose(riders.reshape(mp_count, half_count, 2, slab), (2, 1, 0, 3))
    draft_logits = lax.dot_general(
        riders.reshape(2 * half_count, model_width),
        vocab_weight,
        (((1,), (1,)), ((), ())),
        preferred_element_type=f32,
    ).reshape(req_count * req_local, draft_count, vocab_local)
    residual_rows = lax.dynamic_slice_in_dim(residual, mp_place * row_share, row_share, 0)
    own_rows = jnp.sum(shares.astype(f32), axis=0)
    row_square = jnp.mean(own_rows * own_rows, axis=-1, keepdims=True)
    layer_out = (
        residual_rows.astype(f32)
        + own_rows * lax.rsqrt(row_square + norm_epsilon) * gain_rows[3]
    ).astype(bf16)
    return (draft_logits, layer_out, accepted_kv)


def solution(mesh):
    placed = (
        P("req", None),
        P(None, None, "mp"),
        P(("req", "mp"), None),
        P("req", None),
        P("req", None),
        P("req"),
        P("req", None),
        P(("req", "mp"), None, None, None),
        P("req"),
        P(None, None, "mp"),
        P(),
        P(None, "mp"),
        P(None, None, "mp"),
        P("mp", None),
    )
    return jax.shard_map(
        per_device,
        mesh=mesh,
        in_specs=placed,
        out_specs=(
            P(None, None, ("req", "mp")),
            P(("req", "mp"), None),
            P("req", None, None, "mp"),
        ),
        check_vma=False,
    )
```

time: 142 us -> 144 us (1.014)
  blocking collectives: 0 us -> 21.2 us
  waiting for transfers between devices: 54.6 us -> 39.4 us
  starting transfers between devices: 37.8 us -> 32.7 us
  other arithmetic: 7.07 us -> 5.25 us
  Pallas kernels: 10.2 us -> 12 us
    all_to_all x2 -> x1, waiting for transfers between devices: 25 us -> 2.94 us  [broadcast_gather(): return lax.all_to_all(copies, 'mp', 0, 0)]
    all_to_all x0 -> x1, blocking collectives: none -> 21.2 us  [per_device(): attended = lax.all_to_all(attended_copies, 'mp', 0, 0)]
    unnamed x48 -> x53, local copies, waits for them, and re-layouts: 5.59 us -> 13 us
    all_to_all x2 -> x1, starting transfers between devices: 16.3 us -> 11.2 us  [broadcast_gather(): return lax.all_to_all(copies, 'mp', 0, 0)]
    pad x5 -> x0, local copies, waits for them, and re-layouts: 3.24 us -> none  [the longest x3 2.55 us: per_device(): wide = lambda a: jnp.pad(a, ((0, 0), (0, LANES - rows)))]
    all_to_all x1, waiting for transfers between devices: 3.35 us -> 5.75 us  [per_device(): arrived = lax.all_to_all(parts, 'mp', 0, 0)]
    all_to_all x1, waiting for transfers between devices: 10.3 us -> 12.6 us  [per_device(): lax.all_to_all(partial.reshape(mp_count, row_share, model_width), 'mp', 0...]
    broadcast_in_dim x3 -> x0, local copies, waits for them, and re-layouts: 2.27 us -> none  [the longest x2 1.93 us: per_device(): key_gain = jnp.broadcast_to(key_gain[:, None], (HEAD_DIM, LANES))]
  transfers between devices with their start and end apart: 10 -> 9, of which waited for: 5 -> 5; matrix products, arithmetic and copies ran while one was open for 17% -> 10% of each run, Pallas kernels for 6% -> 7%
where the time goes in v2:
time: 144 us; the launch traced here: 142 us
  waiting for transfers between devices  39.4 us (27%)
  starting transfers between devices  32.7 us (23%)
  blocking collectives  21.2 us (15%)
  local copies, waits for them, and re-layouts  21 us (15%)
  Pallas kernels  12 us (8%)
  matrix products  9.22 us (6%)
  other arithmetic  5.25 us (4%)
    all_to_all x1, blocking collectives, per_device(): attended = lax.all_to_all(attended_copies, 'mp', 0, 0)  21.2 us
    all_to_all x1, waiting for transfers between devices, per_device(): projected_out = lax.all_to_all(out_copies, 'mp', 0, 0)  16.3 us
    unnamed x53, local copies, waits for them, and re-layouts  13 us
    all_to_all x1, waiting for transfers between devices, per_device(): lax.all_to_all(partial.reshape(mp_count, row_share, model_width), 'mp', 0...  12.6 us
    all_to_all x1, starting transfers between devices, broadcast_gather(): return lax.all_to_all(copies, 'mp', 0, 0)  11.2 us
    pallas_call x1, Pallas kernels, per_device(): pl.pallas_call(pages_kernel, out_shape=(jax.ShapeDtypeStruct((mp_count, t...  8.78 us
    all_to_all x1, starting transfers between devices, per_device(): arrived = lax.all_to_all(parts, 'mp', 0, 0)  6.68 us
    all_to_all x1, waiting for transfers between devices, per_device(): arrived = lax.all_to_all(parts, 'mp', 0, 0)  5.75 us
  transfers between devices with their start and end apart: 9, of which 5 were waited for; matrix products, arithmetic and copies ran while one was open for 10% of the time, Pallas kernels for 7%

profile of v2, /device:TPU:48, one launch (start us, length us, event | category | flops | bytes accessed | tf_op | source)
XLA Modules:
  0.0 141.8 jit_solution(3143932980845558054)
XLA Ops:
  0.7 1.9 %fusion.4 = bf16[3,48,2,64]{3,1,2,0:T(8,128)(2,1)S(1)} fusion(bf16[2,48,2048,1]{2,1,0,3:T(8,128)(2,1)} %bitcast.58, bf16[2048,3,64]{0,2,1:T(8,128)(2,1)} %param.23), kind=kOutput, calls=%fused_computation.7 | convolution fusion | flops 75515904 | bytes 1216512 | tf_op jit(solution)/shard_map/rtd,dce->ctre/dot_general | solution.py:630
  3.7 11.2 %all-to-all-start = ((bf16[32,56,128]{2,1,0:T(8,128)(2,1)}), bf16[32,56,128]{2,1,0:T(8,128)(2,1)S(1)}, u32[]{:S(2)}, u32[]{:S(2)}) async-start(bf16[32,56,128]{2,1,0:T(8,128)(2,1)} %broadcast_in_dim.12), calls=%async_computation | async-start | bytes 917504 | tf_op jit(solution)/shard_map/all_to_all | solution.py:596
  15.7 1.5 %collective-permute-start = (bf16[48,128]{1,0:T(8,128)(2,1)}, bf16[48,128]{1,0:T(8,128)(2,1)}, u32[]{:S(2)}, u32[]{:S(2)}) collective-permute-start(bf16[48,128]{1,0:T(8,128)(2,1)} %squeeze.32.own_key), channel_id=1, source_target_pairs={{0,1},{1,0},{2,3},{3,2},{4,5},{5,4},{6,7},{7,6},{8,9},{9,8},{10,11... | collective-permute-start | bytes 36872 | tf_op jit(solution)/shard_map/ppermute | solution.py:644
  20.0 1.4 collective-permute-start.2
  22.0 1.1 collective-permute-start.4
  24.8 1.8 %collective-permute-done.3 = bf16[4,2048]{1,0:T(4,128)(2,1)S(1)} collective-permute-done((bf16[4,2048]{1,0:T(4,128)(2,1)S(1)}, bf16[4,2048]{1,0:T(4,128)(2,1)S(1)}, u32[]{:S(2)}, u32[]{:S(2)}) %collective-permute-start.3) | collective-permute-done | bytes 16416 | tf_op jit(solution)/shard_map/ppermute | solution.py:650
  26.6 1.3 concatenate.30
  27.9 2.9 %all-to-all-done.gathered = bf16[32,56,128]{2,1,0:T(8,128)(2,1)S(1)} async-done(((bf16[32,56,128]{2,1,0:T(8,128)(2,1)}), bf16[32,56,128]{2,1,0:T(8,128)(2,1)S(1)}, u32[]{:S(2)}, u32[]{:S(2)}) %all-to-all-start) | async-done | bytes 458784 | tf_op jit(solution)/shard_map/all_to_all | solution.py:596
  30.9 2.2 %copy-done.1 = bf16[4,2,128,2048]{3,2,1,0:T(8,128)(2,1)S(1)} copy-done((bf16[4,2,128,2048]{3,2,1,0:T(8,128)(2,1)S(1)}, bf16[4,2,128,2048]{3,2,1,0:T(8,128)(2,1)}, u32[]{:S(2)}) %copy-start.1) | copy-done | bytes 4194328
  34.3 8.8 %pages.1 = (bf16[32,56,128]{2,1,0:T(8,128)(2,1)}, bf16[16,96,128]{2,1,0:T(8,128)(2,1)S(1)}, f32[8,128]{1,0:T(8,128)S(1)}) custom-call(s32[4]{0:T(128)S(1)} %copy-done.13, s32[4]{0:T(128)S(1)} %copy-done.16, bf16[32,56,128]{2,1,0:T(8,128)(2,1)S(1)} %all-to-all-done.gathered, f32[32,128]{1,0:T(8,128)S(1)} %get-tuple-element.38.gains, ...), custom_call_target="tpu_custom_call" | custom-call | flops 536870912 | bytes 4194304 | tf_op jit(solution)/shard_map/pages/pallas_call | solution.py:687
  43.7 6.7 %all-to-all-start.1 = ((bf16[32,56,128]{2,1,0:T(8,128)(2,1)}), bf16[32,56,128]{2,1,0:T(8,128)(2,1)S(1)}, u32[]{:S(2)}, u32[]{:S(2)}) async-start(bf16[32,56,128]{2,1,0:T(8,128)(2,1)} %get-tuple-element.13), calls=%async_computation.1 | async-start | bytes 917504 | tf_op jit(solution)/shard_map/all_to_all | solution.py:709
  51.5 1.8 %add_convert_fusion.1 = bf16[16,4,64]{2,0,1:T(8,128)(2,1)S(1)} fusion(f32[16,64]{1,0:T(8,128)S(1)} %dynamic-slice_convert_fusion, bf16[4,2048,64]{1,2,0:T(8,128)(2,1)} %param.15, bf16[16,2048]{1,0:T(8,128)(2,1)S(1)} %convolution_convert_fusion.1), kind=kOutput, calls=%fused_computation.30 | convolution fusion | flops 16801792 | bytes 1126400 | tf_op jit(solution)/shard_map/rd,kde->rke/dot_general | solution.py:661
  56.7 1.5 %tree.1 = (f32[2,8,128]{2,1,0:T(8,128)S(1)}, f32[48,128]{1,0:T(8,128)S(1)}, f32[2,128]{1,0:T(2,128)S(1)}) custom-call(s32[1]{0:T(128)} %bitcast.8.place, s32[2]{0:T(128)S(1)} %copy-done.17, bf16[16,96,128]{2,1,0:T(8,128)(2,1)S(1)} %get-tuple-element.14.queries, bf16[48,128]{1,0:T(8,128)(2,1)} %squeeze.32.own_key, ...), custom_call_target="tpu_custom_call" | custom-call | flops 16777216 | bytes 1048576 | tf_op jit(solution)/shard_map/tree/pallas_call | solution.py:711
  60.1 5.7 %all-to-all-done.1.parts = bf16[32,56,128]{2,1,0:T(8,128)(2,1)S(1)} async-done(((bf16[32,56,128]{2,1,0:T(8,128)(2,1)}), bf16[32,56,128]{2,1,0:T(8,128)(2,1)S(1)}, u32[]{:S(2)}, u32[]{:S(2)}) %all-to-all-start.1) | async-done | bytes 458784 | tf_op jit(solution)/shard_map/all_to_all | solution.py:709
  68.8 21.2 %all_to_all.25.gathered = bf16[32,64,128]{2,1,0:T(8,128)(2,1)S(1)} all-to-all(bf16[32,64,128]{2,1,0:T(8,128)(2,1)S(1)} %merge.1), channel_id=1, replica_groups=mesh['req'=8,'mp'=32] {'mp'}, dimensions={0} | all-to-all | bytes 1048576 | tf_op jit(solution)/shard_map/all_to_all | solution.py:755
  91.4 5.1 %all-to-all-start.3 = ((bf16[32,64,128]{2,1,0:T(8,128)(2,1)}), bf16[32,64,128]{2,1,0:T(8,128)(2,1)S(1)}, u32[]{:S(2)}, u32[]{:S(2)}) async-start(bf16[32,64,128]{2,1,0:T(8,128)(2,1)} %copy-done.2), calls=%async_computation.3 | async-start | bytes 1048576 | tf_op jit(solution)/shard_map/all_to_all | solution.py:764
  96.5 16.3 %all-to-all-done.3.gathered = bf16[32,64,128]{2,1,0:T(8,128)(2,1)S(1)} async-done(((bf16[32,64,128]{2,1,0:T(8,128)(2,1)}), bf16[32,64,128]{2,1,0:T(8,128)(2,1)S(1)}, u32[]{:S(2)}, u32[]{:S(2)}) %all-to-all-start.3) | async-done | bytes 524320 | tf_op jit(solution)/shard_map/all_to_all | solution.py:764
  112.8 1.0 copy-done.3
  115.0 1.1 convolution_convert_fusion
  116.1 2.1 %reshape.206 = bf16[32,3,2048]{2,1,0:T(4,128)(2,1)} reshape(bf16[96,2048]{1,0:T(8,128)(2,1)} %convolution_convert_fusion) | data formatting | bytes 786432 | tf_op jit(solution)/shard_map/reshape | solution.py:777
  118.2 5.2 %all-to-all-start.4 = ((bf16[32,3,2048]{2,1,0:T(4,128)(2,1)}), bf16[32,3,2048]{2,1,0:T(4,128)(2,1)}, u32[]{:S(2)}, u32[]{:S(2)}) async-start(bf16[32,3,2048]{2,1,0:T(4,128)(2,1)} %reshape.206), calls=%async_computation.4 | async-start | bytes 1048576 | tf_op jit(solution)/shard_map/all_to_all | solution.py:777
  124.4 2.0 %fusion.2 = f32[16,4,384]{2,0,1:T(8,128)S(1)} fusion(bf16[384,2048]{1,0:T(8,128)(2,1)} %param.16, bf16[16,4,2048]{2,1,0:T(4,128)(2,1)S(1)} %dot_general.31), kind=kOutput, calls=%fused_computation.4 | convolution fusion | flops 100663296 | bytes 1933312 | tf_op jit(solution)/shard_map/dot_general | solution.py:781
  127.1 12.6 %all-to-all-done.4 = bf16[32,3,2048]{2,1,0:T(4,128)(2,1)} async-done(((bf16[32,3,2048]{2,1,0:T(4,128)(2,1)}), bf16[32,3,2048]{2,1,0:T(4,128)(2,1)}, u32[]{:S(2)}, u32[]{:S(2)}) %all-to-all-start.4) | async-done | bytes 393248 | tf_op jit(solution)/shard_map/all_to_all | solution.py:777
  139.7 1.3 convert_reduce_fusion
  (117 shorter events, 23.3 us)
Async XLA Ops:
  0.6 113.6 %copy-start = (bf16[2048,2,256]{2,1,0:T(2,128)(2,1)S(1)}, bf16[2048,2,256]{2,1,0:T(2,128)(2,1)}, u32[]{:S(2)}) copy-start(bf16[2048,2,256]{2,1,0:T(2,128)(2,1)} %param.26) | copy-start | bytes 6291460
  0.6 16.5 %copy-start.22 = (bf16[2,2048]{1,0:T(2,128)(2,1)S(1)}, bf16[2,2048]{1,0:T(2,128)(2,1)}, u32[]{:S(2)}) copy-start(bf16[2,2048]{1,0:T(2,128)(2,1)} %param.14) | copy-start | bytes 24580
  0.7 16.5 %copy-start.25 = (s32[2]{0:T(128)S(1)}, s32[2]{0:T(128)}, u32[]{:S(2)}) copy-start(s32[2]{0:T(128)} %param.19) | copy-start | bytes 28
  0.7 16.6 %copy-start.20 = (bf16[4,2048]{1,0:T(4,128)(2,1)S(1)}, bf16[4,2048]{1,0:T(4,128)(2,1)}, u32[]{:S(2)}) copy-start(bf16[4,2048]{1,0:T(4,128)(2,1)} %param.24) | copy-start | bytes 49156
  0.7 16.8 %copy-start.23 = (s32[2,48]{1,0:T(2,128)S(1)}, s32[2,48]{1,0:T(2,128)}, u32[]{:S(2)}) copy-start(s32[2,48]{1,0:T(2,128)} %param.18) | copy-start | bytes 1156
  0.7 18.4 %copy-start.24 = (s32[2,64]{1,0:T(2,128)S(1)}, s32[2,64]{1,0:T(2,128)}, u32[]{:S(2)}) copy-start(s32[2,64]{1,0:T(2,128)} %param.20) | copy-start | bytes 1540
  0.7 19.1 %copy-start.19 = (bf16[2048,64]{0,1:T(8,128)(2,1)S(1)}, bf16[2048,64]{0,1:T(8,128)(2,1)}, u32[]{:S(2)}) copy-start(bf16[2048,64]{0,1:T(8,128)(2,1)} %param.25) | copy-start | bytes 786436
  3.7 27.2 %all-to-all-start = ((bf16[32,56,128]{2,1,0:T(8,128)(2,1)}), bf16[32,56,128]{2,1,0:T(8,128)(2,1)S(1)}, u32[]{:S(2)}, u32[]{:S(2)}) async-start(bf16[32,56,128]{2,1,0:T(8,128)(2,1)} %broadcast_in_dim.12), calls=%async_computation | async-start | bytes 917504 | tf_op jit(solution)/shard_map/all_to_all | solution.py:596
  15.7 38.3 %collective-permute-start = (bf16[48,128]{1,0:T(8,128)(2,1)}, bf16[48,128]{1,0:T(8,128)(2,1)}, u32[]{:S(2)}, u32[]{:S(2)}) collective-permute-start(bf16[48,128]{1,0:T(8,128)(2,1)} %squeeze.32.own_key), channel_id=1, source_target_pairs={{0,1},{1,0},{2,3},{3,2},{4,5},{5,4},{6,7},{7,6},{8,9},{9,8},{10,11... | collective-permute-start | bytes 36872 | tf_op jit(solution)/shard_map/ppermute | solution.py:644
  17.1 2.9 %collective-permute-start.1 = (bf16[2,2048]{1,0:T(2,128)(2,1)S(1)}, bf16[2,2048]{1,0:T(2,128)(2,1)S(1)}, u32[]{:S(2)}, u32[]{:S(2)}) collective-permute-start(bf16[2,2048]{1,0:T(2,128)(2,1)S(1)} %copy-done.22), channel_id=1, source_target_pairs={{0,32},{32,0},{64,96},{96,64},{128,160},{160,128},{192,224},{224,1... | collective-permute-start | bytes 24584 | tf_op jit(solution)/shard_map/ppermute | solution.py:646
  18.5 12.4 %copy-start.9 = (f32[2,48]{1,0:T(2,128)}, f32[2,48]{1,0:T(2,128)S(1)}, u32[]{:S(2)}) copy-start(f32[2,48]{1,0:T(2,128)S(1)} %get-tuple-element.49.depth) | copy-start | bytes 1156
  20.0 4.8 %collective-permute-start.2 = (bf16[4,2048]{1,0:T(4,128)(2,1)S(1)}, bf16[4,2048]{1,0:T(4,128)(2,1)S(1)}, u32[]{:S(2)}, u32[]{:S(2)}) collective-permute-start(bf16[4,2048]{1,0:T(4,128)(2,1)S(1)} %pad_maximum_fusion.3), channel_id=1, source_target_pairs={{0,64},{32,96},{64,128},{96,160},{128,192},{160,224},{192,0},{224,... | collective-permute-start | bytes 49160 | tf_op jit(solution)/shard_map/ppermute | solution.py:650
  21.4 5.2 %collective-permute-start.3 = (bf16[4,2048]{1,0:T(4,128)(2,1)S(1)}, bf16[4,2048]{1,0:T(4,128)(2,1)S(1)}, u32[]{:S(2)}, u32[]{:S(2)}) collective-permute-start(bf16[4,2048]{1,0:T(4,128)(2,1)S(1)} %pad_maximum_fusion.3), channel_id=1, source_target_pairs={{0,128},{32,160},{64,192},{96,224},{128,0},{160,32},{192,64},{224,... | collective-permute-start | bytes 49160 | tf_op jit(solution)/shard_map/ppermute | solution.py:650
  22.0 4.6 %collective-permute-start.4 = (bf16[4,2048]{1,0:T(4,128)(2,1)S(1)}, bf16[4,2048]{1,0:T(4,128)(2,1)S(1)}, u32[]{:S(2)}, u32[]{:S(2)}) collective-permute-start(bf16[4,2048]{1,0:T(4,128)(2,1)S(1)} %pad_maximum_fusion.3), channel_id=1, source_target_pairs={{0,192},{32,224},{64,0},{96,32},{128,64},{160,96},{192,128},{224,1... | collective-permute-start | bytes 49160 | tf_op jit(solution)/shard_map/ppermute | solution.py:650
  30.9 2.2 %copy-start.1 = (bf16[4,2,128,2048]{3,2,1,0:T(8,128)(2,1)S(1)}, bf16[4,2,128,2048]{3,2,1,0:T(8,128)(2,1)}, u32[]{:S(2)}) copy-start(bf16[4,2,128,2048]{3,2,1,0:T(8,128)(2,1)} %cache.1) | copy-start | bytes 12582916
  43.7 10.2 %copy-start.5 = (bf16[48,128]{1,0:T(8,128)(2,1)S(1)}, bf16[48,128]{1,0:T(8,128)(2,1)}, u32[]{:S(2)}) copy-start(bf16[48,128]{1,0:T(8,128)(2,1)} %squeeze.33.own_value) | copy-start | bytes 36868
  43.7 22.2 %all-to-all-start.1 = ((bf16[32,56,128]{2,1,0:T(8,128)(2,1)}), bf16[32,56,128]{2,1,0:T(8,128)(2,1)S(1)}, u32[]{:S(2)}, u32[]{:S(2)}) async-start(bf16[32,56,128]{2,1,0:T(8,128)(2,1)} %get-tuple-element.13), calls=%async_computation.1 | async-start | bytes 917504 | tf_op jit(solution)/shard_map/all_to_all | solution.py:709
  53.9 0.8 copy-start.4
  68.0 28.5 %copy-start.21 = (bf16[4,2048]{1,0:T(4,128)(2,1)S(1)}, bf16[4,2048]{1,0:T(4,128)(2,1)}, u32[]{:S(2)}) copy-start(bf16[4,2048]{1,0:T(4,128)(2,1)} %param.24) | copy-start | bytes 49156
  90.6 0.8 copy-start.2
  91.4 21.5 %all-to-all-start.3 = ((bf16[32,64,128]{2,1,0:T(8,128)(2,1)}), bf16[32,64,128]{2,1,0:T(8,128)(2,1)S(1)}, u32[]{:S(2)}, u32[]{:S(2)}) async-start(bf16[32,64,128]{2,1,0:T(8,128)(2,1)} %copy-done.2), calls=%async_computation.3 | async-start | bytes 1048576 | tf_op jit(solution)/shard_map/all_to_all | solution.py:764
  112.8 1.0 copy-start.3
  113.8 1.2 copy-start.18
  118.2 21.5 %all-to-all-start.4 = ((bf16[32,3,2048]{2,1,0:T(4,128)(2,1)}), bf16[32,3,2048]{2,1,0:T(4,128)(2,1)}, u32[]{:S(2)}, u32[]{:S(2)}) async-start(bf16[32,3,2048]{2,1,0:T(4,128)(2,1)} %reshape.206), calls=%async_computation.4 | async-start | bytes 1048576 | tf_op jit(solution)/shard_map/all_to_all | solution.py:777
  (11 other events, 7.1 us)

commit v3 on v1

v3 whole, which is shorter than its diff:
```python
import functools

import jax
import jax.numpy as jnp
from jax import lax
from jax.experimental import pallas as pl
from jax.experimental.pallas import tpu as pltpu
from jax.sharding import PartitionSpec as P

HEADS = 16
HEAD_DIM = 128
HALF = HEAD_DIM // 2
LANES = 128
SIDE = 4

rope_base = 500000.0
norm_epsilon = 1e-06
masked_score = -1e30


def tree_shape(parents):
    node_count = parents.shape[-1]
    step_one = (
        parents[..., :, None] == jnp.arange(node_count, dtype=jnp.int32)[None, None, :]
    ).astype(jnp.float32)
    step_two = jnp.einsum("rij,rjk->rik", step_one, step_one, precision=lax.Precision.HIGHEST)
    step_three = jnp.einsum("rij,rjk->rik", step_two, step_one, precision=lax.Precision.HIGHEST)
    ancestry = jnp.eye(node_count, dtype=jnp.float32)[None] + step_one + step_two + step_three
    return (ancestry, jnp.sum(ancestry, axis=-1))


def split_three(value):
    top = value.astype(jnp.bfloat16).astype(jnp.float32)
    rest = value - top
    middle = rest.astype(jnp.bfloat16).astype(jnp.float32)
    return top, middle, (rest - middle).astype(jnp.bfloat16).astype(jnp.float32)


def in_first(rows):
    return lax.broadcasted_iota(jnp.int32, (rows, LANES), 1) < HALF


def paired(left, right):
    first = in_first(left.shape[0])
    return (
        jnp.where(first, left, pltpu.roll(right, HALF, 1)),
        jnp.where(first, pltpu.roll(left, HALF, 1), right),
    )


def packed_inverse(squares, width):
    first = in_first(squares.shape[0])
    zero = jnp.zeros_like(squares)
    left = jnp.sum(jnp.where(first, squares, zero), axis=1, keepdims=True)
    right = jnp.sum(jnp.where(first, zero, squares), axis=1, keepdims=True)
    return lax.rsqrt(jnp.where(first, left, right) / width + norm_epsilon)


def spot_of(place):
    return place % SIDE * (2 * HEADS // SIDE) + place // SIDE


def columns_to_rows(columns):
    rest = LANES - columns.shape[0]
    return jnp.concatenate([columns, jnp.zeros((rest, LANES), jnp.float32)], axis=0).T


def project_kernel(inputs, weights, copies, own_key, own_value, rows, columns, sems):
    nodes = own_key.shape[0]
    fetches = [pltpu.make_async_copy(inputs, rows, sems.at[0])]
    for kind in range(3):
        fetches.append(pltpu.make_async_copy(weights.at[kind], columns.at[kind], sems.at[1 + kind]))
    for fetch in fetches:
        fetch.start()
    fetches[0].wait()
    first = in_first(nodes)

    def projected(kind):
        fetches[1 + kind].wait()
        weight = columns[kind]
        product = lax.dot_general(
            rows[...],
            jnp.concatenate([weight, weight], axis=0),
            (((1,), (1,)), ((), ())),
            preferred_element_type=jnp.float32,
        )
        return jnp.where(first, product[:nodes], product[nodes:]).astype(jnp.bfloat16)

    query = projected(0)
    key = projected(1)
    own_key[...] = key
    squares = key.astype(jnp.float32)
    squares = squares * squares
    zero = jnp.zeros_like(squares)
    lane = lax.broadcasted_iota(jnp.int32, (nodes, LANES), 1)
    left = jnp.sum(jnp.where(first, squares, zero), axis=1, keepdims=True)
    right = jnp.sum(jnp.where(first, zero, squares), axis=1, keepdims=True)
    turned = columns_to_rows(jnp.where(lane == 0, left, jnp.where(lane == 1, right, zero)))
    sums = jnp.where(in_first(1), turned[0:1], pltpu.roll(turned[1:2], HALF, 1))
    tail = jnp.concatenate([*split_three(sums), jnp.zeros((5, LANES), jnp.float32)], axis=0)
    chunk = jnp.concatenate([query.astype(jnp.float32), tail], axis=0).astype(jnp.bfloat16)
    for target in range(copies.shape[0]):
        copies[target] = chunk
    own_value[...] = projected(2)


def pages_kernel(counts, gathered, gains, cosine, sine, cache, out, queries, key_square, kv, held, sems):
    pages, _, page_len, width = cache.shape
    nodes = cosine.shape[0]
    groups = sems.shape[0]
    group_width = width // groups

    def fetch(group):
        columns = pl.ds(group * group_width, group_width)
        return pltpu.make_async_copy(
            cache.at[:, :, :, columns], kv.at[:, :, :, columns], sems.at[group]
        )

    for group in range(groups):
        fetch(group).start()
    squares = jnp.zeros((nodes, LANES), jnp.float32)
    extra = jnp.zeros((8, LANES), jnp.float32)
    for source in range(2 * HEADS):
        chunk = gathered[source].astype(jnp.float32)
        squares = squares + chunk[:nodes] * chunk[:nodes]
        extra = extra + chunk[nodes : nodes + 8]
    inverse = packed_inverse(squares, width)
    key_square[...] = extra
    token = lax.broadcasted_iota(jnp.int32, (nodes, page_len), 1)
    bias = []
    for page in range(pages):
        halves = [
            jnp.where(token < counts[2 * page + request : 2 * page + request + 1], 0.0, masked_score)
            for request in range(2)
        ]
        bias.append(jnp.concatenate(halves, axis=0))
    scale = HEAD_DIM ** (-0.5)
    cos_rows = cosine[...]
    sin_rows = sine[...]
    lane = lax.broadcasted_iota(jnp.int32, (2 * nodes, LANES), 1)
    stats = jnp.zeros((2 * nodes, LANES), jnp.float32)
    for head in range(HEADS):
        if head % (HEADS // groups) == 0:
            fetch(head // (HEADS // groups)).wait()
        base = head * HEAD_DIM
        front = gathered[spot_of(2 * head)][:nodes].astype(jnp.float32)
        back = gathered[spot_of(2 * head + 1)][:nodes].astype(jnp.float32)
        front = front * inverse * gains[2 * head : 2 * head + 1]
        back = back * inverse * gains[2 * head + 1 : 2 * head + 2]
        front, back = rotated(front, back, cos_rows, sin_rows)
        query = jnp.concatenate(paired(front, back), axis=0).astype(jnp.bfloat16)
        queries[head] = query
        keys = kv[:, 0, :, base : base + HEAD_DIM].reshape(pages * page_len, HEAD_DIM)
        scores = lax.dot_general(
            query, keys, (((1,), (1,)), ((), ())), preferred_element_type=jnp.float32
        )
        scores = [
            scores[:, page * page_len : (page + 1) * page_len] * scale + bias[page]
            for page in range(pages)
        ]
        top = jnp.max(functools.reduce(jnp.maximum, scores), axis=1, keepdims=True)
        weights = [jnp.exp(score - top) for score in scores]
        total = jnp.sum(functools.reduce(jnp.add, weights), axis=1, keepdims=True)
        values = kv[:, 1, :, base : base + HEAD_DIM].reshape(pages * page_len, HEAD_DIM)
        mixed = jnp.dot(
            jnp.concatenate(weights, axis=1).astype(jnp.bfloat16),
            values,
            preferred_element_type=jnp.float32,
        )
        stats = jnp.where(lane == head, top, stats)
        stats = jnp.where(lane == HEADS + head, total, stats)
        left, right = paired(mixed[:nodes], mixed[nodes:])
        held[2 * head] = left
        held[2 * head + 1] = right
    turned = columns_to_rows(stats)
    shifted = pltpu.roll(turned, HALF - nodes, 1)
    turned = jnp.where(in_first(LANES), turned, shifted)
    rows = [*split_three(turned[:HEADS]), *split_three(turned[HEADS : 2 * HEADS])]
    rows += [jnp.zeros_like(rows[0])] * 2
    for head in range(HEADS):
        tail = jnp.concatenate([row[head : head + 1] for row in rows], axis=0)
        for half in range(2):
            block = jnp.concatenate([held[2 * head + half], tail], axis=0)
            out[spot_of(2 * head + half)] = block.astype(jnp.bfloat16)


def tree_kernel(
    place,
    accepted,
    queries,
    own_key,
    other_key,
    own_value,
    key_square,
    gains,
    cosine,
    sine,
    ancestry,
    depth,
    ride,
    large,
    path_out,
    tree_out,
    large_out,
    sem,
):
    copy = pltpu.make_async_copy(large, large_out, sem)
    copy.start()
    width = 2 * HEADS * HALF
    requests, nodes, _ = ancestry.shape
    head = place[0] // 2
    even = jnp.full((nodes, LANES), place[0] % 2, jnp.int32) == 0
    first = in_first(nodes)
    sums = (key_square[0:1] + key_square[1:2]) + key_square[2:3]
    square = jnp.broadcast_to(sums, (LANES, LANES)).T
    square = jnp.where(first, square[:nodes], square[HALF : HALF + nodes])
    inverse = lax.rsqrt(square / width + norm_epsilon)
    own = own_key[...].astype(jnp.float32)
    other = other_key[...].astype(jnp.float32)
    front = jnp.where(even, own, other) * inverse * gains[pl.ds(2 * head, 1)]
    back = jnp.where(even, other, own) * inverse * gains[pl.ds(2 * head + 1, 1)]
    front, back = rotated(front, back, cosine[...], sine[...])
    kept = jnp.where(even, front, back).astype(jnp.bfloat16)
    keys = paired(front, back)
    value = own_value[...]
    query = queries[head]
    lane = lax.broadcasted_iota(jnp.int32, (nodes, LANES), 1)
    stats = jnp.zeros((nodes, LANES), jnp.float32)
    mixed = []
    pickers = []
    for request in range(requests):
        line = ancestry[request]
        scores = lax.dot_general(
            query[request * nodes : (request + 1) * nodes],
            keys[request].astype(jnp.bfloat16),
            (((1,), (1,)), ((), ())),
            preferred_element_type=jnp.float32,
        ) * (HEAD_DIM ** (-0.5))
        visible = line > 0.5
        scores = jnp.where(visible, scores, masked_score)
        top = jnp.max(scores, axis=1, keepdims=True)
        weights = jnp.where(visible, jnp.exp(scores - top), 0.0)
        total = jnp.sum(weights, axis=1, keepdims=True)
        mixed.append(jnp.dot(weights.astype(jnp.bfloat16), value, preferred_element_type=jnp.float32))
        stats = jnp.where(lane == request, top, stats)
        stats = jnp.where(lane == request + 2, total, stats)
        on_path = ancestry[request, pl.ds(accepted[request], 1), :]
        levels = depth[pl.ds(request, 1), :]
        wanted = (lax.broadcasted_iota(jnp.int32, (8, nodes), 0) + 1).astype(jnp.float32)
        picker = jnp.where(wanted == levels, on_path, 0.0).astype(jnp.bfloat16)
        pickers.append(picker)
    turned = columns_to_rows(stats)
    row = in_first(1)
    tail = [
        jnp.where(row, turned[0:1], pltpu.roll(turned[1:2], HALF, 1)),
        jnp.where(row, turned[2:3], pltpu.roll(turned[3:4], HALF, 1)),
        jnp.zeros((6, LANES), jnp.float32),
    ]
    tree_out[...] = jnp.concatenate(
        [jnp.where(first, mixed[0], mixed[1]), *tail, ride[...].astype(jnp.float32)], axis=0
    )
    for kind, block in enumerate((kept, value)):
        picked = [
            jnp.dot(picker, block, preferred_element_type=jnp.float32) for picker in pickers
        ]
        path_out[kind] = jnp.where(in_first(8), picked[0], picked[1])
    copy.wait()


def merge_kernel(parts, tree, out):
    count = parts.shape[0]
    nodes = parts.shape[1] - 8
    top_tree = tree[nodes : nodes + 1]
    tops = []
    totals = []
    for source in range(count):
        tail = parts[source].astype(jnp.float32)[nodes : nodes + 8]
        tops.append((tail[0:1] + tail[1:2]) + tail[2:3])
        totals.append((tail[3:4] + tail[4:5]) + tail[5:6])
    tops = jnp.concatenate(tops, axis=0)
    totals = jnp.concatenate(totals, axis=0)
    top = jnp.maximum(jnp.max(tops, axis=0, keepdims=True), top_tree)
    factors = jnp.exp(tops - top)
    factor_tree = jnp.exp(top_tree - top)
    total = jnp.sum(factors * totals, axis=0, keepdims=True) + factor_tree * tree[nodes + 1 : nodes + 2]
    shares = jnp.concatenate([factors / total, factor_tree / total], axis=0)
    turned = columns_to_rows(shares)
    first = in_first(nodes)

    def spread(source):
        return jnp.where(
            first,
            turned[0:nodes, source : source + 1],
            turned[HALF : HALF + nodes, source : source + 1],
        )

    mixed = spread(count) * tree[:nodes]
    for source in range(count):
        mixed = mixed + spread(source) * parts[source].astype(jnp.float32)[:nodes]
    result = jnp.concatenate([mixed, tree[nodes + 8 :]], axis=0).astype(jnp.bfloat16)
    for target in range(count):
        out[target] = result


def out_kernel(gathered, weight, drafted, out):
    count = gathered.shape[0]
    nodes = gathered.shape[1] - drafted.shape[0]
    total = jnp.zeros((2 * nodes, LANES), jnp.float32)
    for head in range(count // 2):
        both = paired(
            gathered[spot_of(2 * head)][:nodes].astype(jnp.float32),
            gathered[spot_of(2 * head + 1)][:nodes].astype(jnp.float32),
        )
        block = jnp.concatenate(both, axis=0).astype(jnp.bfloat16)
        total = total + lax.dot_general(
            block,
            weight[:, head * HEAD_DIM : (head + 1) * HEAD_DIM],
            (((1,), (1,)), ((), ())),
            preferred_element_type=jnp.float32,
        )
    packed = jnp.where(in_first(nodes), total[:nodes], total[nodes:])
    result = jnp.concatenate([packed, drafted[...].astype(jnp.float32)], axis=0).astype(jnp.bfloat16)
    for target in range(count):
        out[target] = result


def residual_kernel(gathered, gain, inputs, out, rows, sem):
    fetch = pltpu.make_async_copy(inputs, rows, sem)
    fetch.start()
    count = gathered.shape[0]
    nodes = rows.shape[0] // 2
    squares = jnp.zeros((nodes, LANES), jnp.float32)
    for source in range(count):
        chunk = gathered[source].astype(jnp.float32)[:nodes]
        squares = squares + chunk * chunk
    inverse = packed_inverse(squares, count * HALF)
    fetch.wait()
    for head in range(count // 2):
        both = paired(
            gathered[spot_of(2 * head)].astype(jnp.float32)[:nodes] * inverse,
            gathered[spot_of(2 * head + 1)].astype(jnp.float32)[:nodes] * inverse,
        )
        columns = slice(head * HEAD_DIM, (head + 1) * HEAD_DIM)
        block = jnp.concatenate(both, axis=0) * gain[:, columns]
        out[:, columns] = (rows[:, columns].astype(jnp.float32) + block).astype(jnp.bfloat16)


def down_kernel(hidden, weight, out, held):
    count, chunk_rows, _ = out.shape
    total_rows = hidden.shape[0]
    share = total_rows // count
    line = lax.broadcasted_iota(jnp.int32, (total_rows, total_rows), 0)
    column = lax.broadcasted_iota(jnp.int32, (total_rows, total_rows), 1)
    spot = line % count
    depth = count // SIDE
    owner = spot % depth * SIDE + spot // depth
    turn = (column == owner * share + line // count).astype(jnp.bfloat16)
    rows = jnp.dot(turn, hidden[...], preferred_element_type=jnp.float32).astype(jnp.bfloat16)
    for block in range(chunk_rows // share):
        sums = jnp.dot(
            rows,
            weight[:, block * LANES : (block + 1) * LANES],
            preferred_element_type=jnp.float32,
        )
        for row in range(share):
            held[pl.ds(block * share + row, count, stride=chunk_rows), :] = sums[
                row * count : (row + 1) * count
            ]
    for target in range(count):
        out[target] = held[target * chunk_rows : (target + 1) * chunk_rows].astype(jnp.bfloat16)


def last_kernel(shares, residual, gain, out):
    count, chunk_rows, _ = shares.shape
    share = out.shape[0]
    blocks = chunk_rows // share
    sums = jnp.zeros((chunk_rows, LANES), jnp.float32)
    for source in range(count):
        sums = sums + shares[source].astype(jnp.float32)
    parts = [sums[block * share : (block + 1) * share] for block in range(blocks)]
    squares = functools.reduce(jnp.add, [part * part for part in parts])
    square = jnp.sum(squares, axis=1, keepdims=True) / (blocks * LANES)
    inverse = lax.rsqrt(square + norm_epsilon)
    for block, part in enumerate(parts):
        columns = slice(block * LANES, (block + 1) * LANES)
        grown = residual[:, columns].astype(jnp.float32) + part * inverse * gain[:, columns]
        out[:, columns] = grown.astype(jnp.bfloat16)


def logits_kernel(early, late, vocab, out, table, drafted, sem):
    fetch = pltpu.make_async_copy(vocab, table, sem)
    fetch.start()
    count = early.shape[0]
    start = early.shape[1] - drafted.shape[0] // 4
    for head in range(count // 2):
        left = [part[spot_of(2 * head)].astype(jnp.float32)[start:] for part in (early, late)]
        right = [part[spot_of(2 * head + 1)].astype(jnp.float32)[start:] for part in (early, late)]
        both = paired(jnp.concatenate(left, axis=0), jnp.concatenate(right, axis=0))
        drafted[:, head * HEAD_DIM : (head + 1) * HEAD_DIM] = jnp.concatenate(both, axis=0).astype(
            jnp.bfloat16
        )
    fetch.wait()
    logits = lax.dot_general(
        drafted[...], table[...], (((1,), (1,)), ((), ())), preferred_element_type=jnp.float32
    )
    requests, drafts, _ = out.shape
    for request in range(requests):
        out[request] = logits[request * drafts : (request + 1) * drafts]


def rotated(front, back, cosine, sine):
    return front * cosine - back * sine, back * cosine + front * sine


def vmem(count):
    return [pl.BlockSpec(memory_space=pltpu.VMEM)] * count


SMEM = pl.BlockSpec(memory_space=pltpu.SMEM)


HBM = pl.BlockSpec(memory_space=pltpu.HBM)
MP = ("z", "x")
REQ = ("y", "c")
TURN = ("x", "z")


def limit(mib):
    return pltpu.CompilerParams(vmem_limit_bytes=mib * 2**20)


def exchange(chunks):
    return lax.all_to_all(chunks, TURN, 0, 0)


def per_device(
    draft_hidden,
    draft_weight,
    vocab_weight,
    tree_inputs,
    tree_parent,
    cache_len,
    page_table,
    kv_cache,
    accepted_node,
    qkv_weight,
    norm_gains,
    out_weight,
    gate_up_weight,
    down_weight,
):
    mp_count = lax.axis_size(MP)
    req_count = lax.axis_size(REQ)
    mp_place = lax.axis_index(MP)
    req_place = lax.axis_index(REQ)
    req_local, model_width = draft_hidden.shape
    draft_count = draft_weight.shape[0]
    slab = draft_weight.shape[2]
    vocab_local = vocab_weight.shape[0]
    rows = tree_inputs.shape[0]
    tree_size = tree_parent.shape[1]
    page_count, _, page_len, _ = kv_cache.shape
    table_width = page_table.shape[1]
    bf16 = jnp.bfloat16
    f32 = jnp.float32

    query_copies, own_key, own_value = pl.pallas_call(
        project_kernel,
        out_shape=(
            jax.ShapeDtypeStruct((mp_count, tree_size + 8, LANES), bf16),
            jax.ShapeDtypeStruct((tree_size, LANES), bf16),
            jax.ShapeDtypeStruct((tree_size, LANES), bf16),
        ),
        in_specs=[HBM, HBM],
        out_specs=tuple(vmem(3)),
        scratch_shapes=[
            pltpu.VMEM((rows, model_width), bf16),
            pltpu.VMEM((3, slab, model_width), bf16),
            pltpu.SemaphoreType.DMA((4,)),
        ],
        compiler_params=limit(8),
        name="project",
    )(tree_inputs, jnp.transpose(qkv_weight, (1, 2, 0)))
    gathered = exchange(query_copies)
    other_key = lax.ppermute(own_key, "x", [(i, i ^ 1) for i in range(SIDE)])

    pair = lax.ppermute(draft_hidden, "c", [(0, 1), (1, 0)])
    both = jnp.concatenate([draft_hidden, pair], axis=0)
    turns = req_count // 2
    hidden_parts = [both] + [
        lax.ppermute(both, "y", [(i, (i + k) % turns) for i in range(turns)])
        for k in range(1, turns)
    ]
    hidden_all = jnp.concatenate(hidden_parts, axis=0)
    spot = jnp.arange(req_count * req_local, dtype=jnp.int32)
    turn = spot // (2 * req_local)
    side = (spot // req_local) % 2
    holder = 2 * ((req_place // 2 - turn) % turns) + ((req_place % 2) ^ side)
    origin = holder * req_local + spot % req_local
    order = (origin[None, :] == spot[:, None]).astype(bf16)
    hidden_all = jnp.dot(order, hidden_all, preferred_element_type=f32).astype(bf16)
    draft_raw = jnp.einsum("rd,kde->rke", hidden_all, draft_weight, preferred_element_type=f32)
    own_columns = lax.dynamic_slice_in_dim(hidden_all, mp_place * slab, slab, 1).astype(f32)
    drafted = (own_columns[:, None, :] + jax.nn.silu(draft_raw)).astype(bf16)
    half_count = req_count * req_local * draft_count // 2
    drafted = drafted.reshape(2, half_count, slab)
    drafted = jnp.concatenate([drafted[0], drafted[1]], axis=1)

    ancestry, node_depth = tree_shape(tree_parent)
    positions = cache_len[:, None].astype(f32) + node_depth - 1.0
    freqs = rope_base ** (-jnp.arange(HALF, dtype=f32) * 2.0 / HEAD_DIM)
    angles = positions.T[:, :, None] * freqs[None, None, :]
    angles = angles.reshape(tree_size, LANES)
    cosine = jnp.cos(angles)
    sine = jnp.sin(angles)
    gain_rows = norm_gains.astype(f32)
    twice = gain_rows[:2].reshape(2, mp_count, slab)
    twice = jnp.concatenate([twice, twice], axis=2)

    slots = (req_place * mp_count + mp_place) * page_count + jnp.arange(page_count, dtype=jnp.int32)
    matches = page_table[None, :, :] == slots[:, None, None]
    starts = jnp.arange(table_width, dtype=jnp.int32) * page_len
    left = jnp.clip(cache_len[:, None] - starts[None, :], 0, page_len)
    counts = jnp.sum(jnp.where(matches, left[None], 0), axis=2).reshape(page_count * req_local, 1)
    counts = jnp.broadcast_to(counts, (page_count * req_local, LANES))

    groups = 4
    parts, queries, key_square = pl.pallas_call(
        pages_kernel,
        out_shape=(
            jax.ShapeDtypeStruct((mp_count, tree_size + 8, LANES), bf16),
            jax.ShapeDtypeStruct((HEADS, rows, HEAD_DIM), bf16),
            jax.ShapeDtypeStruct((8, LANES), f32),
        ),
        in_specs=[*vmem(5), HBM],
        out_specs=tuple(vmem(3)),
        scratch_shapes=[
            pltpu.VMEM(kv_cache.shape, bf16),
            pltpu.VMEM((mp_count, tree_size, LANES), f32),
            pltpu.SemaphoreType.DMA((groups,)),
        ],
        compiler_params=limit(60),
        cost_estimate=pl.CostEstimate(
            flops=4 * page_count * page_len * LANES * model_width,
            bytes_accessed=kv_cache.size * 2,
            transcendentals=page_count * page_len * tree_size * HEADS,
        ),
        name="pages",
    )(counts, gathered, twice[0], cosine, sine, kv_cache)
    arrived = exchange(parts)

    ride = half_count // 2
    first_ride, second_ride = drafted[:ride], drafted[ride:]
    path, tree, gate_up_copy = pl.pallas_call(
        tree_kernel,
        out_shape=(
            jax.ShapeDtypeStruct((2, 8, LANES), f32),
            jax.ShapeDtypeStruct((tree_size + 8 + ride, LANES), f32),
            jax.ShapeDtypeStruct(gate_up_weight.shape, bf16),
        ),
        in_specs=[SMEM, SMEM, *vmem(11), HBM],
        out_specs=(*vmem(2), HBM),
        scratch_shapes=[pltpu.SemaphoreType.DMA],
        compiler_params=limit(8),
        cost_estimate=pl.CostEstimate(flops=2**24, bytes_accessed=2**22, transcendentals=2**13),
        name="tree",
    )(
        mp_place.reshape(1),
        accepted_node,
        queries,
        own_key,
        other_key,
        own_value,
        key_square,
        twice[1],
        cosine,
        sine,
        ancestry,
        node_depth,
        first_ride,
        gate_up_weight,
    )
    accepted_kv = jnp.transpose(
        path[:, :draft_count].reshape(2, draft_count, req_local, slab), (2, 1, 0, 3)
    ).astype(bf16)

    out_twice = jnp.concatenate([out_weight.T, out_weight.T], axis=0)
    attended_copies = pl.pallas_call(
        merge_kernel,
        out_shape=jax.ShapeDtypeStruct((mp_count, tree_size + ride, LANES), bf16),
        in_specs=vmem(2),
        out_specs=vmem(1)[0],
        compiler_params=limit(8),
        name="merge",
    )(arrived, tree)
    out_gain = gain_rows[2:3]
    last_gain = gain_rows[3:4]
    attended_copies, out_twice, second_ride, accepted_kv, out_gain, last_gain = (
        lax.optimization_barrier(
            (attended_copies, out_twice, second_ride, accepted_kv, out_gain, last_gain)
        )
    )
    attended = exchange(attended_copies)
    out_copies = pl.pallas_call(
        out_kernel,
        out_shape=jax.ShapeDtypeStruct((mp_count, tree_size + ride, LANES), bf16),
        in_specs=vmem(3),
        out_specs=vmem(1)[0],
        compiler_params=limit(8),
        name="out_columns",
    )(attended, out_twice, second_ride)
    projected_out = exchange(out_copies)
    residual = pl.pallas_call(
        residual_kernel,
        out_shape=jax.ShapeDtypeStruct((rows, model_width), bf16),
        in_specs=[*vmem(2), HBM],
        out_specs=vmem(1)[0],
        scratch_shapes=[pltpu.VMEM((rows, model_width), bf16), pltpu.SemaphoreType.DMA],
        compiler_params=limit(8),
        name="residual",
    )(projected_out, out_gain, tree_inputs)
    gate_up = jnp.einsum("td,dce->tce", residual, gate_up_copy, preferred_element_type=f32)
    hidden = (jax.nn.silu(gate_up[:, 0]) * gate_up[:, 1]).astype(bf16)
    row_share = rows // mp_count
    chunk_rows = row_share * model_width // LANES
    partial = pl.pallas_call(
        down_kernel,
        out_shape=jax.ShapeDtypeStruct((mp_count, chunk_rows, LANES), bf16),
        in_specs=vmem(2),
        out_specs=vmem(1)[0],
        scratch_shapes=[pltpu.VMEM((mp_count * chunk_rows, LANES), f32)],
        compiler_params=limit(8),
        name="down",
    )(hidden, down_weight)
    shares = exchange(partial)

    draft_logits = pl.pallas_call(
        logits_kernel,
        out_shape=jax.ShapeDtypeStruct((req_count * req_local, draft_count, vocab_local), f32),
        in_specs=[*vmem(2), HBM],
        out_specs=vmem(1)[0],
        scratch_shapes=[
            pltpu.VMEM(vocab_weight.shape, bf16),
            pltpu.VMEM((req_count * req_local * draft_count, model_width), bf16),
            pltpu.SemaphoreType.DMA,
        ],
        compiler_params=limit(12),
        cost_estimate=pl.CostEstimate(flops=2**27, bytes_accessed=2**21, transcendentals=0),
        name="logits",
    )(attended, projected_out, vocab_weight)
    residual_rows = lax.dynamic_slice_in_dim(residual, mp_place * row_share, row_share, 0)
    layer_out = pl.pallas_call(
        last_kernel,
        out_shape=jax.ShapeDtypeStruct((row_share, model_width), bf16),
        in_specs=vmem(3),
        out_specs=vmem(1)[0],
        compiler_params=limit(8),
        name="last",
    )(shares, residual_rows, last_gain)
    return (draft_logits, layer_out, accepted_kv)


def solution(mesh):
    chips = mesh.devices.reshape(-1, 2, mesh.devices.shape[1] // SIDE, SIDE)
    mesh = jax.sharding.Mesh(chips, (*REQ, *MP))
    both = (*REQ, *MP)
    placed = (
        P(REQ, None),
        P(None, None, MP),
        P(both, None),
        P(REQ, None),
        P(REQ, None),
        P(REQ),
        P(REQ, None),
        P(both, None, None, None),
        P(REQ),
        P(None, None, MP),
        P(),
        P(None, MP),
        P(None, None, MP),
        P(MP, None),
    )
    return jax.shard_map(
        per_device,
        mesh=mesh,
        in_specs=placed,
        out_specs=(P(None, None, both), P(both, None), P(REQ, None, None, MP)),
        check_vma=False,
    )
```

time: 142 us -> 131 us (0.923); the launches traced: 139 us -> 131 us
  blocking collectives: 0 us -> 43.7 us
  waiting for transfers between devices: 54.6 us -> 29.9 us
  starting transfers between devices: 37.8 us -> 26.2 us
  local copies, waits for them, and re-layouts: 20.3 us -> 8.89 us
  Pallas kernels: 10.2 us -> 17.3 us
  matrix products: 8.35 us -> 1.66 us
  other arithmetic: 7.07 us -> 2.04 us
    all_to_all x0 -> x2, blocking collectives: none -> 43.7 us  [exchange(): return lax.all_to_all(chunks, TURN, 0, 0)]
    all_to_all x5 -> x3, waiting for transfers between devices: 54.6 us -> 26.3 us  [exchange(): return lax.all_to_all(chunks, TURN, 0, 0)]
    all_to_all x5 -> x3, starting transfers between devices: 33.2 us -> 21.1 us  [exchange(): return lax.all_to_all(chunks, TURN, 0, 0)]
    pallas_call x3 -> x9, Pallas kernels: 10.2 us -> 17.3 us  [the longest x1 8.27 us: per_device(): pl.pallas_call(pages_kernel, out_shape=(jax.ShapeDtypeStruct((mp_count, t...]
    dot_general x8 -> x2, matrix products: 7.24 us -> 1 us  [the longest x1 0.54 us: per_device(): jnp.einsum('rd,kde->rke', hidden_all, draft_weight, preferred_element_typ...]
    ppermute x5, waiting for transfers between devices: 0.01 us -> 3.55 us  [the longest x3 3.54 us: per_device(): lax.ppermute(both, 'y', [(i, (i + k) % turns) for i in range(turns)])]
    broadcast_in_dim x5 -> x2, local copies, waits for them, and re-layouts: 4.11 us -> 0.83 us  [per_device(): counts = jnp.broadcast_to(counts, (page_count * req_local, LANES))]
    pad x5 -> x0, local copies, waits for them, and re-layouts: 3.24 us -> none  [the longest x3 2.55 us: per_device(): wide = lambda a: jnp.pad(a, ((0, 0), (0, LANES - rows)))]
  transfers between devices with their start and end apart: 10 -> 8, of which waited for: 5 -> 6; matrix products, arithmetic and copies ran while one was open for 17% -> 4% of each run, Pallas kernels for 6% -> 10%
where the time goes in v3:
time: 131 us
  blocking collectives  43.7 us (33%)
  waiting for transfers between devices  29.9 us (23%)
  starting transfers between devices  26.2 us (20%)
  Pallas kernels  17.3 us (13%)
  local copies, waits for them, and re-layouts  8.89 us (7%)
  other arithmetic  2.04 us (2%)
  matrix products  1.66 us (1%)
    all_to_all x2, blocking collectives, exchange(): return lax.all_to_all(chunks, TURN, 0, 0)  43.7 us
    all_to_all x3, waiting for transfers between devices, exchange(): return lax.all_to_all(chunks, TURN, 0, 0)  26.3 us
    all_to_all x3, starting transfers between devices, exchange(): return lax.all_to_all(chunks, TURN, 0, 0)  21.1 us
    pallas_call x1, Pallas kernels, per_device(): pl.pallas_call(pages_kernel, out_shape=(jax.ShapeDtypeStruct((mp_count, t...  8.27 us
    unnamed x42, local copies, waits for them, and re-layouts  6.66 us
    ppermute x3, waiting for transfers between devices, per_device(): lax.ppermute(both, 'y', [(i, (i + k) % turns) for i in range(turns)])  3.54 us
    ppermute x3, starting transfers between devices, per_device(): lax.ppermute(both, 'y', [(i, (i + k) % turns) for i in range(turns)])  3.43 us
  transfers between devices with their start and end apart: 8, of which 6 were waited for; matrix products, arithmetic and copies ran while one was open for 4% of the time, Pallas kernels for 10%

profile of v3, /device:TPU:48, one launch (start us, length us, event | category | flops | bytes accessed | tf_op | source)
XLA Modules:
  0.0 130.7 jit_solution(17620216310305091678)
XLA Ops:
  0.8 1.0 copy-done.3
  1.8 1.1 copy-done.6
  2.9 2.0 %project.1 = (bf16[32,56,128]{2,1,0:T(8,128)(2,1)}, bf16[48,128]{1,0:T(8,128)(2,1)S(1)}, bf16[48,128]{1,0:T(8,128)(2,1)S(1)}) custom-call(bf16[96,2048]{1,0:T(8,128)(2,1)S(1)} %copy-done.3, bf16[3,64,2048]{2,1,0:T(8,128)(2,1)S(1)} %bitcast.35), custom_call_target="tpu_custom_call" | custom-call | tf_op jit(solution)/shard_map/project/pallas_call | solution.py:467
  4.9 11.2 %all-to-all-start = ((bf16[32,56,128]{2,1,0:T(8,128)(2,1)}), bf16[32,56,128]{2,1,0:T(8,128)(2,1)S(1)}, u32[]{:S(2)}, u32[]{:S(2)}) async-start(bf16[32,56,128]{2,1,0:T(8,128)(2,1)} %get-tuple-element.18), calls=%async_computation | async-start | bytes 917504 | tf_op jit(solution)/shard_map/all_to_all | solution.py:433
  16.1 1.6 %collective-permute-start = (bf16[48,128]{1,0:T(8,128)(2,1)S(1)}, bf16[48,128]{1,0:T(8,128)(2,1)S(1)}, u32[]{:S(2)}, u32[]{:S(2)}) collective-permute-start(bf16[48,128]{1,0:T(8,128)(2,1)S(1)} %get-tuple-element.21.own_key), channel_id=1, source_target_pairs={{0,1},{1,0},{2,3},{3,2},{4,5},{5,4},{6,7},{7,6},{8,9},{9,8},{10,11... | collective-permute-start | bytes 36872 | tf_op jit(solution)/shard_map/ppermute | solution.py:485
  21.2 2.9 %collective-permute-start.3 = (bf16[4,2048]{1,0:T(4,128)(2,1)S(1)}, bf16[4,2048]{1,0:T(4,128)(2,1)S(1)}, u32[]{:S(2)}, u32[]{:S(2)}) collective-permute-start(bf16[4,2048]{1,0:T(4,128)(2,1)S(1)} %pad_maximum_fusion.2), channel_id=1, source_target_pairs={{0,128},{64,192},{128,0},{192,64},{1,129},{65,193},{129,1},{193,65... | collective-permute-start | bytes 49160 | tf_op jit(solution)/shard_map/ppermute | solution.py:491
  24.4 2.0 %collective-permute-done.3 = bf16[4,2048]{1,0:T(4,128)(2,1)S(1)} collective-permute-done((bf16[4,2048]{1,0:T(4,128)(2,1)S(1)}, bf16[4,2048]{1,0:T(4,128)(2,1)S(1)}, u32[]{:S(2)}, u32[]{:S(2)}) %collective-permute-start.3) | collective-permute-done | bytes 16416 | tf_op jit(solution)/shard_map/ppermute | solution.py:491
  26.4 1.4 %collective-permute-done.2 = bf16[4,2048]{1,0:T(4,128)(2,1)S(1)} collective-permute-done((bf16[4,2048]{1,0:T(4,128)(2,1)S(1)}, bf16[4,2048]{1,0:T(4,128)(2,1)S(1)}, u32[]{:S(2)}, u32[]{:S(2)}) %collective-permute-start.2) | collective-permute-done | bytes 16416 | tf_op jit(solution)/shard_map/ppermute | solution.py:491
  27.9 5.1 %all-to-all-done.gathered = bf16[32,56,128]{2,1,0:T(8,128)(2,1)S(1)} async-done(((bf16[32,56,128]{2,1,0:T(8,128)(2,1)}), bf16[32,56,128]{2,1,0:T(8,128)(2,1)S(1)}, u32[]{:S(2)}, u32[]{:S(2)}) %all-to-all-start) | async-done | bytes 458784 | tf_op jit(solution)/shard_map/all_to_all | solution.py:433
  33.7 8.3 %pages.1 = (bf16[32,56,128]{2,1,0:T(8,128)(2,1)}, bf16[16,96,128]{2,1,0:T(8,128)(2,1)}, f32[8,128]{1,0:T(8,128)}) custom-call(s32[8,128]{1,0:T(8,128)} %broadcast_in_dim.15.counts, bf16[32,56,128]{2,1,0:T(8,128)(2,1)} %copy-done.14, f32[32,128]{1,0:T(8,128)} %get-tuple-element.34.gains, f32[48,128]{1,0:T(8,128)} %get-tuple-element.36.cosine, ...), custom_call_target="tpu_custom_call" | custom-call | flops 536870912 | bytes 4194304 | tf_op jit(solution)/shard_map/pages/pallas_call | solution.py:528
  42.1 5.1 %all-to-all-start.1 = ((bf16[32,56,128]{2,1,0:T(8,128)(2,1)}), bf16[32,56,128]{2,1,0:T(8,128)(2,1)S(1)}, u32[]{:S(2)}, u32[]{:S(2)}) async-start(bf16[32,56,128]{2,1,0:T(8,128)(2,1)} %get-tuple-element.19), calls=%async_computation.1 | async-start | bytes 917504 | tf_op jit(solution)/shard_map/all_to_all | solution.py:433
  48.1 1.6 %copy-done.1 = bf16[2048,2,256]{2,1,0:T(2,128)(2,1)S(1)} copy-done((bf16[2048,2,256]{2,1,0:T(2,128)(2,1)S(1)}, bf16[2048,2,256]{2,1,0:T(2,128)(2,1)}, u32[]{:S(2)}) %copy-start.1) | copy-done | bytes 2097176
  49.7 1.5 %tree.1 = (f32[2,8,128]{2,1,0:T(8,128)S(1)}, f32[72,128]{1,0:T(8,128)S(1)}, bf16[2048,2,256]{2,1,0:T(2,128)(2,1)S(1)}) custom-call(s32[1]{0:T(128)} %bitcast.3.place, s32[2]{0:T(128)S(1)} %copy-done.11, bf16[16,96,128]{2,1,0:T(8,128)(2,1)S(1)} %copy-done.7, bf16[48,128]{1,0:T(8,128)(2,1)S(1)} %get-tuple-element.21.own_key, ...), custom_call_target="tpu_custom_call" | custom-call | flops 16777216 | bytes 4194304 | tf_op jit(solution)/shard_map/tree/pallas_call | solution.py:554
  51.2 1.3 %copy-done.12 = bf16[2048,2,256]{2,1,0:T(2,128)(2,1)} copy-done((bf16[2048,2,256]{2,1,0:T(2,128)(2,1)}, bf16[2048,2,256]{2,1,0:T(2,128)(2,1)S(1)}, u32[]{:S(2)}) %copy-start.12) | copy-done | bytes 2097176
  53.2 10.0 %all-to-all-done.1.parts = bf16[32,56,128]{2,1,0:T(8,128)(2,1)S(1)} async-done(((bf16[32,56,128]{2,1,0:T(8,128)(2,1)}), bf16[32,56,128]{2,1,0:T(8,128)(2,1)S(1)}, u32[]{:S(2)}, u32[]{:S(2)}) %all-to-all-start.1) | async-done | bytes 458784 | tf_op jit(solution)/shard_map/all_to_all | solution.py:433
  63.2 0.8 merge.1
  64.0 21.8 %all_to_all.25.gathered.early = bf16[32,64,128]{2,1,0:T(8,128)(2,1)S(1)} all-to-all(bf16[32,64,128]{2,1,0:T(8,128)(2,1)S(1)} %merge.1), channel_id=1, replica_groups=mesh['y'=4,'c'=2,'z'=8,'x'=4] {'x','z'}, dimensions={0} | all-to-all | bytes 1048576 | tf_op jit(solution)/shard_map/all_to_all | solution.py:433
  86.4 21.8 %all_to_all.26.late.gathered = bf16[32,64,128]{2,1,0:T(8,128)(2,1)S(1)} all-to-all(bf16[32,64,128]{2,1,0:T(8,128)(2,1)S(1)} %out_columns.1), channel_id=1, replica_groups=mesh['y'=4,'c'=2,'z'=8,'x'=4] {'x','z'}, dimensions={0} | all-to-all | bytes 1048576 | tf_op jit(solution)/shard_map/all_to_all | solution.py:433
  109.5 1.4 %down.1 = bf16[32,48,128]{2,1,0:T(8,128)(2,1)} custom-call(bf16[96,256]{1,0:T(8,128)(2,1)S(1)} %fusion.4.hidden, bf16[256,2048]{1,0:T(8,128)(2,1)S(1)} %copy-done.5), custom_call_target="tpu_custom_call" | custom-call | tf_op jit(solution)/shard_map/down/pallas_call | solution.py:626
  110.9 4.9 %all-to-all-start.4 = ((bf16[32,48,128]{2,1,0:T(8,128)(2,1)}), bf16[32,48,128]{2,1,0:T(8,128)(2,1)S(1)}, u32[]{:S(2)}, u32[]{:S(2)}) async-start(bf16[32,48,128]{2,1,0:T(8,128)(2,1)} %down.1), calls=%async_computation.4 | async-start | bytes 786432 | tf_op jit(solution)/shard_map/all_to_all | solution.py:433
  115.8 1.4 %copy-done.2 = bf16[384,2048]{1,0:T(8,128)(2,1)S(1)} copy-done((bf16[384,2048]{1,0:T(8,128)(2,1)S(1)}, bf16[384,2048]{1,0:T(8,128)(2,1)}, u32[]{:S(2)}) %copy-start.2) | copy-done | bytes 1572888
  117.2 1.5 %logits.1 = f32[16,4,384]{2,1,0:T(4,128)} custom-call(bf16[32,64,128]{2,1,0:T(8,128)(2,1)S(1)} %all_to_all.25.gathered.early, bf16[32,64,128]{2,1,0:T(8,128)(2,1)S(1)} %all_to_all.26.late.gathered, bf16[384,2048]{1,0:T(8,128)(2,1)S(1)} %copy-done.2), custom_call_target="tpu_custom_call" | custom-call | flops 134217728 | bytes 2097152 | tf_op jit(solution)/shard_map/logits/pallas_call | solution.py:637
  118.7 11.3 %all-to-all-done.4.shares = bf16[32,48,128]{2,1,0:T(8,128)(2,1)S(1)} async-done(((bf16[32,48,128]{2,1,0:T(8,128)(2,1)}), bf16[32,48,128]{2,1,0:T(8,128)(2,1)S(1)}, u32[]{:S(2)}, u32[]{:S(2)}) %all-to-all-start.4) | async-done | bytes 393248 | tf_op jit(solution)/shard_map/all_to_all | solution.py:433
  129.9 0.8 last.1
  (85 shorter events, 8.1 us)
Async XLA Ops:
  0.6 46.7 %copy-start = (bf16[4,2048,64]{1,2,0:T(8,128)(2,1)S(1)}, bf16[4,2048,64]{1,2,0:T(8,128)(2,1)}, u32[]{:S(2)}) copy-start(bf16[4,2048,64]{1,2,0:T(8,128)(2,1)} %param.15) | copy-start | bytes 3145732
  0.6 17.1 %copy-start.20 = (s32[2]{0:T(128)S(1)}, s32[2]{0:T(128)}, u32[]{:S(2)}) copy-start(s32[2]{0:T(128)} %param.19) | copy-start | bytes 28
  0.7 17.4 %copy-start.18 = (s32[2,48]{1,0:T(2,128)S(1)}, s32[2,48]{1,0:T(2,128)}, u32[]{:S(2)}) copy-start(s32[2,48]{1,0:T(2,128)} %param.18) | copy-start | bytes 1156
  0.7 19.9 %collective-permute-start.1 = (bf16[2,2048]{1,0:T(2,128)(2,1)}, bf16[2,2048]{1,0:T(2,128)(2,1)S(1)}, u32[]{:S(2)}, u32[]{:S(2)}) collective-permute-start(bf16[2,2048]{1,0:T(2,128)(2,1)} %param.14), channel_id=1, source_target_pairs={{0,32},{32,0},{1,33},{33,1},{2,34},{34,2},{3,35},{35,3},{4,36},{36... | collective-permute-start | bytes 24584 | tf_op jit(solution)/shard_map/ppermute | solution.py:487
  2.9 15.0 %copy-start.16 = (bf16[4,2048]{1,0:T(4,128)(2,1)S(1)}, bf16[4,2048]{1,0:T(4,128)(2,1)}, u32[]{:S(2)}) copy-start(bf16[4,2048]{1,0:T(4,128)(2,1)} %param.24) | copy-start | bytes 49156
  2.9 16.0 %copy-start.15 = (bf16[2048,64]{0,1:T(8,128)(2,1)S(1)}, bf16[2048,64]{0,1:T(8,128)(2,1)}, u32[]{:S(2)}) copy-start(bf16[2048,64]{0,1:T(8,128)(2,1)} %param.25) | copy-start | bytes 786436
  2.9 16.8 %copy-start.19 = (s32[2,64]{1,0:T(2,128)S(1)}, s32[2,64]{1,0:T(2,128)}, u32[]{:S(2)}) copy-start(s32[2,64]{1,0:T(2,128)} %param.20) | copy-start | bytes 1540
  2.9 17.7 %copy-start.17 = (bf16[2,2048]{1,0:T(2,128)(2,1)S(1)}, bf16[2,2048]{1,0:T(2,128)(2,1)}, u32[]{:S(2)}) copy-start(bf16[2,2048]{1,0:T(2,128)(2,1)} %param.14) | copy-start | bytes 24580
  4.9 28.0 %all-to-all-start = ((bf16[32,56,128]{2,1,0:T(8,128)(2,1)}), bf16[32,56,128]{2,1,0:T(8,128)(2,1)S(1)}, u32[]{:S(2)}, u32[]{:S(2)}) async-start(bf16[32,56,128]{2,1,0:T(8,128)(2,1)} %get-tuple-element.18), calls=%async_computation | async-start | bytes 917504 | tf_op jit(solution)/shard_map/all_to_all | solution.py:433
  16.1 31.9 %collective-permute-start = (bf16[48,128]{1,0:T(8,128)(2,1)S(1)}, bf16[48,128]{1,0:T(8,128)(2,1)S(1)}, u32[]{:S(2)}, u32[]{:S(2)}) collective-permute-start(bf16[48,128]{1,0:T(8,128)(2,1)S(1)} %get-tuple-element.21.own_key), channel_id=1, source_target_pairs={{0,1},{1,0},{2,3},{3,2},{4,5},{5,4},{6,7},{7,6},{8,9},{9,8},{10,11... | collective-permute-start | bytes 36872 | tf_op jit(solution)/shard_map/ppermute | solution.py:485
  20.6 3.8 %collective-permute-start.4 = (bf16[4,2048]{1,0:T(4,128)(2,1)S(1)}, bf16[4,2048]{1,0:T(4,128)(2,1)S(1)}, u32[]{:S(2)}, u32[]{:S(2)}) collective-permute-start(bf16[4,2048]{1,0:T(4,128)(2,1)S(1)} %pad_maximum_fusion.2), channel_id=1, source_target_pairs={{0,192},{64,0},{128,64},{192,128},{1,193},{65,1},{129,65},{193,129... | collective-permute-start | bytes 49160 | tf_op jit(solution)/shard_map/ppermute | solution.py:491
  21.2 5.2 %collective-permute-start.3 = (bf16[4,2048]{1,0:T(4,128)(2,1)S(1)}, bf16[4,2048]{1,0:T(4,128)(2,1)S(1)}, u32[]{:S(2)}, u32[]{:S(2)}) collective-permute-start(bf16[4,2048]{1,0:T(4,128)(2,1)S(1)} %pad_maximum_fusion.2), channel_id=1, source_target_pairs={{0,128},{64,192},{128,0},{192,64},{1,129},{65,193},{129,1},{193,65... | collective-permute-start | bytes 49160 | tf_op jit(solution)/shard_map/ppermute | solution.py:491
  24.1 3.7 %collective-permute-start.2 = (bf16[4,2048]{1,0:T(4,128)(2,1)S(1)}, bf16[4,2048]{1,0:T(4,128)(2,1)S(1)}, u32[]{:S(2)}, u32[]{:S(2)}) collective-permute-start(bf16[4,2048]{1,0:T(4,128)(2,1)S(1)} %pad_maximum_fusion.2), channel_id=1, source_target_pairs={{0,64},{64,128},{128,192},{192,0},{1,65},{65,129},{129,193},{193,1... | collective-permute-start | bytes 49160 | tf_op jit(solution)/shard_map/ppermute | solution.py:491
  42.0 6.0 %copy-start.7 = (bf16[16,96,128]{2,1,0:T(8,128)(2,1)S(1)}, bf16[16,96,128]{2,1,0:T(8,128)(2,1)}, u32[]{:S(2)}) copy-start(bf16[16,96,128]{2,1,0:T(8,128)(2,1)} %get-tuple-element.20.queries) | copy-start | bytes 1179652
  42.0 6.0 %copy-start.8 = (f32[48,128]{1,0:T(8,128)S(1)}, f32[48,128]{1,0:T(8,128)}, u32[]{:S(2)}) copy-start(f32[48,128]{1,0:T(8,128)} %get-tuple-element.35.sine) | copy-start | bytes 73732
  42.0 6.0 %copy-start.9 = (f32[48,128]{1,0:T(8,128)S(1)}, f32[48,128]{1,0:T(8,128)}, u32[]{:S(2)}) copy-start(f32[48,128]{1,0:T(8,128)} %get-tuple-element.36.cosine) | copy-start | bytes 73732
  42.0 6.0 %copy-start.10 = (f32[8,128]{1,0:T(8,128)S(1)}, f32[8,128]{1,0:T(8,128)}, u32[]{:S(2)}) copy-start(f32[8,128]{1,0:T(8,128)} %get-tuple-element.23.key_square) | copy-start | bytes 12292
  42.0 6.0 %copy-start.11 = (s32[2]{0:T(128)S(1)}, s32[2]{0:T(128)}, u32[]{:S(2)}) copy-start(s32[2]{0:T(128)} %accepted.1) | copy-start | bytes 28
  42.1 21.2 %all-to-all-start.1 = ((bf16[32,56,128]{2,1,0:T(8,128)(2,1)}), bf16[32,56,128]{2,1,0:T(8,128)(2,1)S(1)}, u32[]{:S(2)}, u32[]{:S(2)}) async-start(bf16[32,56,128]{2,1,0:T(8,128)(2,1)} %get-tuple-element.19), calls=%async_computation.1 | async-start | bytes 917504 | tf_op jit(solution)/shard_map/all_to_all | solution.py:433
  48.1 1.6 %copy-start.1 = (bf16[2048,2,256]{2,1,0:T(2,128)(2,1)S(1)}, bf16[2048,2,256]{2,1,0:T(2,128)(2,1)}, u32[]{:S(2)}) copy-start(bf16[2048,2,256]{2,1,0:T(2,128)(2,1)} %large.1) | copy-start | bytes 6291460
  63.2 45.0 %copy-start.4 = (bf16[96,2048]{1,0:T(8,128)(2,1)S(1)}, bf16[96,2048]{1,0:T(8,128)(2,1)}, u32[]{:S(2)}) copy-start(bf16[96,2048]{1,0:T(8,128)(2,1)} %inputs.3) | copy-start | bytes 1179652
  85.9 23.0 %copy-start.13 = (bf16[2048,2,256]{2,1,0:T(2,128)(2,1)S(1)}, bf16[2048,2,256]{2,1,0:T(2,128)(2,1)}, u32[]{:S(2)}) copy-start(bf16[2048,2,256]{2,1,0:T(2,128)(2,1)} %copy-done.12) | copy-start | bytes 6291460
  110.9 19.1 %all-to-all-start.4 = ((bf16[32,48,128]{2,1,0:T(8,128)(2,1)}), bf16[32,48,128]{2,1,0:T(8,128)(2,1)S(1)}, u32[]{:S(2)}, u32[]{:S(2)}) async-start(bf16[32,48,128]{2,1,0:T(8,128)(2,1)} %down.1), calls=%async_computation.4 | async-start | bytes 786432 | tf_op jit(solution)/shard_map/all_to_all | solution.py:433
  115.7 1.4 %copy-start.2 = (bf16[384,2048]{1,0:T(8,128)(2,1)S(1)}, bf16[384,2048]{1,0:T(8,128)(2,1)}, u32[]{:S(2)}) copy-start(bf16[384,2048]{1,0:T(8,128)(2,1)} %vocab.1) | copy-start | bytes 4718596
  (5 other events, 5.5 us)

commit v4 on v3

--- a/solution.py
+++ b/solution.py
@@ -65,11 +65,14 @@
     return jnp.concatenate([columns, jnp.zeros((rest, LANES), jnp.float32)], axis=0).T
 
 
-def project_kernel(inputs, weights, copies, own_key, own_value, rows, columns, sems):
+def project_kernel(
+    place, hidden, inputs, weights, draft_weights, copies, own_key, own_value, rows, columns, heads, sems
+):
     nodes = own_key.shape[0]
     fetches = [pltpu.make_async_copy(inputs, rows, sems.at[0])]
     for kind in range(3):
         fetches.append(pltpu.make_async_copy(weights.at[kind], columns.at[kind], sems.at[1 + kind]))
+    fetches.append(pltpu.make_async_copy(draft_weights, heads, sems.at[4]))
     for fetch in fetches:
         fetch.start()
     fetches[0].wait()
@@ -97,14 +100,33 @@
     right = jnp.sum(jnp.where(first, zero, squares), axis=1, keepdims=True)
     turned = columns_to_rows(jnp.where(lane == 0, left, jnp.where(lane == 1, right, zero)))
     sums = jnp.where(in_first(1), turned[0:1], pltpu.roll(turned[1:2], HALF, 1))
-    tail = jnp.concatenate([*split_three(sums), jnp.zeros((5, LANES), jnp.float32)], axis=0)
+    fetches[4].wait()
+    states = hidden[...]
+    start = pl.multiple_of(place[0] // 2 * LANES, LANES)
+    own = hidden[:, pl.ds(start, LANES)].astype(jnp.float32)
+    swapped = pltpu.roll(own, HALF, 1)
+    here = jnp.full(own.shape, place[0] % 2, jnp.int32) == lax.broadcasted_iota(jnp.int32, own.shape, 1) // HALF
+    own = jnp.where(here, own, swapped)
+    pairs = []
+    for pair in range(heads.shape[0] // LANES):
+        raw = lax.dot_general(
+            states,
+            heads[pair * LANES : (pair + 1) * LANES],
+            (((1,), (1,)), ((), ())),
+            preferred_element_type=jnp.float32,
+        )
+        pairs.append(own + raw / (1.0 + jnp.exp(-raw)))
+    drafted = [part[r : r + 1] for r in range(states.shape[0]) for part in pairs]
+    tail = jnp.concatenate([*split_three(sums), *drafted, jnp.zeros_like(sums)], axis=0)
     chunk = jnp.concatenate([query.astype(jnp.float32), tail], axis=0).astype(jnp.bfloat16)
     for target in range(copies.shape[0]):
         copies[target] = chunk
     own_value[...] = projected(2)
 
 
-def pages_kernel(counts, gathered, gains, cosine, sine, cache, out, queries, key_square, kv, held, sems):
+def pages_kernel(
+    counts, gathered, gains, cosine, sine, cache, out, queries, key_square, drafts, kv, held, sems
+):
     pages, _, page_len, width = cache.shape
     nodes = cosine.shape[0]
     groups = sems.shape[0]
@@ -126,6 +148,13 @@
         extra = extra + chunk[nodes : nodes + 8]
     inverse = packed_inverse(squares, width)
     key_square[...] = extra
+    for head in range(HEADS):
+        tails = [gathered[spot_of(2 * head + side)].astype(jnp.float32)[nodes:] for side in range(2)]
+        even, odd = paired(*tails)
+        lines = [part[row : row + 1] for row in range(3, 7) for part in (even, odd)]
+        drafts[:, head * HEAD_DIM : (head + 1) * HEAD_DIM] = jnp.concatenate(lines, axis=0).astype(
+            jnp.bfloat16
+        )
     token = lax.broadcasted_iota(jnp.int32, (nodes, page_len), 1)
     bias = []
     for page in range(pages):
@@ -197,7 +226,6 @@
     sine,
     ancestry,
     depth,
-    ride,
     large,
     path_out,
     tree_out,
@@ -257,7 +285,7 @@
         jnp.zeros((6, LANES), jnp.float32),
     ]
     tree_out[...] = jnp.concatenate(
-        [jnp.where(first, mixed[0], mixed[1]), *tail, ride[...].astype(jnp.float32)], axis=0
+        [jnp.where(first, mixed[0], mixed[1]), *tail], axis=0
     )
     for kind, block in enumerate((kept, value)):
         picked = [
@@ -297,14 +325,14 @@
     mixed = spread(count) * tree[:nodes]
     for source in range(count):
         mixed = mixed + spread(source) * parts[source].astype(jnp.float32)[:nodes]
-    result = jnp.concatenate([mixed, tree[nodes + 8 :]], axis=0).astype(jnp.bfloat16)
+    result = mixed.astype(jnp.bfloat16)
     for target in range(count):
         out[target] = result
 
 
-def out_kernel(gathered, weight, drafted, out):
+def out_kernel(gathered, weight, out):
     count = gathered.shape[0]
-    nodes = gathered.shape[1] - drafted.shape[0]
+    nodes = gathered.shape[1]
     total = jnp.zeros((2 * nodes, LANES), jnp.float32)
     for head in range(count // 2):
         both = paired(
@@ -318,8 +346,7 @@
             (((1,), (1,)), ((), ())),
             preferred_element_type=jnp.float32,
         )
-    packed = jnp.where(in_first(nodes), total[:nodes], total[nodes:])
-    result = jnp.concatenate([packed, drafted[...].astype(jnp.float32)], axis=0).astype(jnp.bfloat16)
+    result = jnp.where(in_first(nodes), total[:nodes], total[nodes:]).astype(jnp.bfloat16)
     for target in range(count):
         out[target] = result
 
@@ -387,25 +414,17 @@
         out[:, columns] = grown.astype(jnp.bfloat16)
 
 
-def logits_kernel(early, late, vocab, out, table, drafted, sem):
+def logits_kernel(origins, drafts, vocab, out, table, sem):
     fetch = pltpu.make_async_copy(vocab, table, sem)
     fetch.start()
-    count = early.shape[0]
-    start = early.shape[1] - drafted.shape[0] // 4
-    for head in range(count // 2):
-        left = [part[spot_of(2 * head)].astype(jnp.float32)[start:] for part in (early, late)]
-        right = [part[spot_of(2 * head + 1)].astype(jnp.float32)[start:] for part in (early, late)]
-        both = paired(jnp.concatenate(left, axis=0), jnp.concatenate(right, axis=0))
-        drafted[:, head * HEAD_DIM : (head + 1) * HEAD_DIM] = jnp.concatenate(both, axis=0).astype(
-            jnp.bfloat16
-        )
+    requests, levels, _ = out.shape
+    vectors = drafts[...]
     fetch.wait()
     logits = lax.dot_general(
-        drafted[...], table[...], (((1,), (1,)), ((), ())), preferred_element_type=jnp.float32
-    )
-    requests, drafts, _ = out.shape
-    for request in range(requests):
-        out[request] = logits[request * drafts : (request + 1) * drafts]
+        vectors, table[...], (((1,), (1,)), ((), ())), preferred_element_type=jnp.float32
+    )
+    for spot in range(requests):
+        out[pl.ds(origins[spot], 1)] = logits[spot * levels : (spot + 1) * levels][None]
 
 
 def rotated(front, back, cosine, sine):
@@ -471,40 +490,26 @@
             jax.ShapeDtypeStruct((tree_size, LANES), bf16),
             jax.ShapeDtypeStruct((tree_size, LANES), bf16),
         ),
-        in_specs=[HBM, HBM],
+        in_specs=[SMEM, *vmem(1), HBM, HBM, HBM],
         out_specs=tuple(vmem(3)),
         scratch_shapes=[
             pltpu.VMEM((rows, model_width), bf16),
             pltpu.VMEM((3, slab, model_width), bf16),
-            pltpu.SemaphoreType.DMA((4,)),
+            pltpu.VMEM((draft_count * slab, model_width), bf16),
+            pltpu.SemaphoreType.DMA((5,)),
         ],
-        compiler_params=limit(8),
+        compiler_params=limit(60),
+        cost_estimate=pl.CostEstimate(flops=2**32, bytes_accessed=0, transcendentals=0),
         name="project",
-    )(tree_inputs, jnp.transpose(qkv_weight, (1, 2, 0)))
+    )(
+        mp_place.reshape(1),
+        draft_hidden,
+        tree_inputs,
+        jnp.transpose(qkv_weight, (1, 2, 0)),
+        jnp.transpose(draft_weight, (0, 2, 1)).reshape(draft_count * slab, model_width),
+    )
     gathered = exchange(query_copies)
     other_key = lax.ppermute(own_key, "x", [(i, i ^ 1) for i in range(SIDE)])
-
-    pair = lax.ppermute(draft_hidden, "c", [(0, 1), (1, 0)])
-    both = jnp.concatenate([draft_hidden, pair], axis=0)
-    turns = req_count // 2
-    hidden_parts = [both] + [
-        lax.ppermute(both, "y", [(i, (i + k) % turns) for i in range(turns)])
-        for k in range(1, turns)
-    ]
-    hidden_all = jnp.concatenate(hidden_parts, axis=0)
-    spot = jnp.arange(req_count * req_local, dtype=jnp.int32)
-    turn = spot // (2 * req_local)
-    side = (spot // req_local) % 2
-    holder = 2 * ((req_place // 2 - turn) % turns) + ((req_place % 2) ^ side)
-    origin = holder * req_local + spot % req_local
-    order = (origin[None, :] == spot[:, None]).astype(bf16)
-    hidden_all = jnp.dot(order, hidden_all, preferred_element_type=f32).astype(bf16)
-    draft_raw = jnp.einsum("rd,kde->rke", hidden_all, draft_weight, preferred_element_type=f32)
-    own_columns = lax.dynamic_slice_in_dim(hidden_all, mp_place * slab, slab, 1).astype(f32)
-    drafted = (own_columns[:, None, :] + jax.nn.silu(draft_raw)).astype(bf16)
-    half_count = req_count * req_local * draft_count // 2
-    drafted = drafted.reshape(2, half_count, slab)
-    drafted = jnp.concatenate([drafted[0], drafted[1]], axis=1)
 
     ancestry, node_depth = tree_shape(tree_parent)
     positions = cache_len[:, None].astype(f32) + node_depth - 1.0
@@ -522,47 +527,55 @@
     starts = jnp.arange(table_width, dtype=jnp.int32) * page_len
     left = jnp.clip(cache_len[:, None] - starts[None, :], 0, page_len)
     counts = jnp.sum(jnp.where(matches, left[None], 0), axis=2).reshape(page_count * req_local, 1)
-    counts = jnp.broadcast_to(counts, (page_count * req_local, LANES))
 
     groups = 4
-    parts, queries, key_square = pl.pallas_call(
+    parts, queries, key_square, drafts = pl.pallas_call(
         pages_kernel,
         out_shape=(
             jax.ShapeDtypeStruct((mp_count, tree_size + 8, LANES), bf16),
             jax.ShapeDtypeStruct((HEADS, rows, HEAD_DIM), bf16),
             jax.ShapeDtypeStruct((8, LANES), f32),
+            jax.ShapeDtypeStruct((req_local * draft_count, model_width), bf16),
         ),
         in_specs=[*vmem(5), HBM],
-        out_specs=tuple(vmem(3)),
+        out_specs=tuple(vmem(4)),
         scratch_shapes=[
             pltpu.VMEM(kv_cache.shape, bf16),
             pltpu.VMEM((mp_count, tree_size, LANES), f32),
             pltpu.SemaphoreType.DMA((groups,)),
         ],
-        compiler_params=limit(60),
-        cost_estimate=pl.CostEstimate(
-            flops=4 * page_count * page_len * LANES * model_width,
-            bytes_accessed=kv_cache.size * 2,
-            transcendentals=page_count * page_len * tree_size * HEADS,
-        ),
+        compiler_params=limit(52),
+        cost_estimate=pl.CostEstimate(flops=2**33, bytes_accessed=0, transcendentals=0),
         name="pages",
     )(counts, gathered, twice[0], cosine, sine, kv_cache)
     arrived = exchange(parts)
 
-    ride = half_count // 2
-    first_ride, second_ride = drafted[:ride], drafted[ride:]
+    pair = lax.ppermute(drafts, "c", [(0, 1), (1, 0)])
+    both = jnp.concatenate([drafts, pair], axis=0)
+    turns = req_count // 2
+    drafted = [both] + [
+        lax.ppermute(both, "y", [(i, (i + k) % turns) for i in range(turns)])
+        for k in range(1, turns)
+    ]
+    drafted = jnp.concatenate(drafted, axis=0)
+    spot = jnp.arange(req_count * req_local, dtype=jnp.int32)
+    turn = spot // (2 * req_local)
+    side = (spot // req_local) % 2
+    holder = 2 * ((req_place // 2 - turn) % turns) + ((req_place % 2) ^ side)
+    origins = holder * req_local + spot % req_local
+
     path, tree, gate_up_copy = pl.pallas_call(
         tree_kernel,
         out_shape=(
             jax.ShapeDtypeStruct((2, 8, LANES), f32),
-            jax.ShapeDtypeStruct((tree_size + 8 + ride, LANES), f32),
+            jax.ShapeDtypeStruct((tree_size + 8, LANES), f32),
             jax.ShapeDtypeStruct(gate_up_weight.shape, bf16),
         ),
-        in_specs=[SMEM, SMEM, *vmem(11), HBM],
+        in_specs=[SMEM, SMEM, *vmem(10), HBM],
         out_specs=(*vmem(2), HBM),
         scratch_shapes=[pltpu.SemaphoreType.DMA],
-        compiler_params=limit(8),
-        cost_estimate=pl.CostEstimate(flops=2**24, bytes_accessed=2**22, transcendentals=2**13),
+        compiler_params=limit(60),
+        cost_estimate=pl.CostEstimate(flops=2**31, bytes_accessed=0, transcendentals=2**13),
         name="tree",
     )(
         mp_place.reshape(1),
@@ -577,7 +590,6 @@
         sine,
         ancestry,
         node_depth,
-        first_ride,
         gate_up_weight,
     )
     accepted_kv = jnp.transpose(
@@ -587,7 +599,7 @@
     out_twice = jnp.concatenate([out_weight.T, out_weight.T], axis=0)
     attended_copies = pl.pallas_call(
         merge_kernel,
-        out_shape=jax.ShapeDtypeStruct((mp_count, tree_size + ride, LANES), bf16),
+        out_shape=jax.ShapeDtypeStruct((mp_count, tree_size, LANES), bf16),
         in_specs=vmem(2),
         out_specs=vmem(1)[0],
         compiler_params=limit(8),
@@ -595,21 +607,22 @@
     )(arrived, tree)
     out_gain = gain_rows[2:3]
     last_gain = gain_rows[3:4]
-    attended_copies, out_twice, second_ride, accepted_kv, out_gain, last_gain = (
+    attended_copies, out_twice, accepted_kv, out_gain, last_gain, drafted, origins = (
         lax.optimization_barrier(
-            (attended_copies, out_twice, second_ride, accepted_kv, out_gain, last_gain)
+            (attended_copies, out_twice, accepted_kv, out_gain, last_gain, drafted, origins)
         )
     )
     attended = exchange(attended_copies)
     out_copies = pl.pallas_call(
         out_kernel,
-        out_shape=jax.ShapeDtypeStruct((mp_count, tree_size + ride, LANES), bf16),
-        in_specs=vmem(3),
+        out_shape=jax.ShapeDtypeStruct((mp_count, tree_size, LANES), bf16),
+        in_specs=vmem(2),
         out_specs=vmem(1)[0],
         compiler_params=limit(8),
         name="out_columns",
-    )(attended, out_twice, second_ride)
+    )(attended, out_twice)
     projected_out = exchange(out_copies)
+    projected_out, drafted, origins = lax.optimization_barrier((projected_out, drafted, origins))
     residual = pl.pallas_call(
         residual_kernel,
         out_shape=jax.ShapeDtypeStruct((rows, model_width), bf16),
@@ -637,17 +650,13 @@
     draft_logits = pl.pallas_call(
         logits_kernel,
         out_shape=jax.ShapeDtypeStruct((req_count * req_local, draft_count, vocab_local), f32),
-        in_specs=[*vmem(2), HBM],
+        in_specs=[SMEM, *vmem(1), HBM],
         out_specs=vmem(1)[0],
-        scratch_shapes=[
-            pltpu.VMEM(vocab_weight.shape, bf16),
-            pltpu.VMEM((req_count * req_local * draft_count, model_width), bf16),
-            pltpu.SemaphoreType.DMA,
-        ],
-        compiler_params=limit(12),
-        cost_estimate=pl.CostEstimate(flops=2**27, bytes_accessed=2**21, transcendentals=0),
+        scratch_shapes=[pltpu.VMEM(vocab_weight.shape, bf16), pltpu.SemaphoreType.DMA],
+        compiler_params=limit(60),
+        cost_estimate=pl.CostEstimate(flops=2**31, bytes_accessed=0, transcendentals=0),
         name="logits",
-    )(attended, projected_out, vocab_weight)
+    )(origins, drafted, vocab_weight)
     residual_rows = lax.dynamic_slice_in_dim(residual, mp_place * row_share, row_share, 0)
     layer_out = pl.pallas_call(
         last_kernel,

time: 131 us -> 187 us (1.43); the launches traced: 131 us -> 185 us
  Pallas kernels: 17.3 us -> 85.5 us
  waiting for transfers between devices: 29.9 us -> 24.1 us
  local copies, waits for them, and re-layouts: 8.89 us -> 4.44 us
  blocking collectives: 43.7 us -> 40.9 us
    pallas_call x1, Pallas kernels: 1.51 us -> 66.3 us  [per_device(): pl.pallas_call(tree_kernel, out_shape=(jax.ShapeDtypeStruct((2, 8, LANES)...]
    all_to_all x3, waiting for transfers between devices: 26.3 us -> 19.9 us  [exchange(): return lax.all_to_all(chunks, TURN, 0, 0)]
    unnamed x42 -> x35, local copies, waits for them, and re-layouts: 6.66 us -> 2.31 us
    all_to_all x2, blocking collectives: 43.7 us -> 40.9 us  [exchange(): return lax.all_to_all(chunks, TURN, 0, 0)]
    pallas_call x1, Pallas kernels: 2.01 us -> 4.21 us  [per_device(): pl.pallas_call(project_kernel, out_shape=(jax.ShapeDtypeStruct((mp_count,...]
    pallas_call x1, Pallas kernels: 1.49 us -> 3.61 us  [per_device(): pl.pallas_call(logits_kernel, out_shape=jax.ShapeDtypeStruct((req_count *...]
  transfers between devices with their start and end apart: 8 -> 8, of which waited for: 6 -> 4; matrix products, arithmetic and copies ran while one was open for 4% -> 3% of each run, Pallas kernels for 10% -> 42%
where the time goes in v4:
time: 187 us; the launch traced here: 185 us
  Pallas kernels  85.5 us (46%)
  blocking collectives  40.9 us (22%)
  starting transfers between devices  25.4 us (14%)
  waiting for transfers between devices  24.1 us (13%)
  local copies, waits for them, and re-layouts  4.44 us (2%)
    pallas_call x1, Pallas kernels, per_device(): pl.pallas_call(tree_kernel, out_shape=(jax.ShapeDtypeStruct((2, 8, LANES)...  66.3 us
    all_to_all x2, blocking collectives, exchange(): return lax.all_to_all(chunks, TURN, 0, 0)  40.9 us
    all_to_all x3, starting transfers between devices, exchange(): return lax.all_to_all(chunks, TURN, 0, 0)  20.8 us
    all_to_all x3, waiting for transfers between devices, exchange(): return lax.all_to_all(chunks, TURN, 0, 0)  19.9 us
    pallas_call x1, Pallas kernels, per_device(): pl.pallas_call(pages_kernel, out_shape=(jax.ShapeDtypeStruct((mp_count, t...  7.28 us
    pallas_call x1, Pallas kernels, per_device(): pl.pallas_call(project_kernel, out_shape=(jax.ShapeDtypeStruct((mp_count,...  4.21 us
    ppermute x3, waiting for transfers between devices, per_device(): lax.ppermute(both, 'y', [(i, (i + k) % turns) for i in range(turns)])  4.13 us
  transfers between devices with their start and end apart: 8, of which 4 were waited for; matrix products, arithmetic and copies ran while one was open for 3% of the time, Pallas kernels for 42%

profile of v4, /device:TPU:48, one launch (start us, length us, event | category | flops | bytes accessed | tf_op | source)
XLA Modules:
  0.0 184.6 jit_solution(4276726819842202746)
XLA Ops:
  0.7 4.2 %project.1 = (bf16[32,56,128]{2,1,0:T(8,128)(2,1)}, bf16[48,128]{1,0:T(8,128)(2,1)}, bf16[48,128]{1,0:T(8,128)(2,1)}) custom-call(s32[1]{0:T(128)} %bitcast.place, bf16[2,2048]{1,0:T(2,128)(2,1)} %hidden.1, bf16[96,2048]{1,0:T(8,128)(2,1)} %inputs.3, bf16[3,64,2048]{2,1,0:T(8,128)(2,1)} %bitcast.32, bf16[256,2048]{1,0:T(8,128)(2,1)} %bitcast.31), custom_call_target="tpu_custom_call" | custom-call | flops 4294967296 | tf_op jit(solution)/shard_map/project/pallas_call | solution.py:486
  4.9 11.2 %all-to-all-start = ((bf16[32,56,128]{2,1,0:T(8,128)(2,1)}), bf16[32,56,128]{2,1,0:T(8,128)(2,1)S(1)}, u32[]{:S(2)}, u32[]{:S(2)}) async-start(bf16[32,56,128]{2,1,0:T(8,128)(2,1)} %get-tuple-element.23), calls=%async_computation | async-start | bytes 917504 | tf_op jit(solution)/shard_map/all_to_all | solution.py:452
  16.1 1.6 collective-permute-start
  18.4 0.9 fusion.21
  19.8 0.7 fusion.11
  21.3 11.0 %all-to-all-done.gathered = bf16[32,56,128]{2,1,0:T(8,128)(2,1)S(1)} async-done(((bf16[32,56,128]{2,1,0:T(8,128)(2,1)}), bf16[32,56,128]{2,1,0:T(8,128)(2,1)S(1)}, u32[]{:S(2)}, u32[]{:S(2)}) %all-to-all-start) | async-done | bytes 458784 | tf_op jit(solution)/shard_map/all_to_all | solution.py:452
  32.3 7.3 %pages.1 = (bf16[32,56,128]{2,1,0:T(8,128)(2,1)}, bf16[16,96,128]{2,1,0:T(8,128)(2,1)S(1)}, f32[8,128]{1,0:T(8,128)S(1)}, bf16[8,2048]{1,0:T(8,128)(2,1)S(1)}) custom-call(s32[8,1]{1,0:T(8,128)S(1)} %reshape.83.counts, bf16[32,56,128]{2,1,0:T(8,128)(2,1)S(1)} %all-to-all-done.gathered, f32[32,128]{1,0:T(8,128)S(1)} %get-tuple-element.48.gains, ...), custom_call_target="tpu_custom_call" | custom-call | flops 8589934592 | tf_op jit(solution)/shard_map/pages/pallas_call | solution.py:532
  39.6 0.8 copy-done.5
  40.4 4.9 %all-to-all-start.1 = ((bf16[32,56,128]{2,1,0:T(8,128)(2,1)}), bf16[32,56,128]{2,1,0:T(8,128)(2,1)S(1)}, u32[]{:S(2)}, u32[]{:S(2)}) async-start(bf16[32,56,128]{2,1,0:T(8,128)(2,1)} %get-tuple-element.24), calls=%async_computation.1 | async-start | bytes 917504 | tf_op jit(solution)/shard_map/all_to_all | solution.py:452
  45.3 1.4 collective-permute-start.2
  47.3 66.3 %tree.1 = (f32[2,8,128]{2,1,0:T(8,128)}, f32[56,128]{1,0:T(8,128)}, bf16[2048,2,256]{2,1,0:T(2,128)(2,1)}) custom-call(s32[1]{0:T(128)} %bitcast.place, s32[2]{0:T(128)} %accepted.1, bf16[16,96,128]{2,1,0:T(8,128)(2,1)} %copy-done.5, bf16[48,128]{1,0:T(8,128)(2,1)} %get-tuple-element.26.own_key, bf16[48,128]{1,0:T(8,128)(2,1)} %copy-done.14, ...), custom_call_target="tpu_custom_call" | custom-call | flops 2147483648 | tf_op jit(solution)/shard_map/tree/pallas_call | solution.py:567
  113.6 0.7 slice.58
  115.1 0.6 collective-permute-start.3
  115.7 1.1 collective-permute-start.4
  116.8 4.1 %collective-permute-done.3 = bf16[16,2048]{1,0:T(8,128)(2,1)S(1)} collective-permute-done((bf16[16,2048]{1,0:T(8,128)(2,1)S(1)}, bf16[16,2048]{1,0:T(8,128)(2,1)S(1)}, u32[]{:S(2)}, u32[]{:S(2)}) %collective-permute-start.3) | collective-permute-done | bytes 65568 | tf_op jit(solution)/shard_map/ppermute | solution.py:557
  120.9 0.8 copy-done.2
  121.7 0.7 merge.1
  122.5 23.3 %all_to_all.25.gathered = bf16[32,48,128]{2,1,0:T(8,128)(2,1)S(1)} all-to-all(bf16[32,48,128]{2,1,0:T(8,128)(2,1)S(1)} %merge.1), channel_id=1, replica_groups=mesh['y'=4,'c'=2,'z'=8,'x'=4] {'x','z'}, dimensions={0} | all-to-all | bytes 786432 | tf_op jit(solution)/shard_map/all_to_all | solution.py:452
  146.4 17.6 %all_to_all.26.gathered = bf16[32,48,128]{2,1,0:T(8,128)(2,1)S(1)} all-to-all(bf16[32,48,128]{2,1,0:T(8,128)(2,1)S(1)} %out_columns.1), channel_id=1, replica_groups=mesh['y'=4,'c'=2,'z'=8,'x'=4] {'x','z'}, dimensions={0} | all-to-all | bytes 786432 | tf_op jit(solution)/shard_map/all_to_all | solution.py:452
  165.2 1.4 down.1
  166.5 4.7 %all-to-all-start.4 = ((bf16[32,48,128]{2,1,0:T(8,128)(2,1)}), bf16[32,48,128]{2,1,0:T(8,128)(2,1)S(1)}, u32[]{:S(2)}, u32[]{:S(2)}) async-start(bf16[32,48,128]{2,1,0:T(8,128)(2,1)} %down.1), calls=%async_computation.4 | async-start | bytes 786432 | tf_op jit(solution)/shard_map/all_to_all | solution.py:452
  171.2 3.6 %logits.1 = f32[16,4,384]{2,1,0:T(4,128)} custom-call(s32[16]{0:T(128)} %fusion.12.origins, bf16[64,2048]{1,0:T(8,128)(2,1)} %copy-done.10, bf16[384,2048]{1,0:T(8,128)(2,1)} %vocab.1), custom_call_target="tpu_custom_call" | custom-call | flops 2147483648 | tf_op jit(solution)/shard_map/logits/pallas_call | solution.py:650
  174.9 8.9 %all-to-all-done.4.shares = bf16[32,48,128]{2,1,0:T(8,128)(2,1)S(1)} async-done(((bf16[32,48,128]{2,1,0:T(8,128)(2,1)}), bf16[32,48,128]{2,1,0:T(8,128)(2,1)S(1)}, u32[]{:S(2)}, u32[]{:S(2)}) %all-to-all-start.4) | async-done | bytes 393248 | tf_op jit(solution)/shard_map/all_to_all | solution.py:452
  183.9 0.8 last.1
  (70 shorter events, 5.2 us)
Async XLA Ops:
  0.6 17.1 %copy-start.13 = (s32[2]{0:T(128)S(1)}, s32[2]{0:T(128)}, u32[]{:S(2)}) copy-start(s32[2]{0:T(128)} %param.19) | copy-start | bytes 28
  0.7 17.2 %copy-start.12 = (s32[2,64]{1,0:T(2,128)S(1)}, s32[2,64]{1,0:T(2,128)}, u32[]{:S(2)}) copy-start(s32[2,64]{1,0:T(2,128)} %param.20) | copy-start | bytes 1540
  0.7 17.5 %copy-start.11 = (s32[2,48]{1,0:T(2,128)S(1)}, s32[2,48]{1,0:T(2,128)}, u32[]{:S(2)}) copy-start(s32[2,48]{1,0:T(2,128)} %param.18) | copy-start | bytes 1156
  0.7 19.0 %copy-start.8 = (bf16[4,2048]{1,0:T(4,128)(2,1)S(1)}, bf16[4,2048]{1,0:T(4,128)(2,1)}, u32[]{:S(2)}) copy-start(bf16[4,2048]{1,0:T(4,128)(2,1)} %param.24) | copy-start | bytes 49156
  0.7 20.6 %copy-start.7 = (bf16[2048,64]{0,1:T(8,128)(2,1)S(1)}, bf16[2048,64]{0,1:T(8,128)(2,1)}, u32[]{:S(2)}) copy-start(bf16[2048,64]{0,1:T(8,128)(2,1)} %param.25) | copy-start | bytes 786436
  4.9 27.4 %all-to-all-start = ((bf16[32,56,128]{2,1,0:T(8,128)(2,1)}), bf16[32,56,128]{2,1,0:T(8,128)(2,1)S(1)}, u32[]{:S(2)}, u32[]{:S(2)}) async-start(bf16[32,56,128]{2,1,0:T(8,128)(2,1)} %get-tuple-element.23), calls=%async_computation | async-start | bytes 917504 | tf_op jit(solution)/shard_map/all_to_all | solution.py:452
  16.1 30.6 %collective-permute-start = (bf16[48,128]{1,0:T(8,128)(2,1)}, bf16[48,128]{1,0:T(8,128)(2,1)S(1)}, u32[]{:S(2)}, u32[]{:S(2)}) collective-permute-start(bf16[48,128]{1,0:T(8,128)(2,1)} %get-tuple-element.26.own_key), channel_id=1, source_target_pairs={{0,1},{1,0},{2,3},{3,2},{4,5},{5,4},{6,7},{7,6},{8,9},{9,8},{10,11... | collective-permute-start | bytes 36872 | tf_op jit(solution)/shard_map/ppermute | solution.py:512
  19.2 20.4 %copy-start.9 = (f32[2,48]{1,0:T(2,128)}, f32[2,48]{1,0:T(2,128)S(1)}, u32[]{:S(2)}) copy-start(f32[2,48]{1,0:T(2,128)S(1)} %get-tuple-element.53.depth) | copy-start | bytes 1156
  21.2 18.4 %copy-start.3 = (f32[48,128]{1,0:T(8,128)}, f32[48,128]{1,0:T(8,128)S(1)}, u32[]{:S(2)}) copy-start(f32[48,128]{1,0:T(8,128)S(1)} %get-tuple-element.49.sine) | copy-start | bytes 73732
  21.2 18.4 %copy-start.4 = (f32[48,128]{1,0:T(8,128)}, f32[48,128]{1,0:T(8,128)S(1)}, u32[]{:S(2)}) copy-start(f32[48,128]{1,0:T(8,128)S(1)} %get-tuple-element.50.cosine) | copy-start | bytes 73732
  39.6 0.8 copy-start.5
  40.4 6.3 %copy-start.6 = (f32[8,128]{1,0:T(8,128)}, f32[8,128]{1,0:T(8,128)S(1)}, u32[]{:S(2)}) copy-start(f32[8,128]{1,0:T(8,128)S(1)} %get-tuple-element.28.key_square) | copy-start | bytes 12292
  40.4 4.9 %collective-permute-start.1 = (bf16[8,2048]{1,0:T(8,128)(2,1)S(1)}, bf16[8,2048]{1,0:T(8,128)(2,1)S(1)}, u32[]{:S(2)}, u32[]{:S(2)}) collective-permute-start(bf16[8,2048]{1,0:T(8,128)(2,1)S(1)} %get-tuple-element.31), channel_id=1, source_target_pairs={{0,32},{32,0},{1,33},{33,1},{2,34},{34,2},{3,35},{35,3},{4,36},{36... | collective-permute-start | bytes 98312 | tf_op jit(solution)/shard_map/ppermute | solution.py:553
  40.4 80.5 %all-to-all-start.1 = ((bf16[32,56,128]{2,1,0:T(8,128)(2,1)}), bf16[32,56,128]{2,1,0:T(8,128)(2,1)S(1)}, u32[]{:S(2)}, u32[]{:S(2)}) async-start(bf16[32,56,128]{2,1,0:T(8,128)(2,1)} %get-tuple-element.24), calls=%async_computation.1 | async-start | bytes 917504 | tf_op jit(solution)/shard_map/all_to_all | solution.py:452
  45.3 71.4 %collective-permute-start.2 = (bf16[16,2048]{1,0:T(8,128)(2,1)S(1)}, bf16[16,2048]{1,0:T(8,128)(2,1)S(1)}, u32[]{:S(2)}, u32[]{:S(2)}) collective-permute-start(bf16[16,2048]{1,0:T(8,128)(2,1)S(1)} %get-tuple-element.43), channel_id=1, source_target_pairs={{0,64},{64,128},{128,192},{192,0},{1,65},{65,129},{129,193},{193,1... | collective-permute-start | bytes 196616 | tf_op jit(solution)/shard_map/ppermute | solution.py:557
  46.7 0.6 copy-start.14
  113.6 50.3 %copy-start.1 = (bf16[96,2048]{1,0:T(8,128)(2,1)S(1)}, bf16[96,2048]{1,0:T(8,128)(2,1)}, u32[]{:S(2)}) copy-start(bf16[96,2048]{1,0:T(8,128)(2,1)} %inputs.3) | copy-start | bytes 1179652
  115.1 5.8 %collective-permute-start.3 = (bf16[16,2048]{1,0:T(8,128)(2,1)S(1)}, bf16[16,2048]{1,0:T(8,128)(2,1)S(1)}, u32[]{:S(2)}, u32[]{:S(2)}) collective-permute-start(bf16[16,2048]{1,0:T(8,128)(2,1)S(1)} %get-tuple-element.43), channel_id=1, source_target_pairs={{0,128},{64,192},{128,0},{192,64},{1,129},{65,193},{129,1},{193,65... | collective-permute-start | bytes 196616 | tf_op jit(solution)/shard_map/ppermute | solution.py:557
  115.7 5.2 %collective-permute-start.4 = (bf16[16,2048]{1,0:T(8,128)(2,1)S(1)}, bf16[16,2048]{1,0:T(8,128)(2,1)S(1)}, u32[]{:S(2)}, u32[]{:S(2)}) collective-permute-start(bf16[16,2048]{1,0:T(8,128)(2,1)S(1)} %get-tuple-element.43), channel_id=1, source_target_pairs={{0,192},{64,0},{128,64},{192,128},{1,193},{65,1},{129,65},{193,129... | collective-permute-start | bytes 196616 | tf_op jit(solution)/shard_map/ppermute | solution.py:557
  120.9 43.6 %copy-start.10 = (bf16[64,2048]{1,0:T(8,128)(2,1)}, bf16[64,2048]{1,0:T(8,128)(2,1)S(1)}, u32[]{:S(2)}) copy-start(bf16[64,2048]{1,0:T(8,128)(2,1)S(1)} %constant_dynamic-update-slice_fusion.2.drafts) | copy-start | bytes 786436
  120.9 0.8 copy-start.2
  122.5 42.1 %copy-start.15 = (bf16[2048,2,256]{2,1,0:T(2,128)(2,1)S(1)}, bf16[2048,2,256]{2,1,0:T(2,128)(2,1)}, u32[]{:S(2)}) copy-start(bf16[2048,2,256]{2,1,0:T(2,128)(2,1)} %get-tuple-element.40) | copy-start | bytes 6291460
  163.9 1.2 copy-start
  166.5 17.3 %all-to-all-start.4 = ((bf16[32,48,128]{2,1,0:T(8,128)(2,1)}), bf16[32,48,128]{2,1,0:T(8,128)(2,1)S(1)}, u32[]{:S(2)}, u32[]{:S(2)}) async-start(bf16[32,48,128]{2,1,0:T(8,128)(2,1)} %down.1), calls=%async_computation.4 | async-start | bytes 786432 | tf_op jit(solution)/shard_map/all_to_all | solution.py:452

commit v5 on v4

--- a/solution.py
+++ b/solution.py
@@ -70,28 +70,25 @@
 ):
     nodes = own_key.shape[0]
     fetches = [pltpu.make_async_copy(inputs, rows, sems.at[0])]
-    for kind in range(3):
-        fetches.append(pltpu.make_async_copy(weights.at[kind], columns.at[kind], sems.at[1 + kind]))
-    fetches.append(pltpu.make_async_copy(draft_weights, heads, sems.at[4]))
+    for place_of, kind in enumerate((0, 1, 2, 2)):
+        block = columns.at[pl.ds(place_of * HALF, HALF)]
+        fetches.append(pltpu.make_async_copy(weights.at[kind], block, sems.at[1 + place_of]))
+    fetches.append(pltpu.make_async_copy(draft_weights, heads, sems.at[5]))
     for fetch in fetches:
         fetch.start()
-    fetches[0].wait()
+    for fetch in fetches[:5]:
+        fetch.wait()
     first = in_first(nodes)
-
-    def projected(kind):
-        fetches[1 + kind].wait()
-        weight = columns[kind]
-        product = lax.dot_general(
-            rows[...],
-            jnp.concatenate([weight, weight], axis=0),
-            (((1,), (1,)), ((), ())),
-            preferred_element_type=jnp.float32,
-        )
-        return jnp.where(first, product[:nodes], product[nodes:]).astype(jnp.bfloat16)
-
-    query = projected(0)
-    key = projected(1)
+    product = lax.dot_general(
+        rows[...], columns[...], (((1,), (1,)), ((), ())), preferred_element_type=jnp.float32
+    )
+    query, key = paired(product[:nodes, :LANES], product[nodes:, :LANES])
+    key = key.astype(jnp.bfloat16)
+    query = query.astype(jnp.bfloat16)
     own_key[...] = key
+    own_value[...] = jnp.where(first, product[:nodes, LANES:], product[nodes:, LANES:]).astype(
+        jnp.bfloat16
+    )
     squares = key.astype(jnp.float32)
     squares = squares * squares
     zero = jnp.zeros_like(squares)
@@ -100,28 +97,23 @@
     right = jnp.sum(jnp.where(first, zero, squares), axis=1, keepdims=True)
     turned = columns_to_rows(jnp.where(lane == 0, left, jnp.where(lane == 1, right, zero)))
     sums = jnp.where(in_first(1), turned[0:1], pltpu.roll(turned[1:2], HALF, 1))
-    fetches[4].wait()
+    fetches[5].wait()
     states = hidden[...]
     start = pl.multiple_of(place[0] // 2 * LANES, LANES)
     own = hidden[:, pl.ds(start, LANES)].astype(jnp.float32)
     swapped = pltpu.roll(own, HALF, 1)
     here = jnp.full(own.shape, place[0] % 2, jnp.int32) == lax.broadcasted_iota(jnp.int32, own.shape, 1) // HALF
     own = jnp.where(here, own, swapped)
-    pairs = []
-    for pair in range(heads.shape[0] // LANES):
-        raw = lax.dot_general(
-            states,
-            heads[pair * LANES : (pair + 1) * LANES],
-            (((1,), (1,)), ((), ())),
-            preferred_element_type=jnp.float32,
-        )
-        pairs.append(own + raw / (1.0 + jnp.exp(-raw)))
+    raw = lax.dot_general(
+        states, heads[...], (((1,), (1,)), ((), ())), preferred_element_type=jnp.float32
+    )
+    raw = raw / (1.0 + jnp.exp(-raw))
+    pairs = [own + raw[:, side * LANES : (side + 1) * LANES] for side in range(raw.shape[1] // LANES)]
     drafted = [part[r : r + 1] for r in range(states.shape[0]) for part in pairs]
     tail = jnp.concatenate([*split_three(sums), *drafted, jnp.zeros_like(sums)], axis=0)
     chunk = jnp.concatenate([query.astype(jnp.float32), tail], axis=0).astype(jnp.bfloat16)
     for target in range(copies.shape[0]):
         copies[target] = chunk
-    own_value[...] = projected(2)
 
 
 def pages_kernel(
@@ -168,10 +160,10 @@
     sin_rows = sine[...]
     lane = lax.broadcasted_iota(jnp.int32, (2 * nodes, LANES), 1)
     stats = jnp.zeros((2 * nodes, LANES), jnp.float32)
-    for head in range(HEADS):
+
+    def scored(head):
         if head % (HEADS // groups) == 0:
             fetch(head // (HEADS // groups)).wait()
-        base = head * HEAD_DIM
         front = gathered[spot_of(2 * head)][:nodes].astype(jnp.float32)
         back = gathered[spot_of(2 * head + 1)][:nodes].astype(jnp.float32)
         front = front * inverse * gains[2 * head : 2 * head + 1]
@@ -179,10 +171,21 @@
         front, back = rotated(front, back, cos_rows, sin_rows)
         query = jnp.concatenate(paired(front, back), axis=0).astype(jnp.bfloat16)
         queries[head] = query
-        keys = kv[:, 0, :, base : base + HEAD_DIM].reshape(pages * page_len, HEAD_DIM)
-        scores = lax.dot_general(
-            query, keys, (((1,), (1,)), ((), ())), preferred_element_type=jnp.float32
-        )
+        keys = kv[:, 0, :, head * HEAD_DIM : (head + 1) * HEAD_DIM]
+        return lax.dot_general(
+            query,
+            keys.reshape(pages * page_len, HEAD_DIM),
+            (((1,), (1,)), ((), ())),
+            preferred_element_type=jnp.float32,
+        )
+
+    ahead = 3
+    waiting = [scored(head) for head in range(ahead)]
+    for head in range(HEADS):
+        scores = waiting.pop(0)
+        if head + ahead < HEADS:
+            waiting.append(scored(head + ahead))
+        base = head * HEAD_DIM
         scores = [
             scores[:, page * page_len : (page + 1) * page_len] * scale + bias[page]
             for page in range(pages)
@@ -295,10 +298,11 @@
     copy.wait()
 
 
-def merge_kernel(parts, tree, out):
+def merge_kernel(parts, tree_part, out, tree, sem):
     count = parts.shape[0]
     nodes = parts.shape[1] - 8
-    top_tree = tree[nodes : nodes + 1]
+    fetch = pltpu.make_async_copy(tree_part, tree, sem)
+    fetch.start()
     tops = []
     totals = []
     for source in range(count):
@@ -307,6 +311,8 @@
         totals.append((tail[3:4] + tail[4:5]) + tail[5:6])
     tops = jnp.concatenate(tops, axis=0)
     totals = jnp.concatenate(totals, axis=0)
+    fetch.wait()
+    top_tree = tree[nodes : nodes + 1]
     top = jnp.maximum(jnp.max(tops, axis=0, keepdims=True), top_tree)
     factors = jnp.exp(tops - top)
     factor_tree = jnp.exp(top_tree - top)
@@ -494,9 +500,9 @@
         out_specs=tuple(vmem(3)),
         scratch_shapes=[
             pltpu.VMEM((rows, model_width), bf16),
-            pltpu.VMEM((3, slab, model_width), bf16),
+            pltpu.VMEM((4 * slab, model_width), bf16),
             pltpu.VMEM((draft_count * slab, model_width), bf16),
-            pltpu.SemaphoreType.DMA((5,)),
+            pltpu.SemaphoreType.DMA((6,)),
         ],
         compiler_params=limit(60),
         cost_estimate=pl.CostEstimate(flops=2**32, bytes_accessed=0, transcendentals=0),
@@ -550,20 +556,6 @@
     )(counts, gathered, twice[0], cosine, sine, kv_cache)
     arrived = exchange(parts)
 
-    pair = lax.ppermute(drafts, "c", [(0, 1), (1, 0)])
-    both = jnp.concatenate([drafts, pair], axis=0)
-    turns = req_count // 2
-    drafted = [both] + [
-        lax.ppermute(both, "y", [(i, (i + k) % turns) for i in range(turns)])
-        for k in range(1, turns)
-    ]
-    drafted = jnp.concatenate(drafted, axis=0)
-    spot = jnp.arange(req_count * req_local, dtype=jnp.int32)
-    turn = spot // (2 * req_local)
-    side = (spot // req_local) % 2
-    holder = 2 * ((req_place // 2 - turn) % turns) + ((req_place % 2) ^ side)
-    origins = holder * req_local + spot % req_local
-
     path, tree, gate_up_copy = pl.pallas_call(
         tree_kernel,
         out_shape=(
@@ -572,9 +564,9 @@
             jax.ShapeDtypeStruct(gate_up_weight.shape, bf16),
         ),
         in_specs=[SMEM, SMEM, *vmem(10), HBM],
-        out_specs=(*vmem(2), HBM),
+        out_specs=tuple(vmem(3)),
         scratch_shapes=[pltpu.SemaphoreType.DMA],
-        compiler_params=limit(60),
+        compiler_params=limit(52),
         cost_estimate=pl.CostEstimate(flops=2**31, bytes_accessed=0, transcendentals=2**13),
         name="tree",
     )(
@@ -592,6 +584,20 @@
         node_depth,
         gate_up_weight,
     )
+    pair = lax.ppermute(drafts, "c", [(0, 1), (1, 0)])
+    both = jnp.concatenate([drafts, pair], axis=0)
+    turns = req_count // 2
+    drafted = [both] + [
+        lax.ppermute(both, "y", [(i, (i + k) % turns) for i in range(turns)])
+        for k in range(1, turns)
+    ]
+    drafted = jnp.concatenate(drafted, axis=0)
+    spot = jnp.arange(req_count * req_local, dtype=jnp.int32)
+    turn = spot // (2 * req_local)
+    side = (spot // req_local) % 2
+    holder = 2 * ((req_place // 2 - turn) % turns) + ((req_place % 2) ^ side)
+    origins = holder * req_local + spot % req_local
+
     accepted_kv = jnp.transpose(
         path[:, :draft_count].reshape(2, draft_count, req_local, slab), (2, 1, 0, 3)
     ).astype(bf16)
@@ -600,9 +606,11 @@
     attended_copies = pl.pallas_call(
         merge_kernel,
         out_shape=jax.ShapeDtypeStruct((mp_count, tree_size, LANES), bf16),
-        in_specs=vmem(2),
+        in_specs=[*vmem(1), HBM],
         out_specs=vmem(1)[0],
+        scratch_shapes=[pltpu.VMEM((tree_size + 8, LANES), f32), pltpu.SemaphoreType.DMA],
         compiler_params=limit(8),
+        cost_estimate=pl.CostEstimate(flops=2**31, bytes_accessed=0, transcendentals=0),
         name="merge",
     )(arrived, tree)
     out_gain = gain_rows[2:3]

time: 187 us -> 122 us (0.65)
  Pallas kernels: 85.5 us -> 21.1 us
  waiting for transfers between devices: 24.1 us -> 31.6 us
  local copies, waits for them, and re-layouts: 4.44 us -> 1.57 us
  blocking collectives: 40.9 us -> 38.6 us
    pallas_call x1, Pallas kernels: 66.3 us -> 3.48 us  [per_device(): pl.pallas_call(tree_kernel, out_shape=(jax.ShapeDtypeStruct((2, 8, LANES)...]
    all_to_all x3, waiting for transfers between devices: 19.9 us -> 27.5 us  [exchange(): return lax.all_to_all(chunks, TURN, 0, 0)]
    all_to_all x2, blocking collectives: 40.9 us -> 38.6 us  [exchange(): return lax.all_to_all(chunks, TURN, 0, 0)]
    unnamed x35 -> x27, local copies, waits for them, and re-layouts: 2.31 us -> 0.17 us
    pallas_call x1, Pallas kernels: 7.28 us -> 5.17 us  [per_device(): pl.pallas_call(pages_kernel, out_shape=(jax.ShapeDtypeStruct((mp_count, t...]
  transfers between devices with their start and end apart: 8 -> 8, of which waited for: 4 -> 4; matrix products, arithmetic and copies ran while one was open for 3% -> 3% of each run, Pallas kernels for 42% -> 10%
where the time goes in v5:
time: 122 us; the launch traced here: 121 us
  blocking collectives  38.6 us (32%)
  waiting for transfers between devices  31.6 us (26%)
  starting transfers between devices  25.4 us (21%)
  Pallas kernels  21.1 us (17%)
  local copies, waits for them, and re-layouts  1.57 us (1%)
    all_to_all x2, blocking collectives, exchange(): return lax.all_to_all(chunks, TURN, 0, 0)  38.6 us
    all_to_all x3, waiting for transfers between devices, exchange(): return lax.all_to_all(chunks, TURN, 0, 0)  27.5 us
    all_to_all x3, starting transfers between devices, exchange(): return lax.all_to_all(chunks, TURN, 0, 0)  20.7 us
    pallas_call x1, Pallas kernels, per_device(): pl.pallas_call(pages_kernel, out_shape=(jax.ShapeDtypeStruct((mp_count, t...  5.17 us
    pallas_call x1, Pallas kernels, per_device(): pl.pallas_call(project_kernel, out_shape=(jax.ShapeDtypeStruct((mp_count,...  4.75 us
    ppermute x3, waiting for transfers between devices, per_device(): lax.ppermute(both, 'y', [(i, (i + k) % turns) for i in range(turns)])  4.12 us
    pallas_call x1, Pallas kernels, per_device(): pl.pallas_call(logits_kernel, out_shape=jax.ShapeDtypeStruct((req_count *...  3.62 us
    pallas_call x1, Pallas kernels, per_device(): pl.pallas_call(tree_kernel, out_shape=(jax.ShapeDtypeStruct((2, 8, LANES)...  3.48 us
  transfers between devices with their start and end apart: 8, of which 4 were waited for; matrix products, arithmetic and copies ran while one was open for 3% of the time, Pallas kernels for 10%

profile of v5, /device:TPU:48, one launch (start us, length us, event | category | flops | bytes accessed | tf_op | source)
XLA Modules:
  0.0 121.4 jit_solution(17210436010768205451)
XLA Ops:
  0.7 4.8 %project.1 = (bf16[32,56,128]{2,1,0:T(8,128)(2,1)}, bf16[48,128]{1,0:T(8,128)(2,1)}, bf16[48,128]{1,0:T(8,128)(2,1)}) custom-call(s32[1]{0:T(128)} %bitcast.place, bf16[2,2048]{1,0:T(2,128)(2,1)} %hidden.1, bf16[96,2048]{1,0:T(8,128)(2,1)} %inputs.3, bf16[3,64,2048]{2,1,0:T(8,128)(2,1)} %bitcast.32, bf16[256,2048]{1,0:T(8,128)(2,1)} %bitcast.31), custom_call_target="tpu_custom_call" | custom-call | flops 4294967296 | tf_op jit(solution)/shard_map/project/pallas_call | solution.py:492
  5.4 11.2 %all-to-all-start = ((bf16[32,56,128]{2,1,0:T(8,128)(2,1)}), bf16[32,56,128]{2,1,0:T(8,128)(2,1)S(1)}, u32[]{:S(2)}, u32[]{:S(2)}) async-start(bf16[32,56,128]{2,1,0:T(8,128)(2,1)} %get-tuple-element.23), calls=%async_computation | async-start | bytes 917504 | tf_op jit(solution)/shard_map/all_to_all | solution.py:458
  16.7 1.6 %collective-permute-start = (bf16[48,128]{1,0:T(8,128)(2,1)}, bf16[48,128]{1,0:T(8,128)(2,1)S(1)}, u32[]{:S(2)}, u32[]{:S(2)}) collective-permute-start(bf16[48,128]{1,0:T(8,128)(2,1)} %get-tuple-element.26.own_key), channel_id=1, source_target_pairs={{0,1},{1,0},{2,3},{3,2},{4,5},{5,4},{6,7},{7,6},{8,9},{9,8},{10,11... | collective-permute-start | bytes 36872 | tf_op jit(solution)/shard_map/ppermute | solution.py:518
  19.9 0.5 fusion.12.origins
  20.6 12.2 %all-to-all-done.gathered = bf16[32,56,128]{2,1,0:T(8,128)(2,1)S(1)} async-done(((bf16[32,56,128]{2,1,0:T(8,128)(2,1)}), bf16[32,56,128]{2,1,0:T(8,128)(2,1)S(1)}, u32[]{:S(2)}, u32[]{:S(2)}) %all-to-all-start) | async-done | bytes 458784 | tf_op jit(solution)/shard_map/all_to_all | solution.py:458
  32.9 5.2 %pages.1 = (bf16[32,56,128]{2,1,0:T(8,128)(2,1)}, bf16[16,96,128]{2,1,0:T(8,128)(2,1)S(1)}, f32[8,128]{1,0:T(8,128)S(1)}, bf16[8,2048]{1,0:T(8,128)(2,1)S(1)}) custom-call(s32[8,1]{1,0:T(8,128)S(1)} %reshape.83.counts, bf16[32,56,128]{2,1,0:T(8,128)(2,1)S(1)} %all-to-all-done.gathered, f32[32,128]{1,0:T(8,128)S(1)} %get-tuple-element.48.gains, ...), custom_call_target="tpu_custom_call" | custom-call | flops 8589934592 | tf_op jit(solution)/shard_map/pages/pallas_call | solution.py:538
  38.2 4.9 %all-to-all-start.1 = ((bf16[32,56,128]{2,1,0:T(8,128)(2,1)}), bf16[32,56,128]{2,1,0:T(8,128)(2,1)S(1)}, u32[]{:S(2)}, u32[]{:S(2)}) async-start(bf16[32,56,128]{2,1,0:T(8,128)(2,1)} %get-tuple-element.24), calls=%async_computation.1 | async-start | bytes 917504 | tf_op jit(solution)/shard_map/all_to_all | solution.py:458
  43.1 1.4 %collective-permute-start.2 = (bf16[16,2048]{1,0:T(8,128)(2,1)S(1)}, bf16[16,2048]{1,0:T(8,128)(2,1)S(1)}, u32[]{:S(2)}, u32[]{:S(2)}) collective-permute-start(bf16[16,2048]{1,0:T(8,128)(2,1)S(1)} %get-tuple-element.43), channel_id=1, source_target_pairs={{0,64},{64,128},{128,192},{192,0},{1,65},{65,129},{129,193},{193,1... | collective-permute-start | bytes 196616 | tf_op jit(solution)/shard_map/ppermute | solution.py:591
  44.5 3.5 %tree.1 = (f32[2,8,128]{2,1,0:T(8,128)S(1)}, f32[56,128]{1,0:T(8,128)S(1)}, bf16[2048,2,256]{2,1,0:T(2,128)(2,1)}) custom-call(s32[1]{0:T(128)} %bitcast.place, s32[2]{0:T(128)S(1)} %copy-done.3, bf16[16,96,128]{2,1,0:T(8,128)(2,1)S(1)} %get-tuple-element.25.queries, bf16[48,128]{1,0:T(8,128)(2,1)S(1)} %copy-done.2, ...), custom_call_target="tpu_custom_call" | custom-call | flops 2147483648 | tf_op jit(solution)/shard_map/tree/pallas_call | solution.py:559
  48.0 0.6 copy.52
  48.6 0.6 collective-permute-start.3
  49.3 1.1 collective-permute-start.4
  50.3 4.1 %collective-permute-done.3 = bf16[16,2048]{1,0:T(8,128)(2,1)S(1)} collective-permute-done((bf16[16,2048]{1,0:T(8,128)(2,1)S(1)}, bf16[16,2048]{1,0:T(8,128)(2,1)S(1)}, u32[]{:S(2)}, u32[]{:S(2)}) %collective-permute-start.3) | collective-permute-done | bytes 65568 | tf_op jit(solution)/shard_map/ppermute | solution.py:591
  54.5 5.4 %all-to-all-done.1.parts = bf16[32,56,128]{2,1,0:T(8,128)(2,1)S(1)} async-done(((bf16[32,56,128]{2,1,0:T(8,128)(2,1)}), bf16[32,56,128]{2,1,0:T(8,128)(2,1)S(1)}, u32[]{:S(2)}, u32[]{:S(2)}) %all-to-all-start.1) | async-done | bytes 458784 | tf_op jit(solution)/shard_map/all_to_all | solution.py:458
  59.9 0.8 merge.1
  60.7 19.6 %all_to_all.25.gathered = bf16[32,48,128]{2,1,0:T(8,128)(2,1)S(1)} all-to-all(bf16[32,48,128]{2,1,0:T(8,128)(2,1)S(1)} %merge.1), channel_id=1, replica_groups=mesh['y'=4,'c'=2,'z'=8,'x'=4] {'x','z'}, dimensions={0} | all-to-all | bytes 786432 | tf_op jit(solution)/shard_map/all_to_all | solution.py:458
  80.3 0.5 out_columns.1
  80.9 19.0 %all_to_all.26.gathered = bf16[32,48,128]{2,1,0:T(8,128)(2,1)S(1)} all-to-all(bf16[32,48,128]{2,1,0:T(8,128)(2,1)S(1)} %out_columns.1), channel_id=1, replica_groups=mesh['y'=4,'c'=2,'z'=8,'x'=4] {'x','z'}, dimensions={0} | all-to-all | bytes 786432 | tf_op jit(solution)/shard_map/all_to_all | solution.py:458
  99.8 0.6 residual.1
  101.0 1.4 %down.1 = bf16[32,48,128]{2,1,0:T(8,128)(2,1)} custom-call(bf16[96,256]{1,0:T(8,128)(2,1)S(1)} %fusion.4.hidden, bf16[256,2048]{1,0:T(8,128)(2,1)S(1)} %copy-done), custom_call_target="tpu_custom_call" | custom-call | tf_op jit(solution)/shard_map/down/pallas_call | solution.py:647
  102.4 4.6 %all-to-all-start.4 = ((bf16[32,48,128]{2,1,0:T(8,128)(2,1)}), bf16[32,48,128]{2,1,0:T(8,128)(2,1)S(1)}, u32[]{:S(2)}, u32[]{:S(2)}) async-start(bf16[32,48,128]{2,1,0:T(8,128)(2,1)} %down.1), calls=%async_computation.4 | async-start | bytes 786432 | tf_op jit(solution)/shard_map/all_to_all | solution.py:458
  107.1 3.6 %logits.1 = f32[16,4,384]{2,1,0:T(4,128)} custom-call(s32[16]{0:T(128)} %fusion.12.origins, bf16[64,2048]{1,0:T(8,128)(2,1)} %copy-done.7, bf16[384,2048]{1,0:T(8,128)(2,1)} %vocab.1), custom_call_target="tpu_custom_call" | custom-call | flops 2147483648 | tf_op jit(solution)/shard_map/logits/pallas_call | solution.py:658
  110.7 9.9 %all-to-all-done.4.shares = bf16[32,48,128]{2,1,0:T(8,128)(2,1)S(1)} async-done(((bf16[32,48,128]{2,1,0:T(8,128)(2,1)}), bf16[32,48,128]{2,1,0:T(8,128)(2,1)S(1)}, u32[]{:S(2)}, u32[]{:S(2)}) %all-to-all-start.4) | async-done | bytes 393248 | tf_op jit(solution)/shard_map/all_to_all | solution.py:458
  120.6 0.8 last.1
  (62 shorter events, 2.7 us)
Async XLA Ops:
  0.6 17.6 %copy-start.10 = (s32[2]{0:T(128)S(1)}, s32[2]{0:T(128)}, u32[]{:S(2)}) copy-start(s32[2]{0:T(128)} %param.19) | copy-start | bytes 28
  0.7 17.7 %copy-start.9 = (s32[2,64]{1,0:T(2,128)S(1)}, s32[2,64]{1,0:T(2,128)}, u32[]{:S(2)}) copy-start(s32[2,64]{1,0:T(2,128)} %param.20) | copy-start | bytes 1540
  0.7 18.1 %copy-start.8 = (s32[2,48]{1,0:T(2,128)S(1)}, s32[2,48]{1,0:T(2,128)}, u32[]{:S(2)}) copy-start(s32[2,48]{1,0:T(2,128)} %param.18) | copy-start | bytes 1156
  0.7 19.1 %copy-start.6 = (bf16[4,2048]{1,0:T(4,128)(2,1)S(1)}, bf16[4,2048]{1,0:T(4,128)(2,1)}, u32[]{:S(2)}) copy-start(bf16[4,2048]{1,0:T(4,128)(2,1)} %param.24) | copy-start | bytes 49156
  0.7 19.9 %copy-start.5 = (bf16[2048,64]{0,1:T(8,128)(2,1)S(1)}, bf16[2048,64]{0,1:T(8,128)(2,1)}, u32[]{:S(2)}) copy-start(bf16[2048,64]{0,1:T(8,128)(2,1)} %param.25) | copy-start | bytes 786436
  5.4 27.4 %all-to-all-start = ((bf16[32,56,128]{2,1,0:T(8,128)(2,1)}), bf16[32,56,128]{2,1,0:T(8,128)(2,1)S(1)}, u32[]{:S(2)}, u32[]{:S(2)}) async-start(bf16[32,56,128]{2,1,0:T(8,128)(2,1)} %get-tuple-element.23), calls=%async_computation | async-start | bytes 917504 | tf_op jit(solution)/shard_map/all_to_all | solution.py:458
  16.7 27.8 %collective-permute-start = (bf16[48,128]{1,0:T(8,128)(2,1)}, bf16[48,128]{1,0:T(8,128)(2,1)S(1)}, u32[]{:S(2)}, u32[]{:S(2)}) collective-permute-start(bf16[48,128]{1,0:T(8,128)(2,1)} %get-tuple-element.26.own_key), channel_id=1, source_target_pairs={{0,1},{1,0},{2,3},{3,2},{4,5},{5,4},{6,7},{7,6},{8,9},{9,8},{10,11... | collective-permute-start | bytes 36872 | tf_op jit(solution)/shard_map/ppermute | solution.py:518
  32.9 11.6 %copy-start.2 = (bf16[48,128]{1,0:T(8,128)(2,1)S(1)}, bf16[48,128]{1,0:T(8,128)(2,1)}, u32[]{:S(2)}) copy-start(bf16[48,128]{1,0:T(8,128)(2,1)} %get-tuple-element.26.own_key) | copy-start | bytes 36868
  32.9 11.6 %copy-start.3 = (s32[2]{0:T(128)S(1)}, s32[2]{0:T(128)}, u32[]{:S(2)}) copy-start(s32[2]{0:T(128)} %accepted.1) | copy-start | bytes 28
  32.9 11.6 %copy-start.4 = (bf16[48,128]{1,0:T(8,128)(2,1)S(1)}, bf16[48,128]{1,0:T(8,128)(2,1)}, u32[]{:S(2)}) copy-start(bf16[48,128]{1,0:T(8,128)(2,1)} %get-tuple-element.27.own_value) | copy-start | bytes 36868
  38.0 5.0 %collective-permute-start.1 = (bf16[8,2048]{1,0:T(8,128)(2,1)S(1)}, bf16[8,2048]{1,0:T(8,128)(2,1)S(1)}, u32[]{:S(2)}, u32[]{:S(2)}) collective-permute-start(bf16[8,2048]{1,0:T(8,128)(2,1)S(1)} %get-tuple-element.31), channel_id=1, source_target_pairs={{0,32},{32,0},{1,33},{33,1},{2,34},{34,2},{3,35},{35,3},{4,36},{36... | collective-permute-start | bytes 98312 | tf_op jit(solution)/shard_map/ppermute | solution.py:587
  38.2 21.7 %all-to-all-start.1 = ((bf16[32,56,128]{2,1,0:T(8,128)(2,1)}), bf16[32,56,128]{2,1,0:T(8,128)(2,1)S(1)}, u32[]{:S(2)}, u32[]{:S(2)}) async-start(bf16[32,56,128]{2,1,0:T(8,128)(2,1)} %get-tuple-element.24), calls=%async_computation.1 | async-start | bytes 917504 | tf_op jit(solution)/shard_map/all_to_all | solution.py:458
  43.1 7.2 %collective-permute-start.2 = (bf16[16,2048]{1,0:T(8,128)(2,1)S(1)}, bf16[16,2048]{1,0:T(8,128)(2,1)S(1)}, u32[]{:S(2)}, u32[]{:S(2)}) collective-permute-start(bf16[16,2048]{1,0:T(8,128)(2,1)S(1)} %get-tuple-element.43), channel_id=1, source_target_pairs={{0,64},{64,128},{128,192},{192,0},{1,65},{65,129},{129,193},{193,1... | collective-permute-start | bytes 196616 | tf_op jit(solution)/shard_map/ppermute | solution.py:591
  48.6 5.8 %collective-permute-start.3 = (bf16[16,2048]{1,0:T(8,128)(2,1)S(1)}, bf16[16,2048]{1,0:T(8,128)(2,1)S(1)}, u32[]{:S(2)}, u32[]{:S(2)}) collective-permute-start(bf16[16,2048]{1,0:T(8,128)(2,1)S(1)} %get-tuple-element.43), channel_id=1, source_target_pairs={{0,128},{64,192},{128,0},{192,64},{1,129},{65,193},{129,1},{193,65... | collective-permute-start | bytes 196616 | tf_op jit(solution)/shard_map/ppermute | solution.py:591
  49.3 5.2 %collective-permute-start.4 = (bf16[16,2048]{1,0:T(8,128)(2,1)S(1)}, bf16[16,2048]{1,0:T(8,128)(2,1)S(1)}, u32[]{:S(2)}, u32[]{:S(2)}) collective-permute-start(bf16[16,2048]{1,0:T(8,128)(2,1)S(1)} %get-tuple-element.43), channel_id=1, source_target_pairs={{0,192},{64,0},{128,64},{192,128},{1,193},{65,1},{129,65},{193,129... | collective-permute-start | bytes 196616 | tf_op jit(solution)/shard_map/ppermute | solution.py:591
  54.5 6.2 %copy-start.7 = (bf16[64,2048]{1,0:T(8,128)(2,1)}, bf16[64,2048]{1,0:T(8,128)(2,1)S(1)}, u32[]{:S(2)}) copy-start(bf16[64,2048]{1,0:T(8,128)(2,1)S(1)} %constant_dynamic-update-slice_fusion.2.drafts) | copy-start | bytes 786436
  60.7 39.2 %copy-start.1 = (bf16[96,2048]{1,0:T(8,128)(2,1)S(1)}, bf16[96,2048]{1,0:T(8,128)(2,1)}, u32[]{:S(2)}) copy-start(bf16[96,2048]{1,0:T(8,128)(2,1)} %inputs.3) | copy-start | bytes 1179652
  60.7 39.7 %copy-start.11 = (bf16[2048,2,256]{2,1,0:T(2,128)(2,1)S(1)}, bf16[2048,2,256]{2,1,0:T(2,128)(2,1)}, u32[]{:S(2)}) copy-start(bf16[2048,2,256]{2,1,0:T(2,128)(2,1)} %get-tuple-element.40) | copy-start | bytes 6291460
  99.8 1.2 %copy-start = (bf16[256,2048]{1,0:T(8,128)(2,1)S(1)}, bf16[256,2048]{1,0:T(8,128)(2,1)}, u32[]{:S(2)}) copy-start(bf16[256,2048]{1,0:T(8,128)(2,1)} %weight.1) | copy-start | bytes 3145732
  102.4 18.2 %all-to-all-start.4 = ((bf16[32,48,128]{2,1,0:T(8,128)(2,1)}), bf16[32,48,128]{2,1,0:T(8,128)(2,1)S(1)}, u32[]{:S(2)}, u32[]{:S(2)}) async-start(bf16[32,48,128]{2,1,0:T(8,128)(2,1)} %down.1), calls=%async_computation.4 | async-start | bytes 786432 | tf_op jit(solution)/shard_map/all_to_all | solution.py:458

commit v6 on v5

--- a/solution.py
+++ b/solution.py
@@ -80,8 +80,8 @@
         fetch.wait()
     first = in_first(nodes)
     product = lax.dot_general(
-        rows[...], columns[...], (((1,), (1,)), ((), ())), preferred_element_type=jnp.float32
-    )
+        columns[...], rows[...], (((1,), (1,)), ((), ())), preferred_element_type=jnp.float32
+    ).T
     query, key = paired(product[:nodes, :LANES], product[nodes:, :LANES])
     key = key.astype(jnp.bfloat16)
     query = query.astype(jnp.bfloat16)
@@ -105,8 +105,8 @@
     here = jnp.full(own.shape, place[0] % 2, jnp.int32) == lax.broadcasted_iota(jnp.int32, own.shape, 1) // HALF
     own = jnp.where(here, own, swapped)
     raw = lax.dot_general(
-        states, heads[...], (((1,), (1,)), ((), ())), preferred_element_type=jnp.float32
-    )
+        heads[...], states, (((1,), (1,)), ((), ())), preferred_element_type=jnp.float32
+    ).T
     raw = raw / (1.0 + jnp.exp(-raw))
     pairs = [own + raw[:, side * LANES : (side + 1) * LANES] for side in range(raw.shape[1] // LANES)]
     drafted = [part[r : r + 1] for r in range(states.shape[0]) for part in pairs]
@@ -116,8 +116,71 @@
         copies[target] = chunk
 
 
+def tree_part(place, query, own_key, other_key, own_value, sums, gains, cosine, sine, ancestry):
+    requests, nodes, _ = ancestry.shape
+    width = 2 * HEADS * HALF
+    head = place[0] // 2
+    parity = jnp.full((nodes, LANES), place[0] % 2, jnp.int32)
+    even = parity == 0
+    side = lax.broadcasted_iota(jnp.int32, (nodes, LANES), 1) // HALF
+    first = in_first(nodes)
+    square = jnp.broadcast_to(sums, (LANES, LANES)).T
+    square = jnp.where(first, square[:nodes], square[HALF : HALF + nodes])
+    inverse = lax.rsqrt(square / width + norm_epsilon)
+    own = own_key[...].astype(jnp.float32)
+    other = other_key[...].astype(jnp.float32)
+    front = jnp.where(even, own, other) * inverse * gains[pl.ds(2 * head, 1)]
+    back = jnp.where(even, other, own) * inverse * gains[pl.ds(2 * head + 1, 1)]
+    front, back = rotated(front, back, cosine[...], sine[...])
+    kept = jnp.where(even, front, back).astype(jnp.bfloat16)
+    keys = paired(front, back)
+    value = own_value[...]
+    tops, totals, mixed = [], [], []
+    for request in range(requests):
+        scores = lax.dot_general(
+            query[request * nodes : (request + 1) * nodes],
+            keys[request].astype(jnp.bfloat16),
+            (((1,), (1,)), ((), ())),
+            preferred_element_type=jnp.float32,
+        ) * (HEAD_DIM ** (-0.5))
+        visible = ancestry[request] > 0.5
+        scores = jnp.where(visible, scores, masked_score)
+        top = jnp.max(scores, axis=1, keepdims=True)
+        weights = jnp.where(visible, jnp.exp(scores - top), 0.0)
+        tops.append(top)
+        totals.append(jnp.sum(weights, axis=1, keepdims=True))
+        found = jnp.dot(weights.astype(jnp.bfloat16), value, preferred_element_type=jnp.float32)
+        turned = pltpu.roll(found, HALF, 1)
+        lined = jnp.where(parity == request, found, turned)
+        mixed.append(jnp.where(side == parity, lined, 0.0))
+    return (
+        jnp.concatenate(tops, axis=0),
+        jnp.concatenate(totals, axis=0),
+        jnp.concatenate(mixed, axis=0),
+        kept,
+    )
+
+
 def pages_kernel(
-    counts, gathered, gains, cosine, sine, cache, out, queries, key_square, drafts, kv, held, sems
+    place,
+    counts,
+    gathered,
+    gains,
+    key_gains,
+    cosine,
+    sine,
+    own_key,
+    other_key,
+    own_value,
+    ancestry,
+    cache,
+    out,
+    drafts,
+    kept_out,
+    kv,
+    held,
+    queries,
+    sems,
 ):
     pages, _, page_len, width = cache.shape
     nodes = cosine.shape[0]
@@ -139,7 +202,7 @@
         squares = squares + chunk[:nodes] * chunk[:nodes]
         extra = extra + chunk[nodes : nodes + 8]
     inverse = packed_inverse(squares, width)
-    key_square[...] = extra
+    sums = (extra[0:1] + extra[1:2]) + extra[2:3]
     for head in range(HEADS):
         tails = [gathered[spot_of(2 * head + side)].astype(jnp.float32)[nodes:] for side in range(2)]
         even, odd = paired(*tails)
@@ -160,6 +223,9 @@
     sin_rows = sine[...]
     lane = lax.broadcasted_iota(jnp.int32, (2 * nodes, LANES), 1)
     stats = jnp.zeros((2 * nodes, LANES), jnp.float32)
+    count = out.shape[0]
+    share = 2 * nodes // count
+    chunk_rows = share * HEADS
 
     def scored(head):
         if head % (HEADS // groups) == 0:
@@ -201,181 +267,158 @@
         )
         stats = jnp.where(lane == head, top, stats)
         stats = jnp.where(lane == HEADS + head, total, stats)
-        left, right = paired(mixed[:nodes], mixed[nodes:])
-        held[2 * head] = left
-        held[2 * head + 1] = right
-    turned = columns_to_rows(stats)
-    shifted = pltpu.roll(turned, HALF - nodes, 1)
-    turned = jnp.where(in_first(LANES), turned, shifted)
-    rows = [*split_three(turned[:HEADS]), *split_three(turned[HEADS : 2 * HEADS])]
+        for row in range(share):
+            held[pl.ds(row * HEADS + head, count, stride=chunk_rows), :] = mixed[
+                row * count : (row + 1) * count
+            ]
+    own_head = place[0] // 2
+    tree_top, tree_total, tree_mixed, kept = tree_part(
+        place, queries[own_head], own_key, other_key, own_value, sums, key_gains, cosine, sine, ancestry
+    )
+    kept_out[...] = kept
+    is_top = lane == own_head
+    is_total = lane == HEADS + own_head
+    top = jnp.sum(jnp.where(is_top, stats, 0.0), axis=1, keepdims=True)
+    total = jnp.sum(jnp.where(is_total, stats, 0.0), axis=1, keepdims=True)
+    both_top = jnp.maximum(top, tree_top)
+    page_factor = jnp.exp(top - both_top)
+    tree_factor = jnp.exp(tree_top - both_top)
+    adds = (1 - place[0] % 2).astype(jnp.float32)
+    stats = jnp.where(is_top, both_top, stats)
+    stats = jnp.where(is_total, total * page_factor + tree_total * tree_factor * adds, stats)
+    tree_mixed = tree_mixed * tree_factor
+    for row in range(share):
+        spot = pl.ds(row * HEADS + own_head, count, stride=chunk_rows)
+        lines = slice(row * count, (row + 1) * count)
+        held[spot, :] = held[spot, :] * page_factor[lines] + tree_mixed[lines]
+    spread = lax.broadcasted_iota(jnp.int32, (count, LANES), 1) // HEADS
+
+    def by_device(kind):
+        found = jnp.zeros((count, LANES), jnp.float32)
+        for row in range(share):
+            turned = pltpu.roll(
+                stats[row * count : (row + 1) * count], (row - kind) * HEADS % LANES, 1
+            )
+            found = jnp.where(spread == row, turned, found)
+        return found
+
+    rows = [*split_three(by_device(0)), *split_three(by_device(1))]
     rows += [jnp.zeros_like(rows[0])] * 2
-    for head in range(HEADS):
-        tail = jnp.concatenate([row[head : head + 1] for row in rows], axis=0)
-        for half in range(2):
-            block = jnp.concatenate([held[2 * head + half], tail], axis=0)
-            out[spot_of(2 * head + half)] = block.astype(jnp.bfloat16)
-
-
-def tree_kernel(
-    place,
-    accepted,
-    queries,
-    own_key,
-    other_key,
-    own_value,
-    key_square,
-    gains,
-    cosine,
-    sine,
-    ancestry,
-    depth,
-    large,
-    path_out,
-    tree_out,
-    large_out,
-    sem,
-):
-    copy = pltpu.make_async_copy(large, large_out, sem)
-    copy.start()
-    width = 2 * HEADS * HALF
+    for target in range(count):
+        tail = jnp.concatenate([row[target : target + 1] for row in rows], axis=0)
+        block = jnp.concatenate(
+            [held[target * chunk_rows : (target + 1) * chunk_rows], tail], axis=0
+        )
+        out[target] = block.astype(jnp.bfloat16)
+
+
+def path_kernel(accepted, kept, own_value, ancestry, depth, out):
     requests, nodes, _ = ancestry.shape
-    head = place[0] // 2
-    even = jnp.full((nodes, LANES), place[0] % 2, jnp.int32) == 0
-    first = in_first(nodes)
-    sums = (key_square[0:1] + key_square[1:2]) + key_square[2:3]
-    square = jnp.broadcast_to(sums, (LANES, LANES)).T
-    square = jnp.where(first, square[:nodes], square[HALF : HALF + nodes])
-    inverse = lax.rsqrt(square / width + norm_epsilon)
-    own = own_key[...].astype(jnp.float32)
-    other = other_key[...].astype(jnp.float32)
-    front = jnp.where(even, own, other) * inverse * gains[pl.ds(2 * head, 1)]
-    back = jnp.where(even, other, own) * inverse * gains[pl.ds(2 * head + 1, 1)]
-    front, back = rotated(front, back, cosine[...], sine[...])
-    kept = jnp.where(even, front, back).astype(jnp.bfloat16)
-    keys = paired(front, back)
-    value = own_value[...]
-    query = queries[head]
-    lane = lax.broadcasted_iota(jnp.int32, (nodes, LANES), 1)
-    stats = jnp.zeros((nodes, LANES), jnp.float32)
-    mixed = []
     pickers = []
     for request in range(requests):
-        line = ancestry[request]
-        scores = lax.dot_general(
-            query[request * nodes : (request + 1) * nodes],
-            keys[request].astype(jnp.bfloat16),
-            (((1,), (1,)), ((), ())),
-            preferred_element_type=jnp.float32,
-        ) * (HEAD_DIM ** (-0.5))
-        visible = line > 0.5
-        scores = jnp.where(visible, scores, masked_score)
-        top = jnp.max(scores, axis=1, keepdims=True)
-        weights = jnp.where(visible, jnp.exp(scores - top), 0.0)
-        total = jnp.sum(weights, axis=1, keepdims=True)
-        mixed.append(jnp.dot(weights.astype(jnp.bfloat16), value, preferred_element_type=jnp.float32))
-        stats = jnp.where(lane == request, top, stats)
-        stats = jnp.where(lane == request + 2, total, stats)
         on_path = ancestry[request, pl.ds(accepted[request], 1), :]
         levels = depth[pl.ds(request, 1), :]
         wanted = (lax.broadcasted_iota(jnp.int32, (8, nodes), 0) + 1).astype(jnp.float32)
-        picker = jnp.where(wanted == levels, on_path, 0.0).astype(jnp.bfloat16)
-        pickers.append(picker)
-    turned = columns_to_rows(stats)
-    row = in_first(1)
-    tail = [
-        jnp.where(row, turned[0:1], pltpu.roll(turned[1:2], HALF, 1)),
-        jnp.where(row, turned[2:3], pltpu.roll(turned[3:4], HALF, 1)),
-        jnp.zeros((6, LANES), jnp.float32),
-    ]
-    tree_out[...] = jnp.concatenate(
-        [jnp.where(first, mixed[0], mixed[1]), *tail], axis=0
-    )
-    for kind, block in enumerate((kept, value)):
+        pickers.append(jnp.where(wanted == levels, on_path, 0.0).astype(jnp.bfloat16))
+    for kind, block in enumerate((kept[...], own_value[...])):
         picked = [
             jnp.dot(picker, block, preferred_element_type=jnp.float32) for picker in pickers
         ]
-        path_out[kind] = jnp.where(in_first(8), picked[0], picked[1])
+        out[kind] = jnp.where(in_first(8), picked[0], picked[1])
+
+
+def order_kernel(side, own, *rest):
+    *others, out = rest
+    for turn, block in enumerate((own, *others)):
+        out[pl.ds((side[0] + SIDE - turn) % SIDE, 1)] = block[...][None]
+
+
+def held_kernel(large, out, sem):
+    copy = pltpu.make_async_copy(large, out, sem)
+    copy.start()
     copy.wait()
 
 
-def merge_kernel(parts, tree_part, out, tree, sem):
+def merge_kernel(parts, out):
     count = parts.shape[0]
-    nodes = parts.shape[1] - 8
-    fetch = pltpu.make_async_copy(tree_part, tree, sem)
-    fetch.start()
+    rows = parts.shape[1] - 8
     tops = []
     totals = []
     for source in range(count):
-        tail = parts[source].astype(jnp.float32)[nodes : nodes + 8]
+        tail = parts[source].astype(jnp.float32)[rows:]
         tops.append((tail[0:1] + tail[1:2]) + tail[2:3])
         totals.append((tail[3:4] + tail[4:5]) + tail[5:6])
     tops = jnp.concatenate(tops, axis=0)
     totals = jnp.concatenate(totals, axis=0)
-    fetch.wait()
-    top_tree = tree[nodes : nodes + 1]
-    top = jnp.maximum(jnp.max(tops, axis=0, keepdims=True), top_tree)
-    factors = jnp.exp(tops - top)
-    factor_tree = jnp.exp(top_tree - top)
-    total = jnp.sum(factors * totals, axis=0, keepdims=True) + factor_tree * tree[nodes + 1 : nodes + 2]
-    shares = jnp.concatenate([factors / total, factor_tree / total], axis=0)
+    factors = jnp.exp(tops - jnp.max(tops, axis=0, keepdims=True))
+    shares = factors / jnp.sum(factors * totals, axis=0, keepdims=True)
     turned = columns_to_rows(shares)
-    first = in_first(nodes)
-
-    def spread(source):
-        return jnp.where(
-            first,
-            turned[0:nodes, source : source + 1],
-            turned[HALF : HALF + nodes, source : source + 1],
-        )
-
-    mixed = spread(count) * tree[:nodes]
+    mixed = jnp.zeros((rows, LANES), jnp.float32)
     for source in range(count):
-        mixed = mixed + spread(source) * parts[source].astype(jnp.float32)[:nodes]
+        mixed = mixed + turned[:rows, source : source + 1] * parts[source].astype(jnp.float32)[:rows]
     result = mixed.astype(jnp.bfloat16)
-    for target in range(count):
+    for target in range(out.shape[0]):
         out[target] = result
 
 
-def out_kernel(gathered, weight, out):
-    count = gathered.shape[0]
-    nodes = gathered.shape[1]
-    total = jnp.zeros((2 * nodes, LANES), jnp.float32)
-    for head in range(count // 2):
-        both = paired(
-            gathered[spot_of(2 * head)][:nodes].astype(jnp.float32),
-            gathered[spot_of(2 * head + 1)][:nodes].astype(jnp.float32),
-        )
-        block = jnp.concatenate(both, axis=0).astype(jnp.bfloat16)
-        total = total + lax.dot_general(
-            block,
-            weight[:, head * HEAD_DIM : (head + 1) * HEAD_DIM],
-            (((1,), (1,)), ((), ())),
-            preferred_element_type=jnp.float32,
-        )
-    result = jnp.where(in_first(nodes), total[:nodes], total[nodes:]).astype(jnp.bfloat16)
-    for target in range(count):
+def out_kernel(gathered, weight, out, wide, rows):
+    depth, chunk_rows, _ = gathered.shape
+    for source in range(depth):
+        wide[source * chunk_rows : (source + 1) * chunk_rows] = gathered[source].astype(jnp.float32)
+    for head in range(HEADS):
+        lines = [
+            wide[pl.ds(row * HEADS + head, depth, stride=chunk_rows), :]
+            for row in range(chunk_rows // HEADS)
+        ]
+        rows[:, head * HEAD_DIM : (head + 1) * HEAD_DIM] = jnp.concatenate(lines, axis=0)
+    product = lax.dot_general(
+        rows[...].astype(jnp.bfloat16),
+        weight[...],
+        (((1,), (1,)), ((), ())),
+        preferred_element_type=jnp.float32,
+    )
+    result = jnp.concatenate([product[:, :LANES], product[:, LANES:]], axis=0).astype(jnp.bfloat16)
+    for target in range(out.shape[0]):
         out[target] = result
 
 
 def residual_kernel(gathered, gain, inputs, out, rows, sem):
     fetch = pltpu.make_async_copy(inputs, rows, sem)
     fetch.start()
-    count = gathered.shape[0]
-    nodes = rows.shape[0] // 2
-    squares = jnp.zeros((nodes, LANES), jnp.float32)
-    for source in range(count):
-        chunk = gathered[source].astype(jnp.float32)[:nodes]
-        squares = squares + chunk * chunk
-    inverse = packed_inverse(squares, count * HALF)
+    count, chunk_rows, _ = gathered.shape
+    depth = count // SIDE
+    lines = chunk_rows // 2
+    width = out.shape[1]
+    eight = lines // 3
+
+    def block(side, place, half):
+        chunk = gathered[side * depth + place].astype(jnp.float32)
+        return chunk[half * lines : (half + 1) * lines]
+
+    def in_order(parts):
+        return jnp.concatenate(
+            [parts[side][row * eight : (row + 1) * eight] for row in range(3) for side in range(SIDE)],
+            axis=0,
+        )
+
+    inverses = []
+    for side in range(SIDE):
+        squares = jnp.zeros((lines, LANES), jnp.float32)
+        for place in range(depth):
+            for half in range(2):
+                found = block(side, place, half)
+                squares = squares + found * found
+        square = jnp.sum(squares, axis=1, keepdims=True) / width
+        inverses.append(jnp.broadcast_to(lax.rsqrt(square + norm_epsilon), (lines, LANES)))
+    inverse = in_order(inverses)
     fetch.wait()
-    for head in range(count // 2):
-        both = paired(
-            gathered[spot_of(2 * head)].astype(jnp.float32)[:nodes] * inverse,
-            gathered[spot_of(2 * head + 1)].astype(jnp.float32)[:nodes] * inverse,
-        )
-        columns = slice(head * HEAD_DIM, (head + 1) * HEAD_DIM)
-        block = jnp.concatenate(both, axis=0) * gain[:, columns]
-        out[:, columns] = (rows[:, columns].astype(jnp.float32) + block).astype(jnp.bfloat16)
+    for place in range(depth):
+        for half in range(2):
+            start = (2 * place + half) * LANES
+            columns = slice(start, start + LANES)
+            found = in_order([block(side, place, half) for side in range(SIDE)])
+            grown = rows[:, columns].astype(jnp.float32) + found * inverse * gain[:, columns]
+            out[:, columns] = grown.astype(jnp.bfloat16)
 
 
 def down_kernel(hidden, weight, out, held):
@@ -427,8 +470,8 @@
     vectors = drafts[...]
     fetch.wait()
     logits = lax.dot_general(
-        vectors, table[...], (((1,), (1,)), ((), ())), preferred_element_type=jnp.float32
-    )
+        table[...], vectors, (((1,), (1,)), ((), ())), preferred_element_type=jnp.float32
+    ).T
     for spot in range(requests):
         out[pl.ds(origins[spot], 1)] = logits[spot * levels : (spot + 1) * levels][None]
 
@@ -515,7 +558,22 @@
         jnp.transpose(draft_weight, (0, 2, 1)).reshape(draft_count * slab, model_width),
     )
     gathered = exchange(query_copies)
+    gate_up_copy = pl.pallas_call(
+        held_kernel,
+        out_shape=jax.ShapeDtypeStruct(gate_up_weight.shape, bf16),
+        in_specs=[HBM],
+        out_specs=vmem(1)[0],
+        scratch_shapes=[pltpu.SemaphoreType.DMA],
+        compiler_params=limit(52),
+        cost_estimate=pl.CostEstimate(flops=2**31, bytes_accessed=0, transcendentals=0),
+        name="held",
+    )(gate_up_weight)
+    gathered, gate_up_copy = lax.optimization_barrier((gathered, gate_up_copy))
     other_key = lax.ppermute(own_key, "x", [(i, i ^ 1) for i in range(SIDE)])
+    out_own, other_key = lax.optimization_barrier((out_weight.T, other_key))
+    out_parts = [out_own] + [
+        lax.ppermute(out_own, "x", [(i, (i + k) % SIDE) for i in range(SIDE)]) for k in range(1, SIDE)
+    ]
 
     ancestry, node_depth = tree_shape(tree_parent)
     positions = cache_len[:, None].astype(f32) + node_depth - 1.0
@@ -535,55 +593,58 @@
     counts = jnp.sum(jnp.where(matches, left[None], 0), axis=2).reshape(page_count * req_local, 1)
 
     groups = 4
-    parts, queries, key_square, drafts = pl.pallas_call(
+    parts, drafts, kept = pl.pallas_call(
         pages_kernel,
         out_shape=(
             jax.ShapeDtypeStruct((mp_count, tree_size + 8, LANES), bf16),
-            jax.ShapeDtypeStruct((HEADS, rows, HEAD_DIM), bf16),
-            jax.ShapeDtypeStruct((8, LANES), f32),
             jax.ShapeDtypeStruct((req_local * draft_count, model_width), bf16),
+            jax.ShapeDtypeStruct((tree_size, LANES), bf16),
         ),
-        in_specs=[*vmem(5), HBM],
-        out_specs=tuple(vmem(4)),
+        in_specs=[SMEM, *vmem(10), HBM],
+        out_specs=tuple(vmem(3)),
         scratch_shapes=[
             pltpu.VMEM(kv_cache.shape, bf16),
-            pltpu.VMEM((mp_count, tree_size, LANES), f32),
+            pltpu.VMEM((mp_count * tree_size, LANES), f32),
+            pltpu.VMEM((HEADS, rows, HEAD_DIM), bf16),
             pltpu.SemaphoreType.DMA((groups,)),
         ],
         compiler_params=limit(52),
         cost_estimate=pl.CostEstimate(flops=2**33, bytes_accessed=0, transcendentals=0),
         name="pages",
-    )(counts, gathered, twice[0], cosine, sine, kv_cache)
-    arrived = exchange(parts)
-
-    path, tree, gate_up_copy = pl.pallas_call(
-        tree_kernel,
-        out_shape=(
-            jax.ShapeDtypeStruct((2, 8, LANES), f32),
-            jax.ShapeDtypeStruct((tree_size + 8, LANES), f32),
-            jax.ShapeDtypeStruct(gate_up_weight.shape, bf16),
-        ),
-        in_specs=[SMEM, SMEM, *vmem(10), HBM],
-        out_specs=tuple(vmem(3)),
-        scratch_shapes=[pltpu.SemaphoreType.DMA],
-        compiler_params=limit(52),
-        cost_estimate=pl.CostEstimate(flops=2**31, bytes_accessed=0, transcendentals=2**13),
-        name="tree",
     )(
         mp_place.reshape(1),
-        accepted_node,
-        queries,
+        counts,
+        gathered,
+        twice[0],
+        twice[1],
+        cosine,
+        sine,
         own_key,
         other_key,
         own_value,
-        key_square,
-        twice[1],
-        cosine,
-        sine,
         ancestry,
-        node_depth,
-        gate_up_weight,
-    )
+        kv_cache,
+    )
+    arrived = exchange(parts)
+
+    path = pl.pallas_call(
+        path_kernel,
+        out_shape=jax.ShapeDtypeStruct((2, 8, LANES), f32),
+        in_specs=[SMEM, *vmem(4)],
+        out_specs=vmem(1)[0],
+        compiler_params=limit(8),
+        name="path",
+    )(accepted_node, kept, own_value, ancestry, node_depth)
+    side_place = lax.axis_index("x").reshape(1)
+    out_wide = pl.pallas_call(
+        order_kernel,
+        out_shape=jax.ShapeDtypeStruct((SIDE, slab, model_width), bf16),
+        in_specs=[SMEM, *vmem(SIDE)],
+        out_specs=vmem(1)[0],
+        compiler_params=limit(12),
+        name="order",
+    )(side_place, *out_parts).reshape(SIDE * slab, model_width)
+
     pair = lax.ppermute(drafts, "c", [(0, 1), (1, 0)])
     both = jnp.concatenate([drafts, pair], axis=0)
     turns = req_count // 2
@@ -602,33 +663,34 @@
         path[:, :draft_count].reshape(2, draft_count, req_local, slab), (2, 1, 0, 3)
     ).astype(bf16)
 
-    out_twice = jnp.concatenate([out_weight.T, out_weight.T], axis=0)
     attended_copies = pl.pallas_call(
         merge_kernel,
-        out_shape=jax.ShapeDtypeStruct((mp_count, tree_size, LANES), bf16),
-        in_specs=[*vmem(1), HBM],
-        out_specs=vmem(1)[0],
-        scratch_shapes=[pltpu.VMEM((tree_size + 8, LANES), f32), pltpu.SemaphoreType.DMA],
+        out_shape=jax.ShapeDtypeStruct((mp_count // SIDE, tree_size, LANES), bf16),
+        in_specs=vmem(1),
+        out_specs=vmem(1)[0],
         compiler_params=limit(8),
-        cost_estimate=pl.CostEstimate(flops=2**31, bytes_accessed=0, transcendentals=0),
         name="merge",
-    )(arrived, tree)
+    )(arrived)
     out_gain = gain_rows[2:3]
     last_gain = gain_rows[3:4]
-    attended_copies, out_twice, accepted_kv, out_gain, last_gain, drafted, origins = (
+    attended_copies, out_wide, accepted_kv, out_gain, last_gain, drafted, origins = (
         lax.optimization_barrier(
-            (attended_copies, out_twice, accepted_kv, out_gain, last_gain, drafted, origins)
+            (attended_copies, out_wide, accepted_kv, out_gain, last_gain, drafted, origins)
         )
     )
-    attended = exchange(attended_copies)
+    attended = lax.all_to_all(attended_copies, "z", 0, 0)
     out_copies = pl.pallas_call(
         out_kernel,
         out_shape=jax.ShapeDtypeStruct((mp_count, tree_size, LANES), bf16),
         in_specs=vmem(2),
         out_specs=vmem(1)[0],
+        scratch_shapes=[
+            pltpu.VMEM((mp_count // SIDE * tree_size, LANES), f32),
+            pltpu.VMEM((rows // SIDE, model_width), f32),
+        ],
         compiler_params=limit(8),
         name="out_columns",
-    )(attended, out_twice)
+    )(attended, out_wide)
     projected_out = exchange(out_copies)
     projected_out, drafted, origins = lax.optimization_barrier((projected_out, drafted, origins))
     residual = pl.pallas_call(

time: 122 us -> 112 us (0.918)
  blocking collectives: 38.6 us -> 28.9 us
  waiting for transfers between devices: 31.6 us -> 25.6 us
  starting transfers between devices: 25.4 us -> 30.9 us
    all_to_all x2 -> x1, blocking collectives: 38.6 us -> 17.8 us  [exchange(): return lax.all_to_all(chunks, TURN, 0, 0)]
    all_to_all x0 -> x1, blocking collectives: none -> 11.1 us  [per_device(): attended = lax.all_to_all(attended_copies, 'z', 0, 0)]
    all_to_all x3, waiting for transfers between devices: 27.5 us -> 21.4 us  [exchange(): return lax.all_to_all(chunks, TURN, 0, 0)]
    ppermute x0 -> x3, starting transfers between devices: none -> 5.36 us  [per_device(): lax.ppermute(out_own, 'x', [(i, (i + k) % SIDE) for i in range(SIDE)])]
    pallas_call x2 -> x4, Pallas kernels: 4.26 us -> 4.22 us  [the longest x1 2.99 us: per_device(): pl.pallas_call(held_kernel, out_shape=jax.ShapeDtypeStruct(gate_up_weight...]
  transfers between devices with their start and end apart: 8 -> 11, of which waited for: 4 -> 4; matrix products, arithmetic and copies ran while one was open for 3% -> 3% of each run, Pallas kernels for 10% -> 12%
where the time goes in v6:
time: 112 us; the launch traced here: 111 us
  starting transfers between devices  30.9 us (28%)
  blocking collectives  28.9 us (26%)
  waiting for transfers between devices  25.6 us (23%)
  Pallas kernels  21.3 us (19%)
  local copies, waits for them, and re-layouts  1.62 us (1%)
    all_to_all x3, waiting for transfers between devices, exchange(): return lax.all_to_all(chunks, TURN, 0, 0)  21.4 us
    all_to_all x3, starting transfers between devices, exchange(): return lax.all_to_all(chunks, TURN, 0, 0)  20.8 us
    all_to_all x1, blocking collectives, exchange(): return lax.all_to_all(chunks, TURN, 0, 0)  17.8 us
    all_to_all x1, blocking collectives, per_device(): attended = lax.all_to_all(attended_copies, 'z', 0, 0)  11.1 us
    pallas_call x1, Pallas kernels, per_device(): pl.pallas_call(pages_kernel, out_shape=(jax.ShapeDtypeStruct((mp_count, t...  5.56 us
    ppermute x3, starting transfers between devices, per_device(): lax.ppermute(out_own, 'x', [(i, (i + k) % SIDE) for i in range(SIDE)])  5.36 us
    pallas_call x1, Pallas kernels, per_device(): pl.pallas_call(project_kernel, out_shape=(jax.ShapeDtypeStruct((mp_count,...  4.8 us
    ppermute x3, waiting for transfers between devices, per_device(): lax.ppermute(both, 'y', [(i, (i + k) % turns) for i in range(turns)])  4.12 us
  transfers between devices with their start and end apart: 11, of which 4 were waited for; matrix products, arithmetic and copies ran while one was open for 3% of the time, Pallas kernels for 12%

profile of v6, /device:TPU:48, one launch (start us, length us, event | category | flops | bytes accessed | tf_op | source)
XLA Modules:
  0.0 111.4 jit_solution(11879707343090181322)
XLA Ops:
  0.6 4.8 %project.1 = (bf16[32,56,128]{2,1,0:T(8,128)(2,1)}, bf16[48,128]{1,0:T(8,128)(2,1)}, bf16[48,128]{1,0:T(8,128)(2,1)}) custom-call(s32[1]{0:T(128)} %bitcast.place, bf16[2,2048]{1,0:T(2,128)(2,1)} %hidden.1, bf16[96,2048]{1,0:T(8,128)(2,1)} %inputs.3, bf16[3,64,2048]{2,1,0:T(8,128)(2,1)} %bitcast.38, bf16[256,2048]{1,0:T(8,128)(2,1)} %bitcast.37), custom_call_target="tpu_custom_call" | custom-call | flops 4294967296 | tf_op jit(solution)/shard_map/project/pallas_call | solution.py:535
  5.5 11.2 %all-to-all-start = ((bf16[32,56,128]{2,1,0:T(8,128)(2,1)}), bf16[32,56,128]{2,1,0:T(8,128)(2,1)S(1)}, u32[]{:S(2)}, u32[]{:S(2)}) async-start(bf16[32,56,128]{2,1,0:T(8,128)(2,1)} %get-tuple-element.23), calls=%async_computation | async-start | bytes 917504 | tf_op jit(solution)/shard_map/all_to_all | solution.py:501
  16.7 1.6 %collective-permute-start = (bf16[48,128]{1,0:T(8,128)(2,1)}, bf16[48,128]{1,0:T(8,128)(2,1)S(1)}, u32[]{:S(2)}, u32[]{:S(2)}) collective-permute-start(bf16[48,128]{1,0:T(8,128)(2,1)} %get-tuple-element.25.own_key), channel_id=1, source_target_pairs={{0,1},{1,0},{2,3},{3,2},{4,5},{5,4},{6,7},{7,6},{8,9},{9,8},{10,11... | collective-permute-start | bytes 36872 | tf_op jit(solution)/shard_map/ppermute | solution.py:572
  18.4 3.0 %held.1 = bf16[2048,2,256]{2,1,0:T(2,128)(2,1)} custom-call(bf16[2048,2,256]{2,1,0:T(2,128)(2,1)} %large.1), custom_call_target="tpu_custom_call" | custom-call | flops 2147483648 | tf_op jit(solution)/shard_map/held/pallas_call | solution.py:561
  23.1 0.6 collective-permute-start.1
  23.7 3.0 %collective-permute-start.2 = (bf16[64,2048]{1,0:T(8,128)(2,1)S(1)}, bf16[64,2048]{1,0:T(8,128)(2,1)S(1)}, u32[]{:S(2)}, u32[]{:S(2)}) collective-permute-start(bf16[64,2048]{1,0:T(8,128)(2,1)S(1)} %bitcast.33), channel_id=1, source_target_pairs={{0,2},{1,3},{2,0},{3,1},{4,6},{5,7},{6,4},{7,5},{8,10},{9,11},{10,... | collective-permute-start | bytes 786440 | tf_op jit(solution)/shard_map/ppermute | solution.py:575
  26.6 1.8 %collective-permute-start.3 = (bf16[64,2048]{1,0:T(8,128)(2,1)S(1)}, bf16[64,2048]{1,0:T(8,128)(2,1)S(1)}, u32[]{:S(2)}, u32[]{:S(2)}) collective-permute-start(bf16[64,2048]{1,0:T(8,128)(2,1)S(1)} %bitcast.34), channel_id=1, source_target_pairs={{0,3},{1,0},{2,1},{3,2},{4,7},{5,4},{6,5},{7,6},{8,11},{9,8},{10,9... | collective-permute-start | bytes 786440 | tf_op jit(solution)/shard_map/ppermute | solution.py:575
  28.5 4.4 %all-to-all-done.gathered = bf16[32,56,128]{2,1,0:T(8,128)(2,1)S(1)} async-done(((bf16[32,56,128]{2,1,0:T(8,128)(2,1)}), bf16[32,56,128]{2,1,0:T(8,128)(2,1)S(1)}, u32[]{:S(2)}, u32[]{:S(2)}) %all-to-all-start) | async-done | bytes 458784 | tf_op jit(solution)/shard_map/all_to_all | solution.py:501
  32.9 5.6 %pages.1 = (bf16[32,56,128]{2,1,0:T(8,128)(2,1)}, bf16[8,2048]{1,0:T(8,128)(2,1)S(1)}, bf16[48,128]{1,0:T(8,128)(2,1)S(1)}) custom-call(s32[1]{0:T(128)} %bitcast.place, s32[8,1]{1,0:T(8,128)S(1)} %reshape.91.counts, bf16[32,56,128]{2,1,0:T(8,128)(2,1)S(1)} %all-to-all-done.gathered, f32[32,128]{1,0:T(8,128)S(1)} %get-tuple-element.48.gains, ...), custom_call_target="tpu_custom_call" | custom-call | flops 8589934592 | tf_op jit(solution)/shard_map/pages/pallas_call | solution.py:596
  38.6 4.9 %all-to-all-start.1 = ((bf16[32,56,128]{2,1,0:T(8,128)(2,1)}), bf16[32,56,128]{2,1,0:T(8,128)(2,1)S(1)}, u32[]{:S(2)}, u32[]{:S(2)}) async-start(bf16[32,56,128]{2,1,0:T(8,128)(2,1)} %get-tuple-element.28), calls=%async_computation.1 | async-start | bytes 917504 | tf_op jit(solution)/shard_map/all_to_all | solution.py:501
  43.5 1.4 %collective-permute-start.5 = (bf16[16,2048]{1,0:T(8,128)(2,1)S(1)}, bf16[16,2048]{1,0:T(8,128)(2,1)S(1)}, u32[]{:S(2)}, u32[]{:S(2)}) collective-permute-start(bf16[16,2048]{1,0:T(8,128)(2,1)S(1)} %get-tuple-element.43), channel_id=1, source_target_pairs={{0,64},{64,128},{128,192},{192,0},{1,65},{65,129},{129,193},{193,1... | collective-permute-start | bytes 196616 | tf_op jit(solution)/shard_map/ppermute | solution.py:652
  45.6 0.7 path.1
  46.3 0.6 copy.52
  46.9 0.6 collective-permute-start.6
  47.5 1.1 collective-permute-start.7
  48.6 4.1 %collective-permute-done.6 = bf16[16,2048]{1,0:T(8,128)(2,1)S(1)} collective-permute-done((bf16[16,2048]{1,0:T(8,128)(2,1)S(1)}, bf16[16,2048]{1,0:T(8,128)(2,1)S(1)}, u32[]{:S(2)}, u32[]{:S(2)}) %collective-permute-start.6) | collective-permute-done | bytes 65568 | tf_op jit(solution)/shard_map/ppermute | solution.py:652
  52.7 7.6 %all-to-all-done.1.parts = bf16[32,56,128]{2,1,0:T(8,128)(2,1)S(1)} async-done(((bf16[32,56,128]{2,1,0:T(8,128)(2,1)}), bf16[32,56,128]{2,1,0:T(8,128)(2,1)S(1)}, u32[]{:S(2)}, u32[]{:S(2)}) %all-to-all-start.1) | async-done | bytes 458784 | tf_op jit(solution)/shard_map/all_to_all | solution.py:501
  60.8 11.1 %all_to_all.25.gathered = bf16[8,48,128]{2,1,0:T(8,128)(2,1)S(1)} all-to-all(bf16[8,48,128]{2,1,0:T(8,128)(2,1)S(1)} %merge.1), channel_id=1, replica_groups=mesh['y'=4,'c'=2,'z'=8,'x'=4] {'z'}, dimensions={0} | all-to-all | bytes 196608 | tf_op jit(solution)/shard_map/all_to_all | solution.py:681
  72.4 17.8 %all_to_all.26.gathered = bf16[32,48,128]{2,1,0:T(8,128)(2,1)S(1)} all-to-all(bf16[32,48,128]{2,1,0:T(8,128)(2,1)S(1)} %out_columns.1), channel_id=1, replica_groups=mesh['y'=4,'c'=2,'z'=8,'x'=4] {'x','z'}, dimensions={0} | all-to-all | bytes 786432 | tf_op jit(solution)/shard_map/all_to_all | solution.py:501
  91.4 1.4 %down.1 = bf16[32,48,128]{2,1,0:T(8,128)(2,1)} custom-call(bf16[96,256]{1,0:T(8,128)(2,1)S(1)} %fusion.4.hidden, bf16[256,2048]{1,0:T(8,128)(2,1)S(1)} %copy-done), custom_call_target="tpu_custom_call" | custom-call | tf_op jit(solution)/shard_map/down/pallas_call | solution.py:709
  92.8 4.7 %all-to-all-start.4 = ((bf16[32,48,128]{2,1,0:T(8,128)(2,1)}), bf16[32,48,128]{2,1,0:T(8,128)(2,1)S(1)}, u32[]{:S(2)}, u32[]{:S(2)}) async-start(bf16[32,48,128]{2,1,0:T(8,128)(2,1)} %down.1), calls=%async_computation.4 | async-start | bytes 786432 | tf_op jit(solution)/shard_map/all_to_all | solution.py:501
  97.5 3.6 %logits.1 = f32[16,4,384]{2,1,0:T(4,128)} custom-call(s32[16]{0:T(128)} %fusion.12.origins, bf16[64,2048]{1,0:T(8,128)(2,1)} %copy-done.7, bf16[384,2048]{1,0:T(8,128)(2,1)} %vocab.1), custom_call_target="tpu_custom_call" | custom-call | flops 2147483648 | tf_op jit(solution)/shard_map/logits/pallas_call | solution.py:720
  101.2 9.4 %all-to-all-done.4.shares = bf16[32,48,128]{2,1,0:T(8,128)(2,1)S(1)} async-done(((bf16[32,48,128]{2,1,0:T(8,128)(2,1)}), bf16[32,48,128]{2,1,0:T(8,128)(2,1)S(1)}, u32[]{:S(2)}, u32[]{:S(2)}) %all-to-all-start.4) | async-done | bytes 393248 | tf_op jit(solution)/shard_map/all_to_all | solution.py:501
  110.6 0.8 last.1
  (69 shorter events, 4.8 us)
Async XLA Ops:
  0.6 17.6 %copy-start.10 = (s32[2]{0:T(128)S(1)}, s32[2]{0:T(128)}, u32[]{:S(2)}) copy-start(s32[2]{0:T(128)} %param.19) | copy-start | bytes 28
  5.5 27.4 %all-to-all-start = ((bf16[32,56,128]{2,1,0:T(8,128)(2,1)}), bf16[32,56,128]{2,1,0:T(8,128)(2,1)S(1)}, u32[]{:S(2)}, u32[]{:S(2)}) async-start(bf16[32,56,128]{2,1,0:T(8,128)(2,1)} %get-tuple-element.23), calls=%async_computation | async-start | bytes 917504 | tf_op jit(solution)/shard_map/all_to_all | solution.py:501
  16.7 6.4 %collective-permute-start = (bf16[48,128]{1,0:T(8,128)(2,1)}, bf16[48,128]{1,0:T(8,128)(2,1)S(1)}, u32[]{:S(2)}, u32[]{:S(2)}) collective-permute-start(bf16[48,128]{1,0:T(8,128)(2,1)} %get-tuple-element.25.own_key), channel_id=1, source_target_pairs={{0,1},{1,0},{2,3},{3,2},{4,5},{5,4},{6,7},{7,6},{8,9},{9,8},{10,11... | collective-permute-start | bytes 36872 | tf_op jit(solution)/shard_map/ppermute | solution.py:572
  18.4 3.1 %copy-start.6 = (bf16[4,2048]{1,0:T(4,128)(2,1)S(1)}, bf16[4,2048]{1,0:T(4,128)(2,1)}, u32[]{:S(2)}) copy-start(bf16[4,2048]{1,0:T(4,128)(2,1)} %param.24) | copy-start | bytes 49156
  18.4 3.2 %copy-start.8 = (s32[2,48]{1,0:T(2,128)S(1)}, s32[2,48]{1,0:T(2,128)}, u32[]{:S(2)}) copy-start(s32[2,48]{1,0:T(2,128)} %param.18) | copy-start | bytes 1156
  18.4 4.2 %copy-start.9 = (s32[2,64]{1,0:T(2,128)S(1)}, s32[2,64]{1,0:T(2,128)}, u32[]{:S(2)}) copy-start(s32[2,64]{1,0:T(2,128)} %param.20) | copy-start | bytes 1540
  18.4 4.7 %copy-start.2 = (bf16[2048,64]{0,1:T(8,128)(2,1)S(1)}, bf16[2048,64]{0,1:T(8,128)(2,1)}, u32[]{:S(2)}) copy-start(bf16[2048,64]{0,1:T(8,128)(2,1)} %param.25) | copy-start | bytes 786436
  18.4 14.5 %copy-start.3 = (bf16[48,128]{1,0:T(8,128)(2,1)S(1)}, bf16[48,128]{1,0:T(8,128)(2,1)}, u32[]{:S(2)}) copy-start(bf16[48,128]{1,0:T(8,128)(2,1)} %get-tuple-element.27.own_value) | copy-start | bytes 36868
  18.4 14.5 %copy-start.5 = (bf16[48,128]{1,0:T(8,128)(2,1)S(1)}, bf16[48,128]{1,0:T(8,128)(2,1)}, u32[]{:S(2)}) copy-start(bf16[48,128]{1,0:T(8,128)(2,1)} %get-tuple-element.25.own_key) | copy-start | bytes 36868
  23.1 22.3 %collective-permute-start.1 = (bf16[64,2048]{1,0:T(8,128)(2,1)S(1)}, bf16[64,2048]{1,0:T(8,128)(2,1)S(1)}, u32[]{:S(2)}, u32[]{:S(2)}) collective-permute-start(bf16[64,2048]{1,0:T(8,128)(2,1)S(1)} %bitcast.32), channel_id=1, source_target_pairs={{0,1},{1,2},{2,3},{3,0},{4,5},{5,6},{6,7},{7,4},{8,9},{9,10},{10,1... | collective-permute-start | bytes 786440 | tf_op jit(solution)/shard_map/ppermute | solution.py:575
  23.7 21.8 %collective-permute-start.2 = (bf16[64,2048]{1,0:T(8,128)(2,1)S(1)}, bf16[64,2048]{1,0:T(8,128)(2,1)S(1)}, u32[]{:S(2)}, u32[]{:S(2)}) collective-permute-start(bf16[64,2048]{1,0:T(8,128)(2,1)S(1)} %bitcast.33), channel_id=1, source_target_pairs={{0,2},{1,3},{2,0},{3,1},{4,6},{5,7},{6,4},{7,5},{8,10},{9,11},{10,... | collective-permute-start | bytes 786440 | tf_op jit(solution)/shard_map/ppermute | solution.py:575
  26.6 18.8 %collective-permute-start.3 = (bf16[64,2048]{1,0:T(8,128)(2,1)S(1)}, bf16[64,2048]{1,0:T(8,128)(2,1)S(1)}, u32[]{:S(2)}, u32[]{:S(2)}) collective-permute-start(bf16[64,2048]{1,0:T(8,128)(2,1)S(1)} %bitcast.34), channel_id=1, source_target_pairs={{0,3},{1,0},{2,1},{3,2},{4,7},{5,4},{6,5},{7,6},{8,11},{9,8},{10,9... | collective-permute-start | bytes 786440 | tf_op jit(solution)/shard_map/ppermute | solution.py:575
  38.5 7.1 %copy-start.4 = (s32[2]{0:T(128)S(1)}, s32[2]{0:T(128)}, u32[]{:S(2)}) copy-start(s32[2]{0:T(128)} %accepted.1) | copy-start | bytes 28
  38.5 5.1 %collective-permute-start.4 = (bf16[8,2048]{1,0:T(8,128)(2,1)S(1)}, bf16[8,2048]{1,0:T(8,128)(2,1)S(1)}, u32[]{:S(2)}, u32[]{:S(2)}) collective-permute-start(bf16[8,2048]{1,0:T(8,128)(2,1)S(1)} %get-tuple-element.31), channel_id=1, source_target_pairs={{0,32},{32,0},{1,33},{33,1},{2,34},{34,2},{3,35},{35,3},{4,36},{36... | collective-permute-start | bytes 98312 | tf_op jit(solution)/shard_map/ppermute | solution.py:648
  38.6 21.8 %all-to-all-start.1 = ((bf16[32,56,128]{2,1,0:T(8,128)(2,1)}), bf16[32,56,128]{2,1,0:T(8,128)(2,1)S(1)}, u32[]{:S(2)}, u32[]{:S(2)}) async-start(bf16[32,56,128]{2,1,0:T(8,128)(2,1)} %get-tuple-element.28), calls=%async_computation.1 | async-start | bytes 917504 | tf_op jit(solution)/shard_map/all_to_all | solution.py:501
  43.5 5.1 %collective-permute-start.5 = (bf16[16,2048]{1,0:T(8,128)(2,1)S(1)}, bf16[16,2048]{1,0:T(8,128)(2,1)S(1)}, u32[]{:S(2)}, u32[]{:S(2)}) collective-permute-start(bf16[16,2048]{1,0:T(8,128)(2,1)S(1)} %get-tuple-element.43), channel_id=1, source_target_pairs={{0,64},{64,128},{128,192},{192,0},{1,65},{65,129},{129,193},{193,1... | collective-permute-start | bytes 196616 | tf_op jit(solution)/shard_map/ppermute | solution.py:652
  45.5 44.7 %copy-start.1 = (bf16[96,2048]{1,0:T(8,128)(2,1)S(1)}, bf16[96,2048]{1,0:T(8,128)(2,1)}, u32[]{:S(2)}) copy-start(bf16[96,2048]{1,0:T(8,128)(2,1)} %inputs.3) | copy-start | bytes 1179652
  46.9 5.8 %collective-permute-start.6 = (bf16[16,2048]{1,0:T(8,128)(2,1)S(1)}, bf16[16,2048]{1,0:T(8,128)(2,1)S(1)}, u32[]{:S(2)}, u32[]{:S(2)}) collective-permute-start(bf16[16,2048]{1,0:T(8,128)(2,1)S(1)} %get-tuple-element.43), channel_id=1, source_target_pairs={{0,128},{64,192},{128,0},{192,64},{1,129},{65,193},{129,1},{193,65... | collective-permute-start | bytes 196616 | tf_op jit(solution)/shard_map/ppermute | solution.py:652
  47.5 5.2 %collective-permute-start.7 = (bf16[16,2048]{1,0:T(8,128)(2,1)S(1)}, bf16[16,2048]{1,0:T(8,128)(2,1)S(1)}, u32[]{:S(2)}, u32[]{:S(2)}) collective-permute-start(bf16[16,2048]{1,0:T(8,128)(2,1)S(1)} %get-tuple-element.43), channel_id=1, source_target_pairs={{0,192},{64,0},{128,64},{192,128},{1,193},{65,1},{129,65},{193,129... | collective-permute-start | bytes 196616 | tf_op jit(solution)/shard_map/ppermute | solution.py:652
  52.7 38.0 %copy-start.7 = (bf16[64,2048]{1,0:T(8,128)(2,1)}, bf16[64,2048]{1,0:T(8,128)(2,1)S(1)}, u32[]{:S(2)}) copy-start(bf16[64,2048]{1,0:T(8,128)(2,1)S(1)} %constant_dynamic-update-slice_fusion.2.drafts) | copy-start | bytes 786436
  60.3 30.4 %copy-start.11 = (bf16[2048,2,256]{2,1,0:T(2,128)(2,1)S(1)}, bf16[2048,2,256]{2,1,0:T(2,128)(2,1)}, u32[]{:S(2)}) copy-start(bf16[2048,2,256]{2,1,0:T(2,128)(2,1)} %held.1) | copy-start | bytes 6291460
  90.2 1.2 %copy-start = (bf16[256,2048]{1,0:T(8,128)(2,1)S(1)}, bf16[256,2048]{1,0:T(8,128)(2,1)}, u32[]{:S(2)}) copy-start(bf16[256,2048]{1,0:T(8,128)(2,1)} %weight.1) | copy-start | bytes 3145732
  92.8 17.8 %all-to-all-start.4 = ((bf16[32,48,128]{2,1,0:T(8,128)(2,1)}), bf16[32,48,128]{2,1,0:T(8,128)(2,1)S(1)}, u32[]{:S(2)}, u32[]{:S(2)}) async-start(bf16[32,48,128]{2,1,0:T(8,128)(2,1)} %down.1), calls=%async_computation.4 | async-start | bytes 786432 | tf_op jit(solution)/shard_map/all_to_all | solution.py:501

commit v7 on v6

--- a/solution.py
+++ b/solution.py
@@ -69,19 +69,37 @@
     place, hidden, inputs, weights, draft_weights, copies, own_key, own_value, rows, columns, heads, sems
 ):
     nodes = own_key.shape[0]
-    fetches = [pltpu.make_async_copy(inputs, rows, sems.at[0])]
-    for place_of, kind in enumerate((0, 1, 2, 2)):
-        block = columns.at[pl.ds(place_of * HALF, HALF)]
-        fetches.append(pltpu.make_async_copy(weights.at[kind], block, sems.at[1 + place_of]))
-    fetches.append(pltpu.make_async_copy(draft_weights, heads, sems.at[5]))
-    for fetch in fetches:
-        fetch.start()
-    for fetch in fetches[:5]:
-        fetch.wait()
+    pieces = sems.shape[0] - 1
+    depth = rows.shape[1] // pieces
+    fetches = []
+    for piece in range(pieces):
+        part = pl.ds(piece * depth, depth)
+        fetches.append(
+            [pltpu.make_async_copy(inputs.at[:, part], rows.at[:, part], sems.at[piece, 0])]
+            + [
+                pltpu.make_async_copy(
+                    weights.at[kind, :, part],
+                    columns.at[pl.ds(kind * HALF, HALF), part],
+                    sems.at[piece, 1 + kind],
+                )
+                for kind in range(3)
+            ]
+        )
+    drafting = pltpu.make_async_copy(draft_weights, heads, sems.at[pieces, 0])
+    for group in fetches:
+        for fetch in group:
+            fetch.start()
+    drafting.start()
     first = in_first(nodes)
-    product = lax.dot_general(
-        columns[...], rows[...], (((1,), (1,)), ((), ())), preferred_element_type=jnp.float32
-    ).T
+    product = jnp.zeros((rows.shape[0], 2 * LANES), jnp.float32)
+    for piece, group in enumerate(fetches):
+        for fetch in group:
+            fetch.wait()
+        part = slice(piece * depth, (piece + 1) * depth)
+        weight = jnp.concatenate([columns[:, part], columns[2 * HALF :, part]], axis=0)
+        product = product + lax.dot_general(
+            rows[:, part], weight, (((1,), (1,)), ((), ())), preferred_element_type=jnp.float32
+        )
     query, key = paired(product[:nodes, :LANES], product[nodes:, :LANES])
     key = key.astype(jnp.bfloat16)
     query = query.astype(jnp.bfloat16)
@@ -97,7 +115,7 @@
     right = jnp.sum(jnp.where(first, zero, squares), axis=1, keepdims=True)
     turned = columns_to_rows(jnp.where(lane == 0, left, jnp.where(lane == 1, right, zero)))
     sums = jnp.where(in_first(1), turned[0:1], pltpu.roll(turned[1:2], HALF, 1))
-    fetches[5].wait()
+    drafting.wait()
     states = hidden[...]
     start = pl.multiple_of(place[0] // 2 * LANES, LANES)
     own = hidden[:, pl.ds(start, LANES)].astype(jnp.float32)
@@ -245,7 +263,7 @@
             preferred_element_type=jnp.float32,
         )
 
-    ahead = 3
+    ahead = 4
     waiting = [scored(head) for head in range(ahead)]
     for head in range(HEADS):
         scores = waiting.pop(0)
@@ -543,9 +561,9 @@
         out_specs=tuple(vmem(3)),
         scratch_shapes=[
             pltpu.VMEM((rows, model_width), bf16),
-            pltpu.VMEM((4 * slab, model_width), bf16),
+            pltpu.VMEM((3 * slab, model_width), bf16),
             pltpu.VMEM((draft_count * slab, model_width), bf16),
-            pltpu.SemaphoreType.DMA((6,)),
+            pltpu.SemaphoreType.DMA((3, 4)),
         ],
         compiler_params=limit(60),
         cost_estimate=pl.CostEstimate(flops=2**32, bytes_accessed=0, transcendentals=0),

time: 112 us -> 112 us (level)
  no operation moved by 1% of the time
where the time goes in v7:
time: 112 us; the launch traced here: 111 us
  starting transfers between devices  30.9 us (28%)
  blocking collectives  28.9 us (26%)
  waiting for transfers between devices  25.6 us (23%)
  Pallas kernels  21.1 us (19%)
  local copies, waits for them, and re-layouts  1.61 us (1%)
    all_to_all x3, waiting for transfers between devices, exchange(): return lax.all_to_all(chunks, TURN, 0, 0)  21.4 us
    all_to_all x3, starting transfers between devices, exchange(): return lax.all_to_all(chunks, TURN, 0, 0)  20.8 us
    all_to_all x1, blocking collectives, exchange(): return lax.all_to_all(chunks, TURN, 0, 0)  17.8 us
    all_to_all x1, blocking collectives, per_device(): attended = lax.all_to_all(attended_copies, 'z', 0, 0)  11.1 us
    pallas_call x1, Pallas kernels, per_device(): pl.pallas_call(pages_kernel, out_shape=(jax.ShapeDtypeStruct((mp_count, t...  5.52 us
    ppermute x3, starting transfers between devices, per_device(): lax.ppermute(out_own, 'x', [(i, (i + k) % SIDE) for i in range(SIDE)])  5.36 us
    pallas_call x1, Pallas kernels, per_device(): pl.pallas_call(project_kernel, out_shape=(jax.ShapeDtypeStruct((mp_count,...  4.61 us
    ppermute x3, waiting for transfers between devices, per_device(): lax.ppermute(both, 'y', [(i, (i + k) % turns) for i in range(turns)])  4.12 us
  transfers between devices with their start and end apart: 11, of which 4 were waited for; matrix products, arithmetic and copies ran while one was open for 3% of the time, Pallas kernels for 12%

profile of v7, /device:TPU:48, one launch (start us, length us, event | category | flops | bytes accessed | tf_op | source)
XLA Modules:
  0.0 111.1 jit_solution(307868378864398301)
XLA Ops:
  0.6 4.6 %project.1 = (bf16[32,56,128]{2,1,0:T(8,128)(2,1)}, bf16[48,128]{1,0:T(8,128)(2,1)}, bf16[48,128]{1,0:T(8,128)(2,1)}) custom-call(s32[1]{0:T(128)} %bitcast.place, bf16[2,2048]{1,0:T(2,128)(2,1)} %hidden.1, bf16[96,2048]{1,0:T(8,128)(2,1)} %inputs.3, bf16[3,64,2048]{2,1,0:T(8,128)(2,1)} %bitcast.38, bf16[256,2048]{1,0:T(8,128)(2,1)} %bitcast.37), custom_call_target="tpu_custom_call" | custom-call | flops 4294967296 | tf_op jit(solution)/shard_map/project/pallas_call | solution.py:553
  5.3 11.2 %all-to-all-start = ((bf16[32,56,128]{2,1,0:T(8,128)(2,1)}), bf16[32,56,128]{2,1,0:T(8,128)(2,1)S(1)}, u32[]{:S(2)}, u32[]{:S(2)}) async-start(bf16[32,56,128]{2,1,0:T(8,128)(2,1)} %get-tuple-element.23), calls=%async_computation | async-start | bytes 917504 | tf_op jit(solution)/shard_map/all_to_all | solution.py:519
  16.5 1.6 %collective-permute-start = (bf16[48,128]{1,0:T(8,128)(2,1)}, bf16[48,128]{1,0:T(8,128)(2,1)S(1)}, u32[]{:S(2)}, u32[]{:S(2)}) collective-permute-start(bf16[48,128]{1,0:T(8,128)(2,1)} %get-tuple-element.25.own_key), channel_id=1, source_target_pairs={{0,1},{1,0},{2,3},{3,2},{4,5},{5,4},{6,7},{7,6},{8,9},{9,8},{10,11... | collective-permute-start | bytes 36872 | tf_op jit(solution)/shard_map/ppermute | solution.py:590
  18.2 3.0 %held.1 = bf16[2048,2,256]{2,1,0:T(2,128)(2,1)} custom-call(bf16[2048,2,256]{2,1,0:T(2,128)(2,1)} %large.1), custom_call_target="tpu_custom_call" | custom-call | flops 2147483648 | tf_op jit(solution)/shard_map/held/pallas_call | solution.py:579
  22.9 0.6 collective-permute-start.1
  23.5 3.0 %collective-permute-start.2 = (bf16[64,2048]{1,0:T(8,128)(2,1)S(1)}, bf16[64,2048]{1,0:T(8,128)(2,1)S(1)}, u32[]{:S(2)}, u32[]{:S(2)}) collective-permute-start(bf16[64,2048]{1,0:T(8,128)(2,1)S(1)} %bitcast.33), channel_id=1, source_target_pairs={{0,2},{1,3},{2,0},{3,1},{4,6},{5,7},{6,4},{7,5},{8,10},{9,11},{10,... | collective-permute-start | bytes 786440 | tf_op jit(solution)/shard_map/ppermute | solution.py:593
  26.4 1.8 %collective-permute-start.3 = (bf16[64,2048]{1,0:T(8,128)(2,1)S(1)}, bf16[64,2048]{1,0:T(8,128)(2,1)S(1)}, u32[]{:S(2)}, u32[]{:S(2)}) collective-permute-start(bf16[64,2048]{1,0:T(8,128)(2,1)S(1)} %bitcast.34), channel_id=1, source_target_pairs={{0,3},{1,0},{2,1},{3,2},{4,7},{5,4},{6,5},{7,6},{8,11},{9,8},{10,9... | collective-permute-start | bytes 786440 | tf_op jit(solution)/shard_map/ppermute | solution.py:593
  28.3 4.4 %all-to-all-done.gathered = bf16[32,56,128]{2,1,0:T(8,128)(2,1)S(1)} async-done(((bf16[32,56,128]{2,1,0:T(8,128)(2,1)}), bf16[32,56,128]{2,1,0:T(8,128)(2,1)S(1)}, u32[]{:S(2)}, u32[]{:S(2)}) %all-to-all-start) | async-done | bytes 458784 | tf_op jit(solution)/shard_map/all_to_all | solution.py:519
  32.7 5.5 %pages.1 = (bf16[32,56,128]{2,1,0:T(8,128)(2,1)}, bf16[8,2048]{1,0:T(8,128)(2,1)S(1)}, bf16[48,128]{1,0:T(8,128)(2,1)S(1)}) custom-call(s32[1]{0:T(128)} %bitcast.place, s32[8,1]{1,0:T(8,128)S(1)} %reshape.91.counts, bf16[32,56,128]{2,1,0:T(8,128)(2,1)S(1)} %all-to-all-done.gathered, f32[32,128]{1,0:T(8,128)S(1)} %get-tuple-element.48.gains, ...), custom_call_target="tpu_custom_call" | custom-call | flops 8589934592 | tf_op jit(solution)/shard_map/pages/pallas_call | solution.py:614
  38.3 4.9 %all-to-all-start.1 = ((bf16[32,56,128]{2,1,0:T(8,128)(2,1)}), bf16[32,56,128]{2,1,0:T(8,128)(2,1)S(1)}, u32[]{:S(2)}, u32[]{:S(2)}) async-start(bf16[32,56,128]{2,1,0:T(8,128)(2,1)} %get-tuple-element.28), calls=%async_computation.1 | async-start | bytes 917504 | tf_op jit(solution)/shard_map/all_to_all | solution.py:519
  43.3 1.4 %collective-permute-start.5 = (bf16[16,2048]{1,0:T(8,128)(2,1)S(1)}, bf16[16,2048]{1,0:T(8,128)(2,1)S(1)}, u32[]{:S(2)}, u32[]{:S(2)}) collective-permute-start(bf16[16,2048]{1,0:T(8,128)(2,1)S(1)} %get-tuple-element.43), channel_id=1, source_target_pairs={{0,64},{64,128},{128,192},{192,0},{1,65},{65,129},{129,193},{193,1... | collective-permute-start | bytes 196616 | tf_op jit(solution)/shard_map/ppermute | solution.py:670
  45.3 0.7 path.1
  46.1 0.6 copy.52
  46.7 0.6 collective-permute-start.6
  47.3 1.1 collective-permute-start.7
  48.4 4.1 %collective-permute-done.6 = bf16[16,2048]{1,0:T(8,128)(2,1)S(1)} collective-permute-done((bf16[16,2048]{1,0:T(8,128)(2,1)S(1)}, bf16[16,2048]{1,0:T(8,128)(2,1)S(1)}, u32[]{:S(2)}, u32[]{:S(2)}) %collective-permute-start.6) | collective-permute-done | bytes 65568 | tf_op jit(solution)/shard_map/ppermute | solution.py:670
  52.5 7.6 %all-to-all-done.1.parts = bf16[32,56,128]{2,1,0:T(8,128)(2,1)S(1)} async-done(((bf16[32,56,128]{2,1,0:T(8,128)(2,1)}), bf16[32,56,128]{2,1,0:T(8,128)(2,1)S(1)}, u32[]{:S(2)}, u32[]{:S(2)}) %all-to-all-start.1) | async-done | bytes 458784 | tf_op jit(solution)/shard_map/all_to_all | solution.py:519
  60.6 11.1 %all_to_all.25.gathered = bf16[8,48,128]{2,1,0:T(8,128)(2,1)S(1)} all-to-all(bf16[8,48,128]{2,1,0:T(8,128)(2,1)S(1)} %merge.1), channel_id=1, replica_groups=mesh['y'=4,'c'=2,'z'=8,'x'=4] {'z'}, dimensions={0} | all-to-all | bytes 196608 | tf_op jit(solution)/shard_map/all_to_all | solution.py:699
  72.2 17.8 %all_to_all.26.gathered = bf16[32,48,128]{2,1,0:T(8,128)(2,1)S(1)} all-to-all(bf16[32,48,128]{2,1,0:T(8,128)(2,1)S(1)} %out_columns.1), channel_id=1, replica_groups=mesh['y'=4,'c'=2,'z'=8,'x'=4] {'x','z'}, dimensions={0} | all-to-all | bytes 786432 | tf_op jit(solution)/shard_map/all_to_all | solution.py:519
  91.2 1.4 %down.1 = bf16[32,48,128]{2,1,0:T(8,128)(2,1)} custom-call(bf16[96,256]{1,0:T(8,128)(2,1)S(1)} %fusion.4.hidden, bf16[256,2048]{1,0:T(8,128)(2,1)S(1)} %copy-done), custom_call_target="tpu_custom_call" | custom-call | tf_op jit(solution)/shard_map/down/pallas_call | solution.py:727
  92.6 4.7 %all-to-all-start.4 = ((bf16[32,48,128]{2,1,0:T(8,128)(2,1)}), bf16[32,48,128]{2,1,0:T(8,128)(2,1)S(1)}, u32[]{:S(2)}, u32[]{:S(2)}) async-start(bf16[32,48,128]{2,1,0:T(8,128)(2,1)} %down.1), calls=%async_computation.4 | async-start | bytes 786432 | tf_op jit(solution)/shard_map/all_to_all | solution.py:519
  97.3 3.6 %logits.1 = f32[16,4,384]{2,1,0:T(4,128)} custom-call(s32[16]{0:T(128)} %fusion.12.origins, bf16[64,2048]{1,0:T(8,128)(2,1)} %copy-done.7, bf16[384,2048]{1,0:T(8,128)(2,1)} %vocab.1), custom_call_target="tpu_custom_call" | custom-call | flops 2147483648 | tf_op jit(solution)/shard_map/logits/pallas_call | solution.py:738
  100.9 9.4 %all-to-all-done.4.shares = bf16[32,48,128]{2,1,0:T(8,128)(2,1)S(1)} async-done(((bf16[32,48,128]{2,1,0:T(8,128)(2,1)}), bf16[32,48,128]{2,1,0:T(8,128)(2,1)S(1)}, u32[]{:S(2)}, u32[]{:S(2)}) %all-to-all-start.4) | async-done | bytes 393248 | tf_op jit(solution)/shard_map/all_to_all | solution.py:519
  110.4 0.8 last.1
  (69 shorter events, 4.8 us)
Async XLA Ops:
  0.6 17.4 %copy-start.10 = (s32[2]{0:T(128)S(1)}, s32[2]{0:T(128)}, u32[]{:S(2)}) copy-start(s32[2]{0:T(128)} %param.19) | copy-start | bytes 28
  5.3 27.4 %all-to-all-start = ((bf16[32,56,128]{2,1,0:T(8,128)(2,1)}), bf16[32,56,128]{2,1,0:T(8,128)(2,1)S(1)}, u32[]{:S(2)}, u32[]{:S(2)}) async-start(bf16[32,56,128]{2,1,0:T(8,128)(2,1)} %get-tuple-element.23), calls=%async_computation | async-start | bytes 917504 | tf_op jit(solution)/shard_map/all_to_all | solution.py:519
  16.5 6.4 %collective-permute-start = (bf16[48,128]{1,0:T(8,128)(2,1)}, bf16[48,128]{1,0:T(8,128)(2,1)S(1)}, u32[]{:S(2)}, u32[]{:S(2)}) collective-permute-start(bf16[48,128]{1,0:T(8,128)(2,1)} %get-tuple-element.25.own_key), channel_id=1, source_target_pairs={{0,1},{1,0},{2,3},{3,2},{4,5},{5,4},{6,7},{7,6},{8,9},{9,8},{10,11... | collective-permute-start | bytes 36872 | tf_op jit(solution)/shard_map/ppermute | solution.py:590
  18.2 3.1 %copy-start.6 = (bf16[4,2048]{1,0:T(4,128)(2,1)S(1)}, bf16[4,2048]{1,0:T(4,128)(2,1)}, u32[]{:S(2)}) copy-start(bf16[4,2048]{1,0:T(4,128)(2,1)} %param.24) | copy-start | bytes 49156
  18.2 3.2 %copy-start.8 = (s32[2,48]{1,0:T(2,128)S(1)}, s32[2,48]{1,0:T(2,128)}, u32[]{:S(2)}) copy-start(s32[2,48]{1,0:T(2,128)} %param.18) | copy-start | bytes 1156
  18.2 4.2 %copy-start.9 = (s32[2,64]{1,0:T(2,128)S(1)}, s32[2,64]{1,0:T(2,128)}, u32[]{:S(2)}) copy-start(s32[2,64]{1,0:T(2,128)} %param.20) | copy-start | bytes 1540
  18.2 4.7 %copy-start.2 = (bf16[2048,64]{0,1:T(8,128)(2,1)S(1)}, bf16[2048,64]{0,1:T(8,128)(2,1)}, u32[]{:S(2)}) copy-start(bf16[2048,64]{0,1:T(8,128)(2,1)} %param.25) | copy-start | bytes 786436
  18.2 14.5 %copy-start.3 = (bf16[48,128]{1,0:T(8,128)(2,1)S(1)}, bf16[48,128]{1,0:T(8,128)(2,1)}, u32[]{:S(2)}) copy-start(bf16[48,128]{1,0:T(8,128)(2,1)} %get-tuple-element.27.own_value) | copy-start | bytes 36868
  18.2 14.5 %copy-start.5 = (bf16[48,128]{1,0:T(8,128)(2,1)S(1)}, bf16[48,128]{1,0:T(8,128)(2,1)}, u32[]{:S(2)}) copy-start(bf16[48,128]{1,0:T(8,128)(2,1)} %get-tuple-element.25.own_key) | copy-start | bytes 36868
  22.9 22.3 %collective-permute-start.1 = (bf16[64,2048]{1,0:T(8,128)(2,1)S(1)}, bf16[64,2048]{1,0:T(8,128)(2,1)S(1)}, u32[]{:S(2)}, u32[]{:S(2)}) collective-permute-start(bf16[64,2048]{1,0:T(8,128)(2,1)S(1)} %bitcast.32), channel_id=1, source_target_pairs={{0,1},{1,2},{2,3},{3,0},{4,5},{5,6},{6,7},{7,4},{8,9},{9,10},{10,1... | collective-permute-start | bytes 786440 | tf_op jit(solution)/shard_map/ppermute | solution.py:593
  23.5 21.7 %collective-permute-start.2 = (bf16[64,2048]{1,0:T(8,128)(2,1)S(1)}, bf16[64,2048]{1,0:T(8,128)(2,1)S(1)}, u32[]{:S(2)}, u32[]{:S(2)}) collective-permute-start(bf16[64,2048]{1,0:T(8,128)(2,1)S(1)} %bitcast.33), channel_id=1, source_target_pairs={{0,2},{1,3},{2,0},{3,1},{4,6},{5,7},{6,4},{7,5},{8,10},{9,11},{10,... | collective-permute-start | bytes 786440 | tf_op jit(solution)/shard_map/ppermute | solution.py:593
  26.4 18.8 %collective-permute-start.3 = (bf16[64,2048]{1,0:T(8,128)(2,1)S(1)}, bf16[64,2048]{1,0:T(8,128)(2,1)S(1)}, u32[]{:S(2)}, u32[]{:S(2)}) collective-permute-start(bf16[64,2048]{1,0:T(8,128)(2,1)S(1)} %bitcast.34), channel_id=1, source_target_pairs={{0,3},{1,0},{2,1},{3,2},{4,7},{5,4},{6,5},{7,6},{8,11},{9,8},{10,9... | collective-permute-start | bytes 786440 | tf_op jit(solution)/shard_map/ppermute | solution.py:593
  38.2 7.1 %copy-start.4 = (s32[2]{0:T(128)S(1)}, s32[2]{0:T(128)}, u32[]{:S(2)}) copy-start(s32[2]{0:T(128)} %accepted.1) | copy-start | bytes 28
  38.2 5.1 %collective-permute-start.4 = (bf16[8,2048]{1,0:T(8,128)(2,1)S(1)}, bf16[8,2048]{1,0:T(8,128)(2,1)S(1)}, u32[]{:S(2)}, u32[]{:S(2)}) collective-permute-start(bf16[8,2048]{1,0:T(8,128)(2,1)S(1)} %get-tuple-element.31), channel_id=1, source_target_pairs={{0,32},{32,0},{1,33},{33,1},{2,34},{34,2},{3,35},{35,3},{4,36},{36... | collective-permute-start | bytes 98312 | tf_op jit(solution)/shard_map/ppermute | solution.py:666
  38.3 21.8 %all-to-all-start.1 = ((bf16[32,56,128]{2,1,0:T(8,128)(2,1)}), bf16[32,56,128]{2,1,0:T(8,128)(2,1)S(1)}, u32[]{:S(2)}, u32[]{:S(2)}) async-start(bf16[32,56,128]{2,1,0:T(8,128)(2,1)} %get-tuple-element.28), calls=%async_computation.1 | async-start | bytes 917504 | tf_op jit(solution)/shard_map/all_to_all | solution.py:519
  43.3 5.0 %collective-permute-start.5 = (bf16[16,2048]{1,0:T(8,128)(2,1)S(1)}, bf16[16,2048]{1,0:T(8,128)(2,1)S(1)}, u32[]{:S(2)}, u32[]{:S(2)}) collective-permute-start(bf16[16,2048]{1,0:T(8,128)(2,1)S(1)} %get-tuple-element.43), channel_id=1, source_target_pairs={{0,64},{64,128},{128,192},{192,0},{1,65},{65,129},{129,193},{193,1... | collective-permute-start | bytes 196616 | tf_op jit(solution)/shard_map/ppermute | solution.py:670
  45.3 44.7 %copy-start.1 = (bf16[96,2048]{1,0:T(8,128)(2,1)S(1)}, bf16[96,2048]{1,0:T(8,128)(2,1)}, u32[]{:S(2)}) copy-start(bf16[96,2048]{1,0:T(8,128)(2,1)} %inputs.3) | copy-start | bytes 1179652
  46.7 5.8 %collective-permute-start.6 = (bf16[16,2048]{1,0:T(8,128)(2,1)S(1)}, bf16[16,2048]{1,0:T(8,128)(2,1)S(1)}, u32[]{:S(2)}, u32[]{:S(2)}) collective-permute-start(bf16[16,2048]{1,0:T(8,128)(2,1)S(1)} %get-tuple-element.43), channel_id=1, source_target_pairs={{0,128},{64,192},{128,0},{192,64},{1,129},{65,193},{129,1},{193,65... | collective-permute-start | bytes 196616 | tf_op jit(solution)/shard_map/ppermute | solution.py:670
  47.3 5.2 %collective-permute-start.7 = (bf16[16,2048]{1,0:T(8,128)(2,1)S(1)}, bf16[16,2048]{1,0:T(8,128)(2,1)S(1)}, u32[]{:S(2)}, u32[]{:S(2)}) collective-permute-start(bf16[16,2048]{1,0:T(8,128)(2,1)S(1)} %get-tuple-element.43), channel_id=1, source_target_pairs={{0,192},{64,0},{128,64},{192,128},{1,193},{65,1},{129,65},{193,129... | collective-permute-start | bytes 196616 | tf_op jit(solution)/shard_map/ppermute | solution.py:670
  52.5 38.0 %copy-start.7 = (bf16[64,2048]{1,0:T(8,128)(2,1)}, bf16[64,2048]{1,0:T(8,128)(2,1)S(1)}, u32[]{:S(2)}) copy-start(bf16[64,2048]{1,0:T(8,128)(2,1)S(1)} %constant_dynamic-update-slice_fusion.2.drafts) | copy-start | bytes 786436
  60.1 30.4 %copy-start.11 = (bf16[2048,2,256]{2,1,0:T(2,128)(2,1)S(1)}, bf16[2048,2,256]{2,1,0:T(2,128)(2,1)}, u32[]{:S(2)}) copy-start(bf16[2048,2,256]{2,1,0:T(2,128)(2,1)} %held.1) | copy-start | bytes 6291460
  90.0 1.2 %copy-start = (bf16[256,2048]{1,0:T(8,128)(2,1)S(1)}, bf16[256,2048]{1,0:T(8,128)(2,1)}, u32[]{:S(2)}) copy-start(bf16[256,2048]{1,0:T(8,128)(2,1)} %weight.1) | copy-start | bytes 3145732
  92.6 17.8 %all-to-all-start.4 = ((bf16[32,48,128]{2,1,0:T(8,128)(2,1)}), bf16[32,48,128]{2,1,0:T(8,128)(2,1)S(1)}, u32[]{:S(2)}, u32[]{:S(2)}) async-start(bf16[32,48,128]{2,1,0:T(8,128)(2,1)} %down.1), calls=%async_computation.4 | async-start | bytes 786432 | tf_op jit(solution)/shard_map/all_to_all | solution.py:519

commit v8 on v7

--- a/solution.py
+++ b/solution.py
@@ -563,7 +563,7 @@
             pltpu.VMEM((rows, model_width), bf16),
             pltpu.VMEM((3 * slab, model_width), bf16),
             pltpu.VMEM((draft_count * slab, model_width), bf16),
-            pltpu.SemaphoreType.DMA((3, 4)),
+            pltpu.SemaphoreType.DMA((5, 4)),
         ],
         compiler_params=limit(60),
         cost_estimate=pl.CostEstimate(flops=2**32, bytes_accessed=0, transcendentals=0),

time: 112 us -> 112 us (level)
  no operation moved by 1% of the time
where the time goes in v8:
time: 112 us; the launch traced here: 111 us
  starting transfers between devices  30.8 us (28%)
  blocking collectives  28.9 us (26%)
  waiting for transfers between devices  25.6 us (23%)
  Pallas kernels  21 us (19%)
  local copies, waits for them, and re-layouts  1.61 us (1%)
    all_to_all x3, waiting for transfers between devices, exchange(): return lax.all_to_all(chunks, TURN, 0, 0)  21.4 us
    all_to_all x3, starting transfers between devices, exchange(): return lax.all_to_all(chunks, TURN, 0, 0)  20.8 us
    all_to_all x1, blocking collectives, exchange(): return lax.all_to_all(chunks, TURN, 0, 0)  17.8 us
    all_to_all x1, blocking collectives, per_device(): attended = lax.all_to_all(attended_copies, 'z', 0, 0)  11.1 us
    pallas_call x1, Pallas kernels, per_device(): pl.pallas_call(pages_kernel, out_shape=(jax.ShapeDtypeStruct((mp_count, t...  5.52 us
    ppermute x3, starting transfers between devices, per_device(): lax.ppermute(out_own, 'x', [(i, (i + k) % SIDE) for i in range(SIDE)])  5.36 us
    pallas_call x1, Pallas kernels, per_device(): pl.pallas_call(project_kernel, out_shape=(jax.ShapeDtypeStruct((mp_count,...  4.5 us
    ppermute x3, waiting for transfers between devices, per_device(): lax.ppermute(both, 'y', [(i, (i + k) % turns) for i in range(turns)])  4.13 us
  transfers between devices with their start and end apart: 11, of which 4 were waited for; matrix products, arithmetic and copies ran while one was open for 3% of the time, Pallas kernels for 12%

profile of v8, /device:TPU:48, one launch (start us, length us, event | category | flops | bytes accessed | tf_op | source)
XLA Modules:
  0.0 111.0 jit_solution(11798123929165066652)
XLA Ops:
  0.6 4.5 %project.1 = (bf16[32,56,128]{2,1,0:T(8,128)(2,1)}, bf16[48,128]{1,0:T(8,128)(2,1)}, bf16[48,128]{1,0:T(8,128)(2,1)}) custom-call(s32[1]{0:T(128)} %bitcast.place, bf16[2,2048]{1,0:T(2,128)(2,1)} %hidden.1, bf16[96,2048]{1,0:T(8,128)(2,1)} %inputs.3, bf16[3,64,2048]{2,1,0:T(8,128)(2,1)} %bitcast.38, bf16[256,2048]{1,0:T(8,128)(2,1)} %bitcast.37), custom_call_target="tpu_custom_call" | custom-call | flops 4294967296 | tf_op jit(solution)/shard_map/project/pallas_call | solution.py:553
  5.2 11.2 %all-to-all-start = ((bf16[32,56,128]{2,1,0:T(8,128)(2,1)}), bf16[32,56,128]{2,1,0:T(8,128)(2,1)S(1)}, u32[]{:S(2)}, u32[]{:S(2)}) async-start(bf16[32,56,128]{2,1,0:T(8,128)(2,1)} %get-tuple-element.23), calls=%async_computation | async-start | bytes 917504 | tf_op jit(solution)/shard_map/all_to_all | solution.py:519
  16.4 1.6 %collective-permute-start = (bf16[48,128]{1,0:T(8,128)(2,1)}, bf16[48,128]{1,0:T(8,128)(2,1)S(1)}, u32[]{:S(2)}, u32[]{:S(2)}) collective-permute-start(bf16[48,128]{1,0:T(8,128)(2,1)} %get-tuple-element.25.own_key), channel_id=1, source_target_pairs={{0,1},{1,0},{2,3},{3,2},{4,5},{5,4},{6,7},{7,6},{8,9},{9,8},{10,11... | collective-permute-start | bytes 36872 | tf_op jit(solution)/shard_map/ppermute | solution.py:590
  18.1 3.0 %held.1 = bf16[2048,2,256]{2,1,0:T(2,128)(2,1)} custom-call(bf16[2048,2,256]{2,1,0:T(2,128)(2,1)} %large.1), custom_call_target="tpu_custom_call" | custom-call | flops 2147483648 | tf_op jit(solution)/shard_map/held/pallas_call | solution.py:579
  22.8 0.6 collective-permute-start.1
  23.4 3.0 %collective-permute-start.2 = (bf16[64,2048]{1,0:T(8,128)(2,1)S(1)}, bf16[64,2048]{1,0:T(8,128)(2,1)S(1)}, u32[]{:S(2)}, u32[]{:S(2)}) collective-permute-start(bf16[64,2048]{1,0:T(8,128)(2,1)S(1)} %bitcast.33), channel_id=1, source_target_pairs={{0,2},{1,3},{2,0},{3,1},{4,6},{5,7},{6,4},{7,5},{8,10},{9,11},{10,... | collective-permute-start | bytes 786440 | tf_op jit(solution)/shard_map/ppermute | solution.py:593
  26.3 1.8 %collective-permute-start.3 = (bf16[64,2048]{1,0:T(8,128)(2,1)S(1)}, bf16[64,2048]{1,0:T(8,128)(2,1)S(1)}, u32[]{:S(2)}, u32[]{:S(2)}) collective-permute-start(bf16[64,2048]{1,0:T(8,128)(2,1)S(1)} %bitcast.34), channel_id=1, source_target_pairs={{0,3},{1,0},{2,1},{3,2},{4,7},{5,4},{6,5},{7,6},{8,11},{9,8},{10,9... | collective-permute-start | bytes 786440 | tf_op jit(solution)/shard_map/ppermute | solution.py:593
  28.2 4.4 %all-to-all-done.gathered = bf16[32,56,128]{2,1,0:T(8,128)(2,1)S(1)} async-done(((bf16[32,56,128]{2,1,0:T(8,128)(2,1)}), bf16[32,56,128]{2,1,0:T(8,128)(2,1)S(1)}, u32[]{:S(2)}, u32[]{:S(2)}) %all-to-all-start) | async-done | bytes 458784 | tf_op jit(solution)/shard_map/all_to_all | solution.py:519
  32.6 5.5 %pages.1 = (bf16[32,56,128]{2,1,0:T(8,128)(2,1)}, bf16[8,2048]{1,0:T(8,128)(2,1)S(1)}, bf16[48,128]{1,0:T(8,128)(2,1)S(1)}) custom-call(s32[1]{0:T(128)} %bitcast.place, s32[8,1]{1,0:T(8,128)S(1)} %reshape.91.counts, bf16[32,56,128]{2,1,0:T(8,128)(2,1)S(1)} %all-to-all-done.gathered, f32[32,128]{1,0:T(8,128)S(1)} %get-tuple-element.48.gains, ...), custom_call_target="tpu_custom_call" | custom-call | flops 8589934592 | tf_op jit(solution)/shard_map/pages/pallas_call | solution.py:614
  38.2 4.9 %all-to-all-start.1 = ((bf16[32,56,128]{2,1,0:T(8,128)(2,1)}), bf16[32,56,128]{2,1,0:T(8,128)(2,1)S(1)}, u32[]{:S(2)}, u32[]{:S(2)}) async-start(bf16[32,56,128]{2,1,0:T(8,128)(2,1)} %get-tuple-element.28), calls=%async_computation.1 | async-start | bytes 917504 | tf_op jit(solution)/shard_map/all_to_all | solution.py:519
  43.2 1.4 %collective-permute-start.5 = (bf16[16,2048]{1,0:T(8,128)(2,1)S(1)}, bf16[16,2048]{1,0:T(8,128)(2,1)S(1)}, u32[]{:S(2)}, u32[]{:S(2)}) collective-permute-start(bf16[16,2048]{1,0:T(8,128)(2,1)S(1)} %get-tuple-element.43), channel_id=1, source_target_pairs={{0,64},{64,128},{128,192},{192,0},{1,65},{65,129},{129,193},{193,1... | collective-permute-start | bytes 196616 | tf_op jit(solution)/shard_map/ppermute | solution.py:670
  45.2 0.7 path.1
  46.0 0.6 copy.52
  46.6 0.6 collective-permute-start.6
  47.2 1.0 collective-permute-start.7
  48.3 4.1 %collective-permute-done.6 = bf16[16,2048]{1,0:T(8,128)(2,1)S(1)} collective-permute-done((bf16[16,2048]{1,0:T(8,128)(2,1)S(1)}, bf16[16,2048]{1,0:T(8,128)(2,1)S(1)}, u32[]{:S(2)}, u32[]{:S(2)}) %collective-permute-start.6) | collective-permute-done | bytes 65568 | tf_op jit(solution)/shard_map/ppermute | solution.py:670
  52.4 7.6 %all-to-all-done.1.parts = bf16[32,56,128]{2,1,0:T(8,128)(2,1)S(1)} async-done(((bf16[32,56,128]{2,1,0:T(8,128)(2,1)}), bf16[32,56,128]{2,1,0:T(8,128)(2,1)S(1)}, u32[]{:S(2)}, u32[]{:S(2)}) %all-to-all-start.1) | async-done | bytes 458784 | tf_op jit(solution)/shard_map/all_to_all | solution.py:519
  60.5 11.1 %all_to_all.25.gathered = bf16[8,48,128]{2,1,0:T(8,128)(2,1)S(1)} all-to-all(bf16[8,48,128]{2,1,0:T(8,128)(2,1)S(1)} %merge.1), channel_id=1, replica_groups=mesh['y'=4,'c'=2,'z'=8,'x'=4] {'z'}, dimensions={0} | all-to-all | bytes 196608 | tf_op jit(solution)/shard_map/all_to_all | solution.py:699
  72.1 17.8 %all_to_all.26.gathered = bf16[32,48,128]{2,1,0:T(8,128)(2,1)S(1)} all-to-all(bf16[32,48,128]{2,1,0:T(8,128)(2,1)S(1)} %out_columns.1), channel_id=1, replica_groups=mesh['y'=4,'c'=2,'z'=8,'x'=4] {'x','z'}, dimensions={0} | all-to-all | bytes 786432 | tf_op jit(solution)/shard_map/all_to_all | solution.py:519
  91.1 1.4 %down.1 = bf16[32,48,128]{2,1,0:T(8,128)(2,1)} custom-call(bf16[96,256]{1,0:T(8,128)(2,1)S(1)} %fusion.4.hidden, bf16[256,2048]{1,0:T(8,128)(2,1)S(1)} %copy-done), custom_call_target="tpu_custom_call" | custom-call | tf_op jit(solution)/shard_map/down/pallas_call | solution.py:727
  92.5 4.7 %all-to-all-start.4 = ((bf16[32,48,128]{2,1,0:T(8,128)(2,1)}), bf16[32,48,128]{2,1,0:T(8,128)(2,1)S(1)}, u32[]{:S(2)}, u32[]{:S(2)}) async-start(bf16[32,48,128]{2,1,0:T(8,128)(2,1)} %down.1), calls=%async_computation.4 | async-start | bytes 786432 | tf_op jit(solution)/shard_map/all_to_all | solution.py:519
  97.2 3.6 %logits.1 = f32[16,4,384]{2,1,0:T(4,128)} custom-call(s32[16]{0:T(128)} %fusion.12.origins, bf16[64,2048]{1,0:T(8,128)(2,1)} %copy-done.7, bf16[384,2048]{1,0:T(8,128)(2,1)} %vocab.1), custom_call_target="tpu_custom_call" | custom-call | flops 2147483648 | tf_op jit(solution)/shard_map/logits/pallas_call | solution.py:738
  100.8 9.4 %all-to-all-done.4.shares = bf16[32,48,128]{2,1,0:T(8,128)(2,1)S(1)} async-done(((bf16[32,48,128]{2,1,0:T(8,128)(2,1)}), bf16[32,48,128]{2,1,0:T(8,128)(2,1)S(1)}, u32[]{:S(2)}, u32[]{:S(2)}) %all-to-all-start.4) | async-done | bytes 393248 | tf_op jit(solution)/shard_map/all_to_all | solution.py:519
  110.3 0.8 last.1
  (69 shorter events, 4.8 us)
Async XLA Ops:
  0.6 17.3 %copy-start.10 = (s32[2]{0:T(128)S(1)}, s32[2]{0:T(128)}, u32[]{:S(2)}) copy-start(s32[2]{0:T(128)} %param.19) | copy-start | bytes 28
  5.2 27.4 %all-to-all-start = ((bf16[32,56,128]{2,1,0:T(8,128)(2,1)}), bf16[32,56,128]{2,1,0:T(8,128)(2,1)S(1)}, u32[]{:S(2)}, u32[]{:S(2)}) async-start(bf16[32,56,128]{2,1,0:T(8,128)(2,1)} %get-tuple-element.23), calls=%async_computation | async-start | bytes 917504 | tf_op jit(solution)/shard_map/all_to_all | solution.py:519
  16.4 6.4 %collective-permute-start = (bf16[48,128]{1,0:T(8,128)(2,1)}, bf16[48,128]{1,0:T(8,128)(2,1)S(1)}, u32[]{:S(2)}, u32[]{:S(2)}) collective-permute-start(bf16[48,128]{1,0:T(8,128)(2,1)} %get-tuple-element.25.own_key), channel_id=1, source_target_pairs={{0,1},{1,0},{2,3},{3,2},{4,5},{5,4},{6,7},{7,6},{8,9},{9,8},{10,11... | collective-permute-start | bytes 36872 | tf_op jit(solution)/shard_map/ppermute | solution.py:590
  18.0 3.1 %copy-start.6 = (bf16[4,2048]{1,0:T(4,128)(2,1)S(1)}, bf16[4,2048]{1,0:T(4,128)(2,1)}, u32[]{:S(2)}) copy-start(bf16[4,2048]{1,0:T(4,128)(2,1)} %param.24) | copy-start | bytes 49156
  18.0 3.2 %copy-start.8 = (s32[2,48]{1,0:T(2,128)S(1)}, s32[2,48]{1,0:T(2,128)}, u32[]{:S(2)}) copy-start(s32[2,48]{1,0:T(2,128)} %param.18) | copy-start | bytes 1156
  18.1 4.2 %copy-start.9 = (s32[2,64]{1,0:T(2,128)S(1)}, s32[2,64]{1,0:T(2,128)}, u32[]{:S(2)}) copy-start(s32[2,64]{1,0:T(2,128)} %param.20) | copy-start | bytes 1540
  18.1 4.7 %copy-start.2 = (bf16[2048,64]{0,1:T(8,128)(2,1)S(1)}, bf16[2048,64]{0,1:T(8,128)(2,1)}, u32[]{:S(2)}) copy-start(bf16[2048,64]{0,1:T(8,128)(2,1)} %param.25) | copy-start | bytes 786436
  18.1 14.5 %copy-start.3 = (bf16[48,128]{1,0:T(8,128)(2,1)S(1)}, bf16[48,128]{1,0:T(8,128)(2,1)}, u32[]{:S(2)}) copy-start(bf16[48,128]{1,0:T(8,128)(2,1)} %get-tuple-element.27.own_value) | copy-start | bytes 36868
  18.1 14.5 %copy-start.5 = (bf16[48,128]{1,0:T(8,128)(2,1)S(1)}, bf16[48,128]{1,0:T(8,128)(2,1)}, u32[]{:S(2)}) copy-start(bf16[48,128]{1,0:T(8,128)(2,1)} %get-tuple-element.25.own_key) | copy-start | bytes 36868
  22.8 22.3 %collective-permute-start.1 = (bf16[64,2048]{1,0:T(8,128)(2,1)S(1)}, bf16[64,2048]{1,0:T(8,128)(2,1)S(1)}, u32[]{:S(2)}, u32[]{:S(2)}) collective-permute-start(bf16[64,2048]{1,0:T(8,128)(2,1)S(1)} %bitcast.32), channel_id=1, source_target_pairs={{0,1},{1,2},{2,3},{3,0},{4,5},{5,6},{6,7},{7,4},{8,9},{9,10},{10,1... | collective-permute-start | bytes 786440 | tf_op jit(solution)/shard_map/ppermute | solution.py:593
  23.4 21.7 %collective-permute-start.2 = (bf16[64,2048]{1,0:T(8,128)(2,1)S(1)}, bf16[64,2048]{1,0:T(8,128)(2,1)S(1)}, u32[]{:S(2)}, u32[]{:S(2)}) collective-permute-start(bf16[64,2048]{1,0:T(8,128)(2,1)S(1)} %bitcast.33), channel_id=1, source_target_pairs={{0,2},{1,3},{2,0},{3,1},{4,6},{5,7},{6,4},{7,5},{8,10},{9,11},{10,... | collective-permute-start | bytes 786440 | tf_op jit(solution)/shard_map/ppermute | solution.py:593
  26.3 18.8 %collective-permute-start.3 = (bf16[64,2048]{1,0:T(8,128)(2,1)S(1)}, bf16[64,2048]{1,0:T(8,128)(2,1)S(1)}, u32[]{:S(2)}, u32[]{:S(2)}) collective-permute-start(bf16[64,2048]{1,0:T(8,128)(2,1)S(1)} %bitcast.34), channel_id=1, source_target_pairs={{0,3},{1,0},{2,1},{3,2},{4,7},{5,4},{6,5},{7,6},{8,11},{9,8},{10,9... | collective-permute-start | bytes 786440 | tf_op jit(solution)/shard_map/ppermute | solution.py:593
  38.1 7.1 %copy-start.4 = (s32[2]{0:T(128)S(1)}, s32[2]{0:T(128)}, u32[]{:S(2)}) copy-start(s32[2]{0:T(128)} %accepted.1) | copy-start | bytes 28
  38.1 5.1 %collective-permute-start.4 = (bf16[8,2048]{1,0:T(8,128)(2,1)S(1)}, bf16[8,2048]{1,0:T(8,128)(2,1)S(1)}, u32[]{:S(2)}, u32[]{:S(2)}) collective-permute-start(bf16[8,2048]{1,0:T(8,128)(2,1)S(1)} %get-tuple-element.31), channel_id=1, source_target_pairs={{0,32},{32,0},{1,33},{33,1},{2,34},{34,2},{3,35},{35,3},{4,36},{36... | collective-permute-start | bytes 98312 | tf_op jit(solution)/shard_map/ppermute | solution.py:666
  38.2 21.8 %all-to-all-start.1 = ((bf16[32,56,128]{2,1,0:T(8,128)(2,1)}), bf16[32,56,128]{2,1,0:T(8,128)(2,1)S(1)}, u32[]{:S(2)}, u32[]{:S(2)}) async-start(bf16[32,56,128]{2,1,0:T(8,128)(2,1)} %get-tuple-element.28), calls=%async_computation.1 | async-start | bytes 917504 | tf_op jit(solution)/shard_map/all_to_all | solution.py:519
  43.2 5.0 %collective-permute-start.5 = (bf16[16,2048]{1,0:T(8,128)(2,1)S(1)}, bf16[16,2048]{1,0:T(8,128)(2,1)S(1)}, u32[]{:S(2)}, u32[]{:S(2)}) collective-permute-start(bf16[16,2048]{1,0:T(8,128)(2,1)S(1)} %get-tuple-element.43), channel_id=1, source_target_pairs={{0,64},{64,128},{128,192},{192,0},{1,65},{65,129},{129,193},{193,1... | collective-permute-start | bytes 196616 | tf_op jit(solution)/shard_map/ppermute | solution.py:670
  45.2 44.7 %copy-start.1 = (bf16[96,2048]{1,0:T(8,128)(2,1)S(1)}, bf16[96,2048]{1,0:T(8,128)(2,1)}, u32[]{:S(2)}) copy-start(bf16[96,2048]{1,0:T(8,128)(2,1)} %inputs.3) | copy-start | bytes 1179652
  46.6 5.8 %collective-permute-start.6 = (bf16[16,2048]{1,0:T(8,128)(2,1)S(1)}, bf16[16,2048]{1,0:T(8,128)(2,1)S(1)}, u32[]{:S(2)}, u32[]{:S(2)}) collective-permute-start(bf16[16,2048]{1,0:T(8,128)(2,1)S(1)} %get-tuple-element.43), channel_id=1, source_target_pairs={{0,128},{64,192},{128,0},{192,64},{1,129},{65,193},{129,1},{193,65... | collective-permute-start | bytes 196616 | tf_op jit(solution)/shard_map/ppermute | solution.py:670
  47.2 5.2 %collective-permute-start.7 = (bf16[16,2048]{1,0:T(8,128)(2,1)S(1)}, bf16[16,2048]{1,0:T(8,128)(2,1)S(1)}, u32[]{:S(2)}, u32[]{:S(2)}) collective-permute-start(bf16[16,2048]{1,0:T(8,128)(2,1)S(1)} %get-tuple-element.43), channel_id=1, source_target_pairs={{0,192},{64,0},{128,64},{192,128},{1,193},{65,1},{129,65},{193,129... | collective-permute-start | bytes 196616 | tf_op jit(solution)/shard_map/ppermute | solution.py:670
  52.4 38.0 %copy-start.7 = (bf16[64,2048]{1,0:T(8,128)(2,1)}, bf16[64,2048]{1,0:T(8,128)(2,1)S(1)}, u32[]{:S(2)}) copy-start(bf16[64,2048]{1,0:T(8,128)(2,1)S(1)} %constant_dynamic-update-slice_fusion.2.drafts) | copy-start | bytes 786436
  60.0 30.4 %copy-start.11 = (bf16[2048,2,256]{2,1,0:T(2,128)(2,1)S(1)}, bf16[2048,2,256]{2,1,0:T(2,128)(2,1)}, u32[]{:S(2)}) copy-start(bf16[2048,2,256]{2,1,0:T(2,128)(2,1)} %held.1) | copy-start | bytes 6291460
  89.9 1.2 %copy-start = (bf16[256,2048]{1,0:T(8,128)(2,1)S(1)}, bf16[256,2048]{1,0:T(8,128)(2,1)}, u32[]{:S(2)}) copy-start(bf16[256,2048]{1,0:T(8,128)(2,1)} %weight.1) | copy-start | bytes 3145732
  92.5 17.8 %all-to-all-start.4 = ((bf16[32,48,128]{2,1,0:T(8,128)(2,1)}), bf16[32,48,128]{2,1,0:T(8,128)(2,1)S(1)}, u32[]{:S(2)}, u32[]{:S(2)}) async-start(bf16[32,48,128]{2,1,0:T(8,128)(2,1)} %down.1), calls=%async_computation.4 | async-start | bytes 786432 | tf_op jit(solution)/shard_map/all_to_all | solution.py:519
